TPU v7x, 32 devices: a whole 2x2x4 slice. The times are simulated.
32 devices in a mesh: dp: 8 (over y, x, core), tower: 4 (over z).
Axes of the slice: x: 2, y: 2, z: 4, core: 2. Of those that a mesh axis runs over, the one named last changes fastest.
Arguments:
- features: bfloat16 [8, 32, 64, 256], P('dp', 'tower'), may hold values from -18 to 18
- crop_ids: int32 [8, 32], P('dp'), may hold values from 0 to 3, never falling along the last dimension, each value on 1 to 16 neighbouring positions
- labels: int32 [8, 32, 64, 9], P('dp', 'tower'), may hold values from -1 to 79
- positive: int32 [8, 32, 64, 9], P('dp', 'tower'), may hold values from 0 to 1
- box_targets: float32 [8, 32, 64, 36], P('dp', 'tower'), may hold values from -4 to 4
- tower_weights: float32 [4, 2, 2304, 256], P(None, None, ('dp', 'tower')), may hold values from -0.1875 to 0.1875
- head_weights: float32 [2304, 756], P(('dp', 'tower')), may hold values from -0.1875 to 0.1875
- biases: float32 [2804], replicated, may hold values from -0.3 to 0.3
- tower_m: float32 [4, 2, 2304, 256], P(None, None, ('dp', 'tower')), may hold values from -0.34785053 to 0.34785053
- tower_v: float32 [4, 2, 2304, 256], P(None, None, ('dp', 'tower')), may hold values from 0.000625 to 0.0025
- head_m: float32 [2304, 756], P(('dp', 'tower')), may hold values from -0.2 to 0.2
- head_v: float32 [2304, 756], P(('dp', 'tower')), may hold values from 0.00019753087 to 0.0007901235
- bias_m: float32 [2804], replicated, may hold values from -0.3888889 to 0.3888889
- bias_v: float32 [2804], replicated, may hold values from 0.0007901235 to 0.003160494
- step_count: int32 [1], replicated, may hold values from 2 to 20
Outputs:
- logits: bfloat16 [8, 32, 64, 720], P('dp', 'tower')
- deltas: bfloat16 [8, 32, 64, 36], P('dp', 'tower')
- loss: float32 [], replicated
- feature_grad: float32 [8, 32, 64, 256], P('dp', 'tower')
- tower_grad: float32 [4, 2304, 256], P(None, ('dp', 'tower'))
- box_tower_grad: float32 [4, 2304, 256], P(None, ('dp', 'tower'))
- head_grad: float32 [2304, 756], P(('dp', 'tower'))
- bias_grad: float32 [2768], replicated
- box_bias_grad: float32 [36], replicated
- tower_new: float32 [4, 2, 2304, 256], P(None, None, ('dp', 'tower'))
- head_new: float32 [2304, 756], P(('dp', 'tower'))
- bias_new: float32 [2804], replicated
- tower_m_new: float32 [4, 2, 2304, 256], P(None, None, ('dp', 'tower'))
- tower_v_new: float32 [4, 2, 2304, 256], P(None, None, ('dp', 'tower'))
- head_m_new: float32 [2304, 756], P(('dp', 'tower'))
- head_v_new: float32 [2304, 756], P(('dp', 'tower'))
- bias_m_new: float32 [2804], replicated
- bias_v_new: float32 [2804], replicated
- tower_copy: bfloat16 [4, 2, 2304, 256], P(None, None, ('dp', 'tower'))
- head_copy: bfloat16 [2304, 756], P(('dp', 'tower'))
Inputs may be any that keep to these rules, and one draw needn't show every extreme that they name: `crop_ids`: crop numbers never fall along a canvas's rows, each crop spans 1 to 16 rows, one spans exactly 16.
All inputs are finite; a program needn't handle non-finite values.
Results may differ from a plain program's by a relative error of at most 0.012.
Values may be sent and summed in bfloat16 or wider, within the bound.
A program may use at most 192 MiB of HBM per device.

v0:
```python
from functools import partial

import jax
import jax.numpy as jnp
from jax import lax
from jax.sharding import PartitionSpec as P

beta_one = 0.9
beta_two = 0.999
adam_eps = 1e-08
learn_rate = 0.03
decay_rate = 0.05
focal_alpha = 0.25
smooth_beta = 1.0 / 9.0


def with_halo(shard, sides, width):
    for axis, dim in sides:
        size, length = (lax.axis_size(axis), shard.shape[dim])
        up = [(i, (i + 1) % size) for i in range(size - 1)]
        down = [(j, i) for i, j in up]
        last = lax.slice_in_dim(shard, length - width, length, axis=dim)
        initial = lax.slice_in_dim(shard, 0, width, axis=dim)
        before = lax.ppermute(last, axis, up)
        after = lax.ppermute(initial, axis, down)
        shard = jnp.concatenate([before, shard, after], axis=dim)
    return shard


def act_rim(values):
    return with_halo(values, (("tower", 2),), 1)


def grad_rim(values):
    return with_halo(values, (("tower", 2),), 1)


def pad_cols(values):
    return jnp.pad(values, ((0, 0), (0, 0), (0, 0), (1, 1), (0, 0)))


def silu_value(values):
    return values * jax.nn.sigmoid(values)


def silu_slope(values):
    sig = jax.nn.sigmoid(values)
    return sig * (1.0 + values * (1.0 - sig))


def conv_forward(padded, weight, out_rows, out_cols):
    stacks, canvases, channels = (padded.shape[0], padded.shape[1], padded.shape[-1])
    summed = None
    for row_off in range(3):
        for col_off in range(3):
            tap_index = row_off * 3 + col_off
            window = padded[
                :, :, row_off : row_off + out_rows, col_off : col_off + out_cols, :
            ].reshape(stacks, -1, channels)
            contrib = jnp.einsum(
                "snk,skm->snm",
                window,
                weight[:, tap_index * channels : (tap_index + 1) * channels, :],
                preferred_element_type=jnp.float32,
            )
            summed = contrib if summed is None else summed + contrib
    return summed.reshape(stacks, canvases, out_rows, out_cols, weight.shape[-1])


def conv_input_grad(grad_pad, weight, out_rows, out_cols):
    stacks, canvases, outputs = (grad_pad.shape[0], grad_pad.shape[1], grad_pad.shape[-1])
    channels = weight.shape[1] // 9
    summed = None
    for row_off in range(3):
        for col_off in range(3):
            tap_index = row_off * 3 + col_off
            window = grad_pad[
                :, :, 2 - row_off : 2 - row_off + out_rows, 2 - col_off : 2 - col_off + out_cols, :
            ].reshape(stacks, -1, outputs)
            contrib = jnp.einsum(
                "snm,skm->snk",
                window,
                weight[:, tap_index * channels : (tap_index + 1) * channels, :],
                preferred_element_type=jnp.float32,
            )
            summed = contrib if summed is None else summed + contrib
    return summed.reshape(stacks, canvases, out_rows, out_cols, channels)


def conv_weight_grad(padded, grads):
    stacks, channels = (padded.shape[0], padded.shape[-1])
    out_rows, out_cols = (grads.shape[2], grads.shape[3])
    flat_grads = grads.reshape(stacks, -1, grads.shape[-1])
    pieces = []
    for row_off in range(3):
        for col_off in range(3):
            window = padded[
                :, :, row_off : row_off + out_rows, col_off : col_off + out_cols, :
            ].reshape(stacks, -1, channels)
            pieces.append(
                jnp.einsum("snk,snm->skm", window, flat_grads, preferred_element_type=jnp.float32)
            )
    return jnp.concatenate(pieces, 1)


def adam_update(weight, grad, first, second, step_float, decay):
    first_new = beta_one * first + (1.0 - beta_one) * grad
    second_new = beta_two * second + (1.0 - beta_two) * grad * grad
    first_hat = first_new / (1.0 - jnp.power(beta_one, step_float))
    second_hat = second_new / (1.0 - jnp.power(beta_two, step_float))
    weight_new = weight - learn_rate * (
        first_hat / (jnp.sqrt(second_hat) + adam_eps) + decay * weight
    )
    return (weight_new, first_new, second_new)


def anchor_masks(label_rows, positive_rows, row_flags, classes):
    valid = (label_rows >= 0) & row_flags[:, :, None, None]
    chosen = valid & (positive_rows > 0)
    targets = (
        (label_rows[..., None] == jnp.arange(classes, dtype=jnp.int32)) & chosen[..., None]
    ).astype(jnp.float32)
    return (valid.astype(jnp.float32), chosen.astype(jnp.float32), targets)


def focal_terms(cls_vals, targets, valid_f):
    logit_view = cls_vals.reshape(targets.shape)
    prob = jax.nn.sigmoid(logit_view)
    cross = jax.nn.softplus(logit_view) - targets * logit_view
    prob_true = prob * targets + (1.0 - prob) * (1.0 - targets)
    alpha_weight = focal_alpha * targets + (1.0 - focal_alpha) * (1.0 - targets)
    return jnp.sum(alpha_weight * (1.0 - prob_true) ** 2 * cross * valid_f[..., None])


def smooth_terms(box_vals, goals, chosen_f):
    diff = box_vals.reshape(chosen_f.shape + (4,)) - goals.reshape(chosen_f.shape + (4,))
    abs_diff = jnp.abs(diff)
    smooth = jnp.where(
        abs_diff < smooth_beta, 0.5 * diff * diff / smooth_beta, abs_diff - 0.5 * smooth_beta
    )
    return jnp.sum(smooth * chosen_f[..., None])


def shards(
    features,
    crop_ids,
    labels,
    positive,
    box_targets,
    tower_weights,
    head_weights,
    biases,
    tower_m,
    tower_v,
    head_m,
    head_v,
    bias_m,
    bias_v,
    step_count,
):
    canvases, row_count, col_count, channels = features.shape
    layers = tower_weights.shape[0]
    anchors = labels.shape[-1]
    head_out = head_weights.shape[1]
    box_out = 4 * anchors
    cls_out = head_out - box_out
    classes = cls_out // anchors
    shard = lax.axis_index("tower")
    tower_low, head_stack = (
        lax.all_gather(tower_weights.astype(jnp.bfloat16), ("dp", "tower"), axis=2, tiled=True),
        lax.all_gather(
            head_weights.astype(jnp.bfloat16)[None, None], ("dp", "tower"), axis=2, tiled=True
        ),
    )
    head_low = head_stack[0, 0]
    tower_bias = biases[: 2 * layers * channels].reshape(layers, 2, channels)
    head_bias = biases[2 * layers * channels :]
    cls_weight = head_low[:, :cls_out][None]
    box_weight = head_low[:, cls_out:][None]
    same_rows = crop_ids[:, 1:] == crop_ids[:, :-1]
    edge_true = jnp.ones((crop_ids.shape[0], 1), dtype=jnp.bool_)
    row_ok = jnp.concatenate([edge_true, same_rows], 1) & jnp.concatenate([same_rows, edge_true], 1)
    own_ok = lax.dynamic_slice_in_dim(row_ok, shard * row_count, row_count, 1)
    own_valid, own_chosen, own_targets = anchor_masks(labels, positive, own_ok, classes)
    count_all = lax.psum(jnp.sum(own_chosen), ("dp", "tower"))
    denom = jnp.maximum(count_all, 1.0)
    grad_scale = 1.0 / denom
    kept = []
    preact = []
    current = features[None]
    for layer in range(layers):
        padded = pad_cols(act_rim(current))
        if layer == 0:
            padded = jnp.broadcast_to(padded, (2,) + padded.shape[1:])
        kept.append(padded)
        summed = (
            conv_forward(padded, tower_low[layer], row_count, col_count)
            + tower_bias[layer][:, None, None, None, :]
        )
        preact.append(summed)
        current = silu_value(summed).astype(jnp.bfloat16)
    head_in = pad_cols(act_rim(current))
    kept.append(head_in)
    cls_raw = conv_forward(head_in[0:1], cls_weight, row_count, col_count)[0] + head_bias[:cls_out]
    box_raw = conv_forward(head_in[1:2], box_weight, row_count, col_count)[0] + head_bias[cls_out:]
    focal_value, focal_back = jax.vjp(
        partial(focal_terms, targets=own_targets, valid_f=own_valid), cls_raw
    )
    smooth_value, smooth_back = jax.vjp(
        partial(smooth_terms, goals=box_targets, chosen_f=own_chosen), box_raw
    )
    loss_local = focal_value + smooth_value
    cls_low = focal_back(grad_scale)[0].astype(jnp.bfloat16)
    box_low = smooth_back(grad_scale)[0].astype(jnp.bfloat16)
    head_wgrad = jnp.concatenate(
        [
            conv_weight_grad(head_in[0:1], cls_low[None])[0],
            conv_weight_grad(head_in[1:2], box_low[None])[0],
        ],
        1,
    )
    head_bgrad = jnp.concatenate(
        [
            jnp.sum(cls_low, axis=(0, 1, 2), dtype=jnp.float32),
            jnp.sum(box_low, axis=(0, 1, 2), dtype=jnp.float32),
        ]
    )
    joined = pad_cols(grad_rim(jnp.concatenate([cls_low, box_low], -1)[None]))
    upstream = jnp.concatenate(
        [
            conv_input_grad(joined[..., :cls_out], cls_weight, row_count, col_count),
            conv_input_grad(joined[..., cls_out:], box_weight, row_count, col_count),
        ],
        0,
    )
    tower_grads = [None] * layers
    bias_grads = [None] * layers
    for layer in reversed(range(layers)):
        grad_low = (upstream * silu_slope(preact[layer])).astype(jnp.bfloat16)
        bias_grads[layer] = jnp.sum(grad_low, axis=(1, 2, 3), dtype=jnp.float32)
        tower_grads[layer] = conv_weight_grad(kept[layer], grad_low)
        padded_grad = pad_cols(grad_rim(grad_low))
        upstream = conv_input_grad(padded_grad, tower_low[layer], row_count, col_count)
    feature_grad = upstream[0] + upstream[1]
    tower_shard, head_pair = (
        lax.psum_scatter(
            jnp.stack(tower_grads, 0), ("dp", "tower"), scatter_dimension=2, tiled=True
        ),
        lax.psum_scatter(head_wgrad[None, None], ("dp", "tower"), scatter_dimension=2, tiled=True),
    )
    head_shard = head_pair[0, 0]
    bias_local = jnp.concatenate([jnp.stack(bias_grads, 0).reshape(-1), head_bgrad])
    logits_out = cls_raw.astype(jnp.bfloat16)
    deltas_out = box_raw.astype(jnp.bfloat16)
    bias_grad, loss_total = lax.psum((bias_local, loss_local), ("dp", "tower"))
    loss = loss_total / denom
    step_float = step_count[0].astype(jnp.float32)
    tower_new, tower_m_new, tower_v_new = adam_update(
        tower_weights, tower_shard, tower_m, tower_v, step_float, decay_rate
    )
    head_new, head_m_new, head_v_new = adam_update(
        head_weights, head_shard, head_m, head_v, step_float, decay_rate
    )
    bias_new, bias_m_new, bias_v_new = adam_update(
        biases, bias_grad, bias_m, bias_v, step_float, 0.0
    )
    split_at = bias_grad.shape[0] - box_out
    return (
        logits_out,
        deltas_out,
        loss,
        feature_grad,
        tower_shard[:, 0],
        tower_shard[:, 1],
        head_shard,
        bias_grad[:split_at],
        bias_grad[split_at:],
        tower_new,
        head_new,
        bias_new,
        tower_m_new,
        tower_v_new,
        head_m_new,
        head_v_new,
        bias_m_new,
        bias_v_new,
        tower_new.astype(jnp.bfloat16),
        head_new.astype(jnp.bfloat16),
    )


def solution(mesh):
    placed = (
        P("dp", "tower", None, None),
        P("dp", None),
        P("dp", "tower", None, None),
        P("dp", "tower", None, None),
        P("dp", "tower", None, None),
        P(None, None, ("dp", "tower"), None),
        P(("dp", "tower"), None),
        P(),
        P(None, None, ("dp", "tower"), None),
        P(None, None, ("dp", "tower"), None),
        P(("dp", "tower"), None),
        P(("dp", "tower"), None),
        P(),
        P(),
        P(),
    )
    return jax.shard_map(
        shards,
        mesh=mesh,
        in_specs=placed,
        out_specs=(
            P("dp", "tower", None, None),
            P("dp", "tower", None, None),
            P(),
            P("dp", "tower", None, None),
            P(None, ("dp", "tower"), None),
            P(None, ("dp", "tower"), None),
            P(("dp", "tower"), None),
            P(),
            P(),
            P(None, None, ("dp", "tower"), None),
            P(("dp", "tower"), None),
            P(),
            P(None, None, ("dp", "tower"), None),
            P(None, None, ("dp", "tower"), None),
            P(("dp", "tower"), None),
            P(("dp", "tower"), None),
            P(),
            P(),
            P(None, None, ("dp", "tower"), None),
            P(("dp", "tower"), None),
        ),
        check_vma=False,
    )
```

profile of v0, /device:TPU:0, one launch (start us, length us, event | category | flops | bytes accessed | tf_op | source)
XLA Modules:
  0.0 654.2 jit_solution(18256691162037994958)
XLA Ops:
  7.2 1.8 convert_element_type.275
  9.9 4.9 collective-permute-start
  14.8 1.3 collective-permute-start.1
  16.1 1.6 convert_element_type.283
  18.8 1.5 convert_reduce_fusion.6
  21.6 42.3 %psum.22 = f32[]{:T(128)} all-reduce(f32[]{:T(128)} %get-tuple-element.127), channel_id=1, replica_groups=mesh['dp'=8,'tower'=4] {'dp','tower'}, use_global_device_ids=true, to_apply=%region_4.5 | all-reduce | flops 1 | bytes 8 | tf_op jit(solution)/shard_map/psum | solution.py:185
  71.0 25.6 %all-gather.4.cloned.1.call-done = bf16[4,2,2304,256]{3,2,1,0:T(8,128)(2,1)} async-done(((bf16[4,2,72,256]{3,2,1,0:T(8,128)(2,1)}), bf16[4,2,2304,256]{3,2,1,0:T(8,128)(2,1)}) %all-gather.4.cloned.1.call-update) | async-done | bytes 9437200 | tf_op jit(solution)/shard_map/all_gather | solution.py:170
  96.6 5.8 slice_bitcast_fusion.1
  108.1 3.3 collective-permute-start.2
  111.5 1.3 collective-permute-start.3
  114.0 4.0 collective-permute-done.3
  118.0 1.4 fusion.70
  126.9 3.6 collective-permute-start.4
  130.5 1.5 collective-permute-start.5
  132.6 1.3 slice.942
  133.9 1.3 slice.962
  137.2 1.6 mul.954
  139.0 1.7 and.74
  141.5 1.7 eq.120
  147.2 1.8 copy.263
  149.2 2.0 copy.268
  151.4 1.7 copy.266
  153.3 2.0 copy.265
  158.2 2.5 copy-done.6
  167.0 5.1 collective-permute-start.6
  172.1 1.3 collective-permute-start.7
  173.4 2.2 slice_bitcast_fusion
  175.7 2.9 collective-permute-done.7
  178.6 1.4 fusion.66
  180.6 1.2 copy-done.8
  188.3 1.7 collective-permute-start.8
  189.9 1.5 collective-permute-start.9
  191.4 1.3 slice_bitcast_fusion.5
  192.8 3.3 collective-permute-done.9
  201.5 5.4 convert_reduce_fusion
  210.2 2.7 copy-done.23
  215.4 1.7 copy.339
  217.1 2.9 convert_reduce_fusion.5
  225.0 3.0 copy.257
  228.0 5.8 fusion.5
  235.6 2.9 collective-permute-start.10
  238.5 1.3 collective-permute-start.11
  239.8 6.3 maximum_bitcast_fusion
  246.0 16.6 %copy.301 = f32[1,1,2304,756]{3,1,0,2:T(1,128)} copy(f32[1,1,2304,756]{2,3,1,0:T(8,128)} %maximum_bitcast_fusion) | data formatting | bytes 13934592 | tf_op jit(solution)/shard_map/broadcast_in_dim | solution.py:249
  262.7 1.5 fusion.51
  274.5 4.8 collective-permute-start.12
  279.3 1.5 collective-permute-start.13
  292.9 4.1 collective-permute-start.14
  297.0 1.3 collective-permute-start.15
  302.8 1.9 collective-permute-done.15
  310.6 2.8 collective-permute-start.16
  313.5 1.5 collective-permute-start.17
  324.8 1.7 convert_reduce_fusion.4
  329.6 6.9 %pad_maximum_fusion = f32[4,2,2304,256]{3,2,1,0:T(8,128)} fusion(f32[1,2,2304,256]{3,2,1,0:T(8,128)S(1)} %bitcast.557, f32[1,2,2304,256]{3,2,1,0:T(8,128)S(1)} %bitcast.558, f32[1,2,2304,256]{3,2,1,0:T(8,128)S(1)} %bitcast.559, f32[1,2,2304,256]{3,2,1,0:T(8,128)S(1)} %bitcast.560), kind=kLoop, calls=%fused_computation | loop fusion | flops 14155776 | bytes 37748736 | tf_op jit(solution)/shard_map/stack | solution.py:247
  337.5 1.6 mul.893
  339.1 1.8 copy.302
  341.0 4.8 multiply_reduce_fusion
  347.5 4.1 collective-permute-start.18
  351.8 1.3 collective-permute-start.19
  353.1 40.9 %all-reduce.11 = (f32[]{:T(128)}, f32[2804]{0:T(1024)S(1)}) all-reduce(f32[]{:T(128)S(6)} %add.1103, f32[2804]{0:T(1024)S(1)} %concatenate.206), channel_id=1, replica_groups=mesh['dp'=8,'tower'=4] {'dp','tower'}, use_global_device_ids=true, to_apply=%region_2.3 | all-reduce | flops 2805 | bytes 22440 | tf_op jit(solution)/shard_map/psum | solution.py:255
  402.0 26.9 %all-reduce.14.cloned.1.call-done = f32[1,1,2304,756]{3,1,0,2:T(1,128)} async-done(((f32[1,1,2304,756]{3,1,0,2:T(1,128)}), f32[1,1,2304,756]{3,1,0,2:T(1,128)}) %all-reduce.14.cloned.1.call-update) | async-done | bytes 6967312
  431.0 210.5 %reduce-scatter.2.cloned.1.call-done = f32[4,2,72,256]{3,2,1,0:T(8,128)} async-done(((f32[4,2,2304,256]{3,2,1,0:T(8,128)}), f32[4,2,72,256]{3,2,1,0:T(8,128)}) %reduce-scatter.2.cloned.1.call-update) | async-done | bytes 589840 | tf_op jit(solution)/shard_map/reduce_scatter | solution.py:246
  641.5 1.9 slice_bitcast_fusion.33
  643.4 2.7 fusion.209
  (560 shorter events, 119.8 us)
Async XLA Ops:
  7.2 89.4 %all-gather.4.cloned.1.call-start = ((), (), s32[]{:S(2)}) async-start(), calls=%async_computation.1 | async-start | bytes 9732096 | tf_op jit(solution)/shard_map/all_gather | solution.py:170
  9.1 164.3 %all-gather.6.cloned.1.call-start = ((), (), s32[]{:S(2)}) async-start(), calls=%async_computation.3 | async-start | bytes 3649536 | tf_op jit(solution)/shard_map/all_gather | solution.py:171
  9.9 54.8 %collective-permute-start = (bf16[1,1,1,64,256]{4,3,2,1,0:T(8,128)(2,1)S(1)}, bf16[1,1,1,64,256]{4,3,2,1,0:T(8,128)(2,1)S(1)}, u32[]{:S(2)}, u32[]{:S(2)}) collective-permute-start(bf16[1,1,1,64,256]{4,3,2,1,0:T(8,128)(2,1)S(1)} %get-tuple-element.261), channel_id=1, source_target_pairs={{0,1},{1,2},{2,3},{4,5},{5,6},{6,7},{8,9},{9,10},{10,11},{12,13},{... | collective-permute-start | bytes 98312 | tf_op jit(solution)/shard_map/ppermute | solution.py:24
  14.8 49.9 %collective-permute-start.1 = (bf16[1,1,1,64,256]{4,3,2,1,0:T(8,128)(2,1)S(1)}, bf16[1,1,1,64,256]{4,3,2,1,0:T(8,128)(2,1)S(1)}, u32[]{:S(2)}, u32[]{:S(2)}) collective-permute-start(bf16[1,1,1,64,256]{4,3,2,1,0:T(8,128)(2,1)S(1)} %get-tuple-element.262), channel_id=1, source_target_pairs={{1,0},{2,1},{3,2},{5,4},{6,5},{7,6},{9,8},{10,9},{11,10},{13,12},{... | collective-permute-start | bytes 98312 | tf_op jit(solution)/shard_map/ppermute | solution.py:25
  17.7 411.2 %all-reduce.14.cloned.1.call-start = ((), (), s32[]{:S(2)}) async-start(), calls=%async_computation.4 | async-start | bytes 14155776
  64.0 59.5 %copy-start.131 = (f32[2,256]{1,0:T(2,128)}, f32[2,256]{1,0:T(2,128)S(1)}, u32[]{:S(2)}) copy-start(f32[2,256]{1,0:T(2,128)S(1)} %add.1027) | copy-start | bytes 6148
  69.7 34.6 %copy-start.87 = (bf16[512,256]{0,1:T(8,128)(2,1)}, bf16[512,256]{0,1:T(8,128)(2,1)S(1)}, u32[]{:S(2)}) copy-start(bf16[512,256]{0,1:T(8,128)(2,1)S(1)} %copy.247) | copy-start | bytes 786436
  69.9 34.8 %copy-start.85 = (bf16[512,256]{0,1:T(8,128)(2,1)}, bf16[512,256]{0,1:T(8,128)(2,1)S(1)}, u32[]{:S(2)}) copy-start(bf16[512,256]{0,1:T(8,128)(2,1)S(1)} %copy.249) | copy-start | bytes 786436
  70.0 35.0 %copy-start.83 = (bf16[512,256]{0,1:T(8,128)(2,1)}, bf16[512,256]{0,1:T(8,128)(2,1)S(1)}, u32[]{:S(2)}) copy-start(bf16[512,256]{0,1:T(8,128)(2,1)S(1)} %copy.251) | copy-start | bytes 786436
  70.2 35.2 %copy-start.79 = (bf16[512,256]{0,1:T(8,128)(2,1)}, bf16[512,256]{0,1:T(8,128)(2,1)S(1)}, u32[]{:S(2)}) copy-start(bf16[512,256]{0,1:T(8,128)(2,1)S(1)} %copy.253) | copy-start | bytes 786436
  102.4 22.2 %copy-start.4 = (bf16[2,2304,256]{2,1,0:T(8,128)(2,1)}, bf16[2,2304,256]{2,1,0:T(8,128)(2,1)S(1)}, u32[]{:S(2)}) copy-start(bf16[2,2304,256]{2,1,0:T(8,128)(2,1)S(1)} %get-tuple-element.132) | copy-start | bytes 7077892
  106.3 17.2 %copy-start.14 = (f32[2,512,256]{2,1,0:T(8,128)}, f32[2,512,256]{2,1,0:T(8,128)S(1)}, u32[]{:S(2)}) copy-start(f32[2,512,256]{2,1,0:T(8,128)S(1)} %convolution_add_fusion.49) | copy-start | bytes 3145732
  108.1 5.9 collective-permute-start.2
  111.5 6.6 %collective-permute-start.3 = (bf16[2,1,1,64,256]{4,3,2,0,1:T(8,128)(2,1)}, bf16[2,1,1,64,256]{4,3,2,0,1:T(8,128)(2,1)}, u32[]{:S(2)}, u32[]{:S(2)}) collective-permute-start(bf16[2,1,1,64,256]{4,3,2,0,1:T(8,128)(2,1)} %get-tuple-element.249), channel_id=1, source_target_pairs={{1,0},{2,1},{3,2},{5,4},{6,5},{7,6},{9,8},{10,9},{11,10},{13,12},{... | collective-permute-start | bytes 196616 | tf_op jit(solution)/shard_map/ppermute | solution.py:25
  112.8 12.2 %copy-start.133 = (f32[2,256]{1,0:T(2,128)}, f32[2,256]{1,0:T(2,128)S(1)}, u32[]{:S(2)}) copy-start(f32[2,256]{1,0:T(2,128)S(1)} %add.1042) | copy-start | bytes 6148
  126.9 28.4 %collective-permute-start.4 = (bf16[2,1,1,64,256]{4,3,2,0,1:T(8,128)(2,1)}, bf16[2,1,1,64,256]{4,3,2,0,1:T(8,128)(2,1)}, u32[]{:S(2)}, u32[]{:S(2)}) collective-permute-start(bf16[2,1,1,64,256]{4,3,2,0,1:T(8,128)(2,1)} %get-tuple-element.244), channel_id=1, source_target_pairs={{0,1},{1,2},{2,3},{4,5},{5,6},{6,7},{8,9},{9,10},{10,11},{12,13},{... | collective-permute-start | bytes 196616 | tf_op jit(solution)/shard_map/ppermute | solution.py:24
  130.5 24.8 %collective-permute-start.5 = (bf16[2,1,1,64,256]{4,3,2,0,1:T(8,128)(2,1)}, bf16[2,1,1,64,256]{4,3,2,0,1:T(8,128)(2,1)}, u32[]{:S(2)}, u32[]{:S(2)}) collective-permute-start(bf16[2,1,1,64,256]{4,3,2,0,1:T(8,128)(2,1)} %get-tuple-element.245), channel_id=1, source_target_pairs={{1,0},{2,1},{3,2},{5,4},{6,5},{7,6},{9,8},{10,9},{11,10},{13,12},{... | collective-permute-start | bytes 196616 | tf_op jit(solution)/shard_map/ppermute | solution.py:25
  141.5 7.5 %copy-start.123 = (f32[8,64,9]{1,2,0:T(8,128)S(1)}, f32[8,64,9]{1,2,0:T(8,128)}, u32[]{:S(2)}) copy-start(f32[8,64,9]{1,2,0:T(8,128)} %copy.343) | copy-start | bytes 55300
  157.5 6.4 copy-start.44
  167.0 8.7 %collective-permute-start.6 = (bf16[2,1,1,64,256]{4,3,2,0,1:T(8,128)(2,1)}, bf16[2,1,1,64,256]{4,3,2,0,1:T(8,128)(2,1)}, u32[]{:S(2)}, u32[]{:S(2)}) collective-permute-start(bf16[2,1,1,64,256]{4,3,2,0,1:T(8,128)(2,1)} %get-tuple-element.240), channel_id=1, source_target_pairs={{0,1},{1,2},{2,3},{4,5},{5,6},{6,7},{8,9},{9,10},{10,11},{12,13},{... | collective-permute-start | bytes 196616 | tf_op jit(solution)/shard_map/ppermute | solution.py:24
  172.1 6.5 collective-permute-start.7
  188.3 4.5 collective-permute-start.8
  189.9 6.2 collective-permute-start.9
  192.7 21.8 %copy-start.28 = (bf16[1,2304,36]{2,1,0:T(8,128)(2,1)}, bf16[1,2304,36]{2,1,0:T(8,128)(2,1)S(1)}, u32[]{:S(2)}) copy-start(bf16[1,2304,36]{2,1,0:T(8,128)(2,1)S(1)} %slice_bitcast_fusion.5) | copy-start | bytes 497668
  196.2 17.1 %copy-start.112 = (bf16[1,1,8,64,256]{4,3,2,0,1:T(8,128)(2,1)}, bf16[1,1,8,64,256]{4,3,2,0,1:T(8,128)(2,1)S(1)}, u32[]{:S(2)}) copy-start(bf16[1,1,8,64,256]{4,3,2,0,1:T(8,128)(2,1)S(1)} %get-tuple-element.235) | copy-start | bytes 786436
  196.2 17.7 %copy-start.110 = (bf16[1,1,8,64,256]{4,3,2,0,1:T(8,128)(2,1)}, bf16[1,1,8,64,256]{4,3,2,0,1:T(8,128)(2,1)S(1)}, u32[]{:S(2)}) copy-start(bf16[1,1,8,64,256]{4,3,2,0,1:T(8,128)(2,1)S(1)} %get-tuple-element.232) | copy-start | bytes 786436
  196.2 18.3 %copy-start.108 = (bf16[1,1,8,64,256]{4,3,2,0,1:T(8,128)(2,1)}, bf16[1,1,8,64,256]{4,3,2,0,1:T(8,128)(2,1)S(1)}, u32[]{:S(2)}) copy-start(bf16[1,1,8,64,256]{4,3,2,0,1:T(8,128)(2,1)S(1)} %get-tuple-element.212) | copy-start | bytes 786436
  198.0 14.9 %copy-start.105 = (bf16[1,1,8,64,256]{4,3,2,0,1:T(8,128)(2,1)}, bf16[1,1,8,64,256]{4,3,2,0,1:T(8,128)(2,1)S(1)}, u32[]{:S(2)}) copy-start(bf16[1,1,8,64,256]{4,3,2,0,1:T(8,128)(2,1)S(1)} %get-tuple-element.184) | copy-start | bytes 786436
  198.0 15.1 %copy-start.95 = (bf16[1,1,8,64,256]{4,3,2,0,1:T(8,128)(2,1)}, bf16[1,1,8,64,256]{4,3,2,0,1:T(8,128)(2,1)S(1)}, u32[]{:S(2)}) copy-start(bf16[1,1,8,64,256]{4,3,2,0,1:T(8,128)(2,1)S(1)} %get-tuple-element.191) | copy-start | bytes 786436
  198.0 15.5 %copy-start.103 = (bf16[1,1,8,64,256]{4,3,2,0,1:T(8,128)(2,1)}, bf16[1,1,8,64,256]{4,3,2,0,1:T(8,128)(2,1)S(1)}, u32[]{:S(2)}) copy-start(bf16[1,1,8,64,256]{4,3,2,0,1:T(8,128)(2,1)S(1)} %get-tuple-element.183) | copy-start | bytes 786436
  198.0 15.7 %copy-start.101 = (bf16[1,1,8,64,256]{4,3,2,0,1:T(8,128)(2,1)}, bf16[1,1,8,64,256]{4,3,2,0,1:T(8,128)(2,1)S(1)}, u32[]{:S(2)}) copy-start(bf16[1,1,8,64,256]{4,3,2,0,1:T(8,128)(2,1)S(1)} %get-tuple-element.182) | copy-start | bytes 786436
  198.0 16.1 %copy-start.99 = (bf16[1,1,8,64,256]{4,3,2,0,1:T(8,128)(2,1)}, bf16[1,1,8,64,256]{4,3,2,0,1:T(8,128)(2,1)S(1)}, u32[]{:S(2)}) copy-start(bf16[1,1,8,64,256]{4,3,2,0,1:T(8,128)(2,1)S(1)} %get-tuple-element.181) | copy-start | bytes 786436
  198.0 16.3 %copy-start.97 = (bf16[1,1,8,64,256]{4,3,2,0,1:T(8,128)(2,1)}, bf16[1,1,8,64,256]{4,3,2,0,1:T(8,128)(2,1)S(1)}, u32[]{:S(2)}) copy-start(bf16[1,1,8,64,256]{4,3,2,0,1:T(8,128)(2,1)S(1)} %get-tuple-element.180) | copy-start | bytes 786436
  217.1 6.2 copy-start.98
  217.1 6.4 copy-start.109
  217.1 6.6 %copy-start.96 = (bf16[1,1,8,64,256]{4,3,2,0,1:T(8,128)(2,1)S(1)}, bf16[1,1,8,64,256]{4,3,2,0,1:T(8,128)(2,1)}, u32[]{:S(2)}) copy-start(bf16[1,1,8,64,256]{4,3,2,0,1:T(8,128)(2,1)} %copy-done.95) | copy-start | bytes 786436
  235.6 27.1 %collective-permute-start.10 = (bf16[1,1,1,64,756]{4,3,2,1,0:T(8,128)(2,1)}, bf16[1,1,1,64,756]{4,3,2,1,0:T(8,128)(2,1)}, u32[]{:S(2)}, u32[]{:S(2)}) collective-permute-start(bf16[1,1,1,64,756]{4,3,2,1,0:T(8,128)(2,1)} %get-tuple-element.154), channel_id=1, source_target_pairs={{0,1},{1,2},{2,3},{4,5},{5,6},{6,7},{8,9},{9,10},{10,11},{12,13},{... | collective-permute-start | bytes 290312 | tf_op jit(solution)/shard_map/ppermute | solution.py:24
  238.5 24.2 %collective-permute-start.11 = (bf16[1,1,1,64,756]{4,3,2,1,0:T(8,128)(2,1)}, bf16[1,1,1,64,756]{4,3,2,1,0:T(8,128)(2,1)}, u32[]{:S(2)}, u32[]{:S(2)}) collective-permute-start(bf16[1,1,1,64,756]{4,3,2,1,0:T(8,128)(2,1)} %get-tuple-element.155), channel_id=1, source_target_pairs={{1,0},{2,1},{3,2},{5,4},{6,5},{7,6},{9,8},{10,9},{11,10},{13,12},{... | collective-permute-start | bytes 290312 | tf_op jit(solution)/shard_map/ppermute | solution.py:25
  262.6 378.8 %reduce-scatter.2.cloned.1.call-start = ((), (), s32[]{:S(2)}) async-start(), calls=%async_computation.2 | async-start | bytes 19464192 | tf_op jit(solution)/shard_map/reduce_scatter | solution.py:246
  274.0 7.8 %copy-start.41 = (bf16[2,1,8,64,256]{4,3,2,0,1:T(8,128)(2,1)S(1)}, bf16[2,1,8,64,256]{4,3,2,0,1:T(8,128)(2,1)}, u32[]{:S(2)}) copy-start(bf16[2,1,8,64,256]{4,3,2,0,1:T(8,128)(2,1)} %copy-done.40) | copy-start | bytes 1572868
  274.4 7.7 %copy-start.77 = (bf16[2,1,8,64,256]{4,3,2,0,1:T(8,128)(2,1)S(1)}, bf16[2,1,8,64,256]{4,3,2,0,1:T(8,128)(2,1)}, u32[]{:S(2)}) copy-start(bf16[2,1,8,64,256]{4,3,2,0,1:T(8,128)(2,1)} %copy-done.76) | copy-start | bytes 1572868
  274.5 11.9 %collective-permute-start.12 = (bf16[2,1,1,64,256]{4,3,2,0,1:T(8,128)(2,1)S(1)}, bf16[2,1,1,64,256]{4,3,2,0,1:T(8,128)(2,1)S(1)}, u32[]{:S(2)}, u32[]{:S(2)}) collective-permute-start(bf16[2,1,1,64,256]{4,3,2,0,1:T(8,128)(2,1)S(1)} %get-tuple-element.230), channel_id=1, source_target_pairs={{0,1},{1,2},{2,3},{4,5},{5,6},{6,7},{8,9},{9,10},{10,11},{12,13},{... | collective-permute-start | bytes 196616 | tf_op jit(solution)/shard_map/ppermute | solution.py:24
  279.3 7.7 %collective-permute-start.13 = (bf16[2,1,1,64,256]{4,3,2,0,1:T(8,128)(2,1)S(1)}, bf16[2,1,1,64,256]{4,3,2,0,1:T(8,128)(2,1)S(1)}, u32[]{:S(2)}, u32[]{:S(2)}) collective-permute-start(bf16[2,1,1,64,256]{4,3,2,0,1:T(8,128)(2,1)S(1)} %get-tuple-element.231), channel_id=1, source_target_pairs={{1,0},{2,1},{3,2},{5,4},{6,5},{7,6},{9,8},{10,9},{11,10},{13,12},{... | collective-permute-start | bytes 196616 | tf_op jit(solution)/shard_map/ppermute | solution.py:25
  292.5 6.2 copy-start.75
  292.9 9.9 %collective-permute-start.14 = (bf16[2,1,1,64,256]{4,3,2,0,1:T(8,128)(2,1)S(1)}, bf16[2,1,1,64,256]{4,3,2,0,1:T(8,128)(2,1)S(1)}, u32[]{:S(2)}, u32[]{:S(2)}) collective-permute-start(bf16[2,1,1,64,256]{4,3,2,0,1:T(8,128)(2,1)S(1)} %get-tuple-element.226), channel_id=1, source_target_pairs={{0,1},{1,2},{2,3},{4,5},{5,6},{6,7},{8,9},{9,10},{10,11},{12,13},{... | collective-permute-start | bytes 196616 | tf_op jit(solution)/shard_map/ppermute | solution.py:24
  297.0 7.7 %collective-permute-start.15 = (bf16[2,1,1,64,256]{4,3,2,0,1:T(8,128)(2,1)S(1)}, bf16[2,1,1,64,256]{4,3,2,0,1:T(8,128)(2,1)S(1)}, u32[]{:S(2)}, u32[]{:S(2)}) collective-permute-start(bf16[2,1,1,64,256]{4,3,2,0,1:T(8,128)(2,1)S(1)} %get-tuple-element.227), channel_id=1, source_target_pairs={{1,0},{2,1},{3,2},{5,4},{6,5},{7,6},{9,8},{10,9},{11,10},{13,12},{... | collective-permute-start | bytes 196616 | tf_op jit(solution)/shard_map/ppermute | solution.py:25
  310.6 8.8 %collective-permute-start.16 = (bf16[2,1,1,64,256]{4,3,2,0,1:T(8,128)(2,1)S(1)}, bf16[2,1,1,64,256]{4,3,2,0,1:T(8,128)(2,1)S(1)}, u32[]{:S(2)}, u32[]{:S(2)}) collective-permute-start(bf16[2,1,1,64,256]{4,3,2,0,1:T(8,128)(2,1)S(1)} %get-tuple-element.222), channel_id=1, source_target_pairs={{0,1},{1,2},{2,3},{4,5},{5,6},{6,7},{8,9},{9,10},{10,11},{12,13},{... | collective-permute-start | bytes 196616 | tf_op jit(solution)/shard_map/ppermute | solution.py:24
  313.5 6.5 collective-permute-start.17
  339.1 7.9 %copy-start.16 = (f32[2,512,256]{2,1,0:T(8,128)S(1)}, f32[2,512,256]{2,1,0:T(8,128)}, u32[]{:S(2)}) copy-start(f32[2,512,256]{2,1,0:T(8,128)} %copy-done.14) | copy-start | bytes 3145732
  339.1 7.9 %copy-start.115 = (f32[2,512,256]{2,1,0:T(8,128)S(1)}, f32[2,512,256]{2,1,0:T(8,128)}, u32[]{:S(2)}) copy-start(f32[2,512,256]{2,1,0:T(8,128)} %get-tuple-element.270) | copy-start | bytes 3145732
  341.0 10.7 %copy-start.140 = (f32[2,256]{1,0:T(2,128)S(1)}, f32[2,256]{1,0:T(2,128)}, u32[]{:S(2)}) copy-start(f32[2,256]{1,0:T(2,128)} %get-tuple-element.125) | copy-start | bytes 6148
  341.0 10.7 %copy-start.141 = (f32[720]{0:T(1024)S(1)}, f32[720]{0:T(1024)}, u32[]{:S(2)}) copy-start(f32[720]{0:T(1024)} %get-tuple-element.116) | copy-start | bytes 8644
  341.0 10.7 %copy-start.142 = (f32[36]{0:T(128)S(1)}, f32[36]{0:T(128)}, u32[]{:S(2)}) copy-start(f32[36]{0:T(128)} %get-tuple-element.114) | copy-start | bytes 436
  341.0 53.0 %copy-start.128 = (f32[2804]{0:T(1024)S(1)}, f32[2804]{0:T(1024)}, u32[]{:S(2)}) copy-start(f32[2804]{0:T(1024)} %param.22) | copy-start | bytes 33652
  341.0 53.0 %copy-start.137 = (f32[2804]{0:T(1024)S(1)}, f32[2804]{0:T(1024)}, u32[]{:S(2)}) copy-start(f32[2804]{0:T(1024)} %param.28) | copy-start | bytes 33652
  341.0 53.0 %copy-start.138 = (f32[2804]{0:T(1024)S(1)}, f32[2804]{0:T(1024)}, u32[]{:S(2)}) copy-start(f32[2804]{0:T(1024)} %param.27) | copy-start | bytes 33652
  347.5 48.3 %collective-permute-start.18 = (bf16[2,1,1,64,256]{4,3,2,0,1:T(8,128)(2,1)S(1)}, bf16[2,1,1,64,256]{4,3,2,0,1:T(8,128)(2,1)S(1)}, u32[]{:S(2)}, u32[]{:S(2)}) collective-permute-start(bf16[2,1,1,64,256]{4,3,2,0,1:T(8,128)(2,1)S(1)} %get-tuple-element.218), channel_id=1, source_target_pairs={{0,1},{1,2},{2,3},{4,5},{5,6},{6,7},{8,9},{9,10},{10,11},{12,13},{... | collective-permute-start | bytes 196616 | tf_op jit(solution)/shard_map/ppermute | solution.py:24
  351.8 44.1 %collective-permute-start.19 = (bf16[2,1,1,64,256]{4,3,2,0,1:T(8,128)(2,1)S(1)}, bf16[2,1,1,64,256]{4,3,2,0,1:T(8,128)(2,1)S(1)}, u32[]{:S(2)}, u32[]{:S(2)}) collective-permute-start(bf16[2,1,1,64,256]{4,3,2,0,1:T(8,128)(2,1)S(1)} %get-tuple-element.219), channel_id=1, source_target_pairs={{1,0},{2,1},{3,2},{5,4},{6,5},{7,6},{9,8},{10,9},{11,10},{13,12},{... | collective-permute-start | bytes 196616 | tf_op jit(solution)/shard_map/ppermute | solution.py:25
  400.8 29.2 %copy-start.116 = (f32[72,756]{1,0:T(8,128)S(1)}, f32[72,756]{1,0:T(8,128)}, u32[]{:S(2)}) copy-start(f32[72,756]{1,0:T(8,128)} %param.21) | copy-start | bytes 653188
  400.8 29.2 %copy-start.125 = (f32[72,756]{1,0:T(8,128)S(1)}, f32[72,756]{1,0:T(8,128)}, u32[]{:S(2)}) copy-start(f32[72,756]{1,0:T(8,128)} %param.26) | copy-start | bytes 653188
  400.8 29.2 %copy-start.126 = (f32[72,756]{1,0:T(8,128)S(1)}, f32[72,756]{1,0:T(8,128)}, u32[]{:S(2)}) copy-start(f32[72,756]{1,0:T(8,128)} %param.25) | copy-start | bytes 653188
  401.1 242.2 %copy-start.78 = (f32[4,2,72,256]{3,2,1,0:T(8,128)S(1)}, f32[4,2,72,256]{3,2,1,0:T(8,128)}, u32[]{:S(2)}) copy-start(f32[4,2,72,256]{3,2,1,0:T(8,128)} %param.20) | copy-start | bytes 1769476
  401.1 242.2 %copy-start.117 = (f32[4,2,72,256]{3,2,1,0:T(8,128)S(1)}, f32[4,2,72,256]{3,2,1,0:T(8,128)}, u32[]{:S(2)}) copy-start(f32[4,2,72,256]{3,2,1,0:T(8,128)} %param.24) | copy-start | bytes 1769476
  401.2 242.2 %copy-start.118 = (f32[4,2,72,256]{3,2,1,0:T(8,128)S(1)}, f32[4,2,72,256]{3,2,1,0:T(8,128)}, u32[]{:S(2)}) copy-start(f32[4,2,72,256]{3,2,1,0:T(8,128)} %param.23) | copy-start | bytes 1769476
  (103 other events, 258.1 us)
Sparse Core Ops, SparseCore 0:
  11.7 84.9 all-gather.3
  100.0 58.7 all-gather.5
  262.8 166.1 all-reduce.13
  436.3 205.0 reduce-scatter.1
where the time goes:
time: 665 us; the launch traced here: 654 us
  waiting for transfers between devices  278 us (42%)
  local copies, waits for them, and re-layouts  102 us (15%)
  blocking collectives  83.2 us (13%)
  matrix products  61.8 us (9%)
  other arithmetic  56.3 us (8%)
  starting transfers between devices  51 us (8%)
  between operations  22.1 us (3%)
    reduce_scatter x1, waiting for transfers between devices, shards(): lax.psum_scatter(jnp.stack(tower_grads, 0), ('dp', 'tower'), scatter_dime...  211 us
    psum x1, blocking collectives, shards(): count_all = lax.psum(jnp.sum(own_chosen), ('dp', 'tower'))  42.3 us
    psum x1, blocking collectives, shards(): bias_grad, loss_total = lax.psum((bias_local, loss_local), ('dp', 'tower'))  40.9 us
    ppermute x10, starting transfers between devices, with_halo(): before = lax.ppermute(last, axis, up)  37.2 us
    unnamed x291, local copies, waits for them, and re-layouts  32 us
    unnamed x5, waiting for transfers between devices  27 us
    all_gather x1, waiting for transfers between devices, shards(): lax.all_gather(tower_weights.astype(jnp.bfloat16), ('dp', 'tower'), axis=...  25.6 us
    dot_general x54, matrix products, conv_forward(): jnp.einsum('snk,skm->snm', window, weight[:, tap_index * channels:(tap_in...  22.4 us
  transfers between devices with their start and end apart: 24, of which 10 were waited for; matrix products, arithmetic and copies ran while one was open for 23% of the time, Pallas kernels for 0%

commit v1 on v0

--- a/solution.py
+++ b/solution.py
@@ -3,6 +3,8 @@
 import jax
 import jax.numpy as jnp
 from jax import lax
+from jax.experimental import pallas as pl
+from jax.experimental.pallas import tpu as pltpu
 from jax.sharding import PartitionSpec as P
 
 beta_one = 0.9
@@ -141,7 +143,7 @@
     return jnp.sum(smooth * chosen_f[..., None])
 
 
-def shards(
+def plain_shards(
     features,
     crop_ids,
     labels,
@@ -289,6 +291,1080 @@
     )
 
 
+MESH = pl.DeviceIdType.MESH
+low = jnp.bfloat16
+full = jnp.float32
+LANES = 128
+CUT = 256
+
+
+def mega_kernel(
+    feat, code, goals, tow, hed, bias,
+    logits, deltas, fgrad, tgrad, hgrad, bsum, loss_out,
+    W, D, RD, RY, RZ, RX, RP, A3, HA, G, Z, U, ACC, FP, CP, GP, LS, ES, FS, FR, CNT, BG, BR,
+    ps, pr, zs, zr, ys, yr, ds, dr, xs, xr, fs, fr, hs, hr, gs, gr, ls, lr, es, er,
+    rds, rdr, rys, ryr, rzs, rzr, rxs, rxr, rps, rpr, ns, nr, bs, br,
+    *, rows, cols, layers, cls_out, box_out, anchors, piece,
+):
+    d = lax.axis_index("dp")
+    z = lax.axis_index("tower")
+    k = lax.rem(d, 2)
+    x = lax.rem(d // 2, 2)
+    y = d // 4
+    sib = d + 1 - 2 * k
+    par = d + 2 - 4 * x
+    yn = d + 4 - 8 * y
+    is_cls = x == 0
+    is_box = x == 1
+    block = 4 * piece
+    px = rows * cols
+    classes = cls_out // anchors
+
+    def remote(src, dst, send, recv, dev):
+        return pltpu.make_async_remote_copy(
+            src_ref=src, dst_ref=dst, send_sem=send, recv_sem=recv, device_id=dev, device_id_type=MESH
+        )
+
+    def blk(yy, xx, kk):
+        return pl.ds(((yy * 2 + xx) * 2 + kk) * block, block)
+
+    def pcs(yy, xx, kk, zz):
+        return pl.ds(((yy * 2 + xx) * 2 + kk) * block + zz * piece, piece)
+
+    def zpeer(o):
+        return lax.rem(z + o, 4)
+
+    def zfrom(o):
+        return lax.rem(z + 4 - o, 4)
+
+    barrier = pltpu.get_barrier_semaphore()
+    for dev in [(sib, z), (par, z), (yn, z)] + [(d, zpeer(o)) for o in (1, 2, 3)]:
+        pl.semaphore_signal(barrier, inc=1, device_id=dev, device_id_type=MESH)
+    pl.semaphore_wait(barrier, 6)
+
+    def slot_of(step):
+        return jnp.where(step == 4, 4 + 2 * x, step)
+
+    def p_send(step):
+        return remote(
+            tow.at[step, 1 - x], W.at[step, pcs(y, x, k, z)], ps.at[step], pr.at[step], (par, z)
+        )
+
+    def p_head(cut, index):
+        return remote(
+            hed.at[cut], W.at[4 + cut, pcs(y, x, k, z)], ps.at[index], pr.at[index], (par, z)
+        )
+
+    def p_recv(step):
+        slot = slot_of(step)
+        there = W.at[slot, pcs(y, 1 - x, k, z)]
+        return remote(there, there, ps.at[step], pr.at[step], (par, z))
+
+    def z_send(step, xx, o):
+        here = W.at[slot_of(step), pcs(y, xx, k, z)]
+        return remote(here, here, zs.at[step, xx, o - 1], zr.at[step, xx, o - 1], (d, zpeer(o)))
+
+    def z_recv(step, xx, o):
+        here = W.at[slot_of(step), pcs(y, xx, k, zfrom(o))]
+        return remote(here, here, zs.at[step, xx, o - 1], zr.at[step, xx, o - 1], (d, zpeer(o)))
+
+    def y_copy(step, xx, yy):
+        here = W.at[slot_of(step), blk(yy, xx, k)]
+        return remote(here, here, ys.at[step, xx], yr.at[step, xx], (yn, z))
+
+    def d_copy(slot, yy, xx, kk):
+        here = W.at[slot, blk(yy, xx, kk)]
+        return remote(here, here, ds.at[slot, yy * 2 + xx], dr.at[slot, yy * 2 + xx], (sib, z))
+
+    def x_copy(yy, xx):
+        here = W.at[6, blk(yy, xx, k)]
+        return remote(here, here, xs.at[yy * 2 + xx], xr.at[yy * 2 + xx], (par, z))
+
+    def has(step):
+        return (step < 5) | is_cls
+
+    def do_z(step):
+        @pl.when(has(step))
+        def _():
+            p_recv(step).wait_recv()
+            for o in (1, 3, 2):
+                for xx in range(2):
+                    z_send(step, xx, o).start()
+
+    def spread(step, yy):
+        slot = slot_of(step)
+        for xx in range(2):
+            d_copy(slot, yy, xx, k).start()
+
+        @pl.when(is_box & (step == 4))
+        def _():
+            for xx in range(2):
+                x_copy(yy, xx).start()
+
+    def do_y(step):
+        @pl.when(has(step))
+        def _():
+            for xx in range(2):
+                for o in (1, 2, 3):
+                    z_recv(step, xx, o).wait_recv()
+            for xx in range(2):
+                y_copy(step, xx, y).start()
+            spread(step, y)
+
+    def do_d(step):
+        @pl.when(has(step))
+        def _():
+            for xx in range(2):
+                y_copy(step, xx, 1 - y).wait_recv()
+            spread(step, 1 - y)
+
+    def gathered(slot):
+        for b in range(4):
+            d_copy(slot, b // 2, b % 2, 1 - k).wait_recv()
+
+    for step in range(4):
+        p_send(step).start()
+        if step == 0:
+            pltpu_feature = remote(feat, FP, fs.at[0], fr.at[0], (par, z))
+        W[step, pcs(y, x, k, z)] = tow[step, x]
+    pltpu_feature.start()
+
+    @pl.when(is_cls)
+    def _():
+        p_head(2, 4).start()
+        W[4, pcs(y, x, k, z)] = hed[0]
+        W[5, pcs(y, x, k, z)] = hed[1]
+
+    @pl.when(is_box)
+    def _():
+        p_head(0, 4).start()
+        p_head(1, 5).start()
+        W[6, pcs(y, x, k, z)] = hed[2]
+
+    code_copy = remote(code, CP.at[x], fs.at[1], fr.at[1], (par, z))
+    code_copy.start()
+    goal_copy = remote(goals, GP.at[x], fs.at[2], fr.at[2], (par, z))
+    CP[x] = code[...]
+    GP[x] = goals[...]
+
+    @pl.when(is_cls)
+    def _():
+        goal_copy.start()
+
+    do_z(0)
+    do_z(1)
+
+    def n_copy(index, dst, dev):
+        return remote(CNT.at[index], CNT.at[dst], ns.at[dst], nr.at[dst], dev)
+
+    picked = (code[...].astype(full) < -110.0).astype(full)
+    CNT[0] = jnp.broadcast_to(jnp.sum(picked.reshape(px // 8, 8, LANES), axis=0).sum(), (8, LANES))
+    n_copy(0, 4, (sib, z)).start()
+
+    col = lax.broadcasted_iota(jnp.int32, (cols, CUT), 0)
+    first_col = col == 0
+    last_col = col == cols - 1
+
+    def move_right(v):
+        return jnp.where(first_col, 0.0, pltpu.roll(v, 1, 0))
+
+    def move_left(v):
+        return jnp.where(last_col, 0.0, pltpu.roll(v, cols - 1, 0))
+
+    def put_row(layer, cv, row, value):
+        at = pl.ds(pl.multiple_of(row * cols, cols), cols)
+        A3[layer, cv, at, 0:CUT] = move_right(value).astype(low)
+        A3[layer, cv, at, CUT : 2 * CUT] = value.astype(low)
+        A3[layer, cv, at, 2 * CUT : 3 * CUT] = move_left(value).astype(low)
+
+    def up_ok():
+        return z > 0
+
+    def down_ok():
+        return z < 3
+
+    def a_edge(layer, side, cv):
+        row = rows if side == 0 else 1
+        src = A3.at[layer, cv, pl.ds(row * cols, cols), pl.ds(CUT, CUT)]
+        dev = (d, lax.rem(z + 1, 4)) if side == 0 else (d, lax.rem(z + 3, 4))
+        return remote(src, HA.at[layer, side, cv], hs.at[layer, side, cv], hr.at[layer, side, cv], dev)
+
+    def send_edges(layer, cvs):
+        @pl.when(down_ok())
+        def _():
+            for cv in cvs:
+                a_edge(layer, 0, cv).start()
+
+        @pl.when(up_ok())
+        def _():
+            for cv in cvs:
+                a_edge(layer, 1, cv).start()
+
+    def take_edges(layer):
+        @pl.when(up_ok())
+        def _():
+            for cv in range(2):
+                a_edge(layer, 0, cv).wait_recv()
+                put_row(layer, cv, 0, HA[layer, 0, cv].astype(full))
+
+        @pl.when(down_ok())
+        def _():
+            for cv in range(2):
+                a_edge(layer, 1, cv).wait_recv()
+                put_row(layer, cv, rows + 1, HA[layer, 1, cv].astype(full))
+
+    def g_edge(slot, side, cv):
+        src = G.at[slot, cv, pl.ds((rows if side == 0 else 1) * cols, cols)]
+        dst = G.at[slot, cv, pl.ds(0 if side == 0 else (rows + 1) * cols, cols)]
+        dev = (d, lax.rem(z + 1, 4)) if side == 0 else (d, lax.rem(z + 3, 4))
+        return remote(src, dst, gs.at[slot, side, cv], gr.at[slot, side, cv], dev)
+
+    def g_recv(slot, side, cv):
+        dst = G.at[slot, cv, pl.ds(0 if side == 0 else (rows + 1) * cols, cols)]
+        return remote(dst, dst, gs.at[slot, side, cv], gr.at[slot, side, cv], (d, lax.rem(z + 1, 4)))
+
+    def send_g(slot):
+        @pl.when(down_ok())
+        def _():
+            for cv in range(2):
+                g_edge(slot, 0, cv).start()
+
+        @pl.when(up_ok())
+        def _():
+            for cv in range(2):
+                g_edge(slot, 1, cv).start()
+
+    def take_g(slot):
+        @pl.when(up_ok())
+        def _():
+            for cv in range(2):
+                g_recv(slot, 0, cv).wait_recv()
+
+        @pl.when(down_ok())
+        def _():
+            for cv in range(2):
+                g_recv(slot, 1, cv).wait_recv()
+
+    def fill(layer_src, cv):
+        def body(r, carry):
+            put_row(0, cv, r + 1, layer_src[pl.ds(pl.multiple_of(r * cols, cols), cols), :].astype(full))
+            return carry
+
+        lax.fori_loop(0, rows, body, 0)
+
+    fill(feat, x)
+    send_edges(0, [x])
+
+    def clear(at, layer_count, slot_count):
+        def a_body(layer, carry):
+            for cv in range(2):
+                A3[layer, cv, at, :] = jnp.zeros((cols, 3 * CUT), low)
+            return carry
+
+        def g_body(slot, carry):
+            for cv in range(2):
+                G[slot, cv, at, :] = jnp.zeros((cols, CUT), low)
+            return carry
+
+        lax.fori_loop(0, layer_count, a_body, 0)
+        lax.fori_loop(0, slot_count, g_body, 0)
+
+    @pl.when(z == 0)
+    def _():
+        clear(pl.ds(0, cols), layers + 1, layers + 3)
+
+    @pl.when(z == 3)
+    def _():
+        clear(pl.ds((rows + 1) * cols, cols), layers + 1, layers + 3)
+
+    BG[...] = jnp.zeros((8, CUT), full)
+
+    n_copy(0, 4, (sib, z)).wait_recv()
+    CNT[1] = CNT[0] + CNT[4]
+    n_copy(1, 5, (yn, z)).start()
+    do_y(0)
+    do_z(2)
+    n_copy(1, 5, (yn, z)).wait_recv()
+    CNT[2] = CNT[1] + CNT[5]
+    n_copy(2, 6, (par, z)).start()
+    pltpu_feature.wait_recv()
+    fill(FP, 1 - x)
+    send_edges(0, [1 - x])
+    n_copy(2, 6, (par, z)).wait_recv()
+    CNT[3] = CNT[2] + CNT[6]
+    for o in (1, 2, 3):
+        n_copy(3, 6 + o, (d, zpeer(o))).start()
+    do_y(1)
+    do_d(0)
+    do_z(3)
+
+    def conv(layer, slot, cv):
+        total = None
+        for dy in range(3):
+            term = jnp.dot(
+                A3[layer, cv, pl.ds(dy * cols, px), :],
+                W[slot, pl.ds(dy * 96, 96)].reshape(3 * CUT, CUT),
+                preferred_element_type=full,
+            )
+            total = term if total is None else total + term
+        return total
+
+    def forward(layer, carry):
+        gathered(layer)
+        take_edges(layer)
+        shift = bias[pl.ds(2 * layer + x, 1), :]
+
+        def canvas(cv, carry):
+            Z[layer, cv] = conv(layer, layer, cv)
+
+            def row(r, carry):
+                at = pl.ds(pl.multiple_of(r * cols, cols), cols)
+                value = Z[layer, cv, at, :] + shift
+                Z[layer, cv, at, :] = value
+                put_row(layer + 1, cv, r + 1, silu_value(value))
+                return carry
+
+            lax.fori_loop(0, rows, row, 0)
+            return carry
+
+        lax.fori_loop(0, 2, canvas, 0)
+        send_edges(layer + 1, range(2))
+        do_y_when = layer + 2
+        do_y(do_y_when)
+        do_d(layer + 1)
+
+        @pl.when(layer < 2)
+        def _():
+            do_z(layer + 4)
+
+        return carry
+
+    lax.fori_loop(0, layers, forward, 0)
+    do_d(5)
+    for o in (1, 2, 3):
+        n_copy(3, 6 + o, (d, zpeer(o))).wait_recv()
+    count = CNT[3] + CNT[7] + CNT[8] + CNT[9]
+    grad_scale = (1.0 / jnp.maximum(count, 1.0))[0:1, 0:1]
+    take_edges(layers)
+
+    def rd_send(slot, b):
+        src = D.at[slot, blk(b // 2, b % 2, 1 - k)]
+        return remote(src, RD.at[slot, b], rds.at[slot, b], rdr.at[slot, b], (sib, z))
+
+    def ry_send(slot, xx):
+        src = D.at[slot, blk(1 - y, xx, k)]
+        return remote(src, RY.at[slot, xx], rys.at[slot, xx], ryr.at[slot, xx], (yn, z))
+
+    def rz_send(slot, xx, o):
+        src = D.at[slot, pcs(y, xx, k, zpeer(o))]
+        return remote(
+            src, RZ.at[slot, xx, o - 1], rzs.at[slot, xx, o - 1], rzr.at[slot, xx, o - 1], (d, zpeer(o))
+        )
+
+    def rx_send(b):
+        src = D.at[6, blk(b // 2, b % 2, k)]
+        return remote(src, RX.at[b], rxs.at[b], rxr.at[b], (par, z))
+
+    def add_into(slot, place, terms):
+        units = block // 3
+
+        def body(i, carry):
+            here = pl.ds(place + i * units, units)
+            there = pl.ds(i * units, units)
+            total = D[slot, here].astype(full)
+            for ref in terms:
+                total = total + ref[there].astype(full)
+            D[slot, here] = total.astype(low)
+            return carry
+
+        lax.fori_loop(0, 3, body, 0)
+
+    def start_of(yy, xx, kk):
+        return ((yy * 2 + xx) * 2 + kk) * block
+
+    def do_rd(slot):
+        for b in range(4):
+            rd_send(slot, b).start()
+
+    def do_ry(slot, relay=False):
+        for xx in range(2):
+            b = (1 - y) * 2 + xx
+            rd_send(slot, b).wait_recv()
+            terms = [RD.at[slot, b]]
+            if relay:
+                rx_send(b).wait_recv()
+                terms.append(RX.at[b])
+            add_into(slot, start_of(1 - y, xx, k), terms)
+            ry_send(slot, xx).start()
+        for xx in range(2):
+            b = y * 2 + xx
+            rd_send(slot, b).wait_recv()
+            terms = [RD.at[slot, b]]
+            if relay:
+                rx_send(b).wait_recv()
+                terms.append(RX.at[b])
+            add_into(slot, start_of(y, xx, k), terms)
+
+    def do_rx():
+        for b in range(4):
+            rd_send(6, b).wait_recv()
+            add_into(6, start_of(b // 2, b % 2, k), [RD.at[6, b]])
+            rx_send(b).start()
+
+    def do_rz(slot):
+        for xx in range(2):
+            ry_send(slot, xx).wait_recv()
+            add_into(slot, start_of(y, xx, k), [RY.at[slot, xx]])
+            for o in (2, 1, 3):
+                rz_send(slot, xx, o).start()
+
+    def piece_sum(slot, xx):
+        total = D[slot, pcs(y, xx, k, z)].astype(full)
+        for o in (1, 2, 3):
+            rz_send(slot, xx, o).wait_recv()
+            total = total + RZ[slot, xx, o - 1].astype(full)
+        return total
+
+    def rp_send(slot, dst):
+        return remote(RP.at[slot], dst, rps.at[slot], rpr.at[slot], (par, z))
+
+    def do_rp(slot, dst_own, dst_other):
+        RP[slot] = piece_sum(slot, 1 - x)
+        rp_send(slot, dst_other).start()
+        dst_own[...] = piece_sum(slot, x)
+
+    def do_rp_layer(layer):
+        do_rp(layer, tgrad.at[layer, x], tgrad.at[layer, x])
+
+    def do_rp_head(slot):
+        do_rp(slot, hgrad.at[slot - 4], hgrad.at[slot - 4])
+
+    def weight_grad(layer, slot):
+        for dy in range(3):
+            total = None
+            for cv in range(2):
+                term = lax.dot_general(
+                    A3[layer, cv, pl.ds(dy * cols, px), :],
+                    G[slot, cv, pl.ds(cols, px), :],
+                    (((0,), (0,)), ((), ())),
+                    preferred_element_type=full,
+                )
+                total = term if total is None else total + term
+            D[slot, pl.ds(dy * 96, 96)] = total.astype(low).reshape(96, 8, CUT)
+
+    def input_grad(slot, add):
+        def canvas(cv, carry):
+            for dx in range(3):
+                total = None
+                for dy in range(3):
+                    term = lax.dot_general(
+                        G[slot, cv, pl.ds((2 - dy) * cols, px), :],
+                        W[slot, pl.ds((3 * dy + dx) * 32, 32)].reshape(CUT, CUT),
+                        (((1,), (1,)), ((), ())),
+                        preferred_element_type=full,
+                    )
+                    total = term if total is None else total + term
+                if add:
+                    U[dx, cv] = U[dx, cv] + total
+                else:
+                    U[dx, cv] = total
+            return carry
+
+        lax.fori_loop(0, 2, canvas, 0)
+
+    def upstream_row(cv, r):
+        at = pl.ds(pl.multiple_of(r * cols, cols), cols)
+        return U[1, cv, at, :] + move_left(U[0, cv, at, :]) + move_right(U[2, cv, at, :])
+
+    def fold(value):
+        return jnp.sum(value.reshape(cols // 8, 8, CUT), axis=0)
+
+    lane = lax.broadcasted_iota(jnp.int32, (1, CUT), 1)
+    lane_tab = lax.broadcasted_iota(jnp.int32, (LANES, CUT), 1)
+    anchor_tab = lax.broadcasted_iota(jnp.int32, (LANES, CUT), 0)
+    box_from = cls_out - 2 * CUT
+
+    def cls_rows(cut, cv, shift):
+        channel = lane_tab + cut * CUT
+        spread_tab = (
+            (channel >= anchor_tab * classes) & (channel < (anchor_tab + 1) * classes) & (channel < cls_out)
+        ).astype(full).astype(low)
+        here = lane + cut * CUT
+        number = here
+        for a in range(1, anchors):
+            number = number - jnp.where(here >= a * classes, classes, 0)
+        number = number.astype(full) - 200.0
+
+        def row(r, carry):
+            b_sum, l_sum = carry
+            at = pl.ds(pl.multiple_of(r * cols, cols), cols)
+            raw = ACC[at, :] + shift
+            LS[cut, cv, at, :] = raw.astype(low)
+            marks = jnp.dot(CP[cv, at, :], spread_tab, preferred_element_type=full)
+            hit = marks == number
+            seen = marks < -50.0
+            s = jnp.where(hit, -raw, raw)
+            e = jnp.exp(-jnp.abs(s))
+            inv = 1.0 / (1.0 + e)
+            other = e * inv
+            q = jnp.where(s >= 0.0, inv, other)
+            p = jnp.where(s >= 0.0, other, inv)
+            soft = jnp.maximum(s, 0.0) + jnp.log1p(e)
+            t = jnp.where(seen, jnp.where(hit, focal_alpha, 1.0 - focal_alpha), 0.0) * q * q
+            slope = t * (2.0 * p * soft + q) * grad_scale
+            g = jnp.where(hit, -slope, slope).astype(low)
+            G[4 + cut, cv, pl.ds(pl.multiple_of((r + 1) * cols, cols), cols), :] = g
+            return b_sum + fold(g.astype(full)), l_sum + fold(t * soft)
+
+        return row
+
+    def box_rows(cut, cv, shift):
+        spot = lane_tab - box_from
+        spread_tab = (
+            (spot >= anchor_tab * 4) & (spot < (anchor_tab + 1) * 4) & (anchor_tab < anchors)
+        ).astype(full).astype(low)
+
+        def row(r, carry):
+            b_sum, l_sum = carry
+            at = pl.ds(pl.multiple_of(r * cols, cols), cols)
+            raw = ACC[at, :] + shift
+            ES[cv, at, :] = raw.astype(low)
+            marks = jnp.dot(CP[cv, at, :], spread_tab, preferred_element_type=full)
+            chosen = marks < -110.0
+            want = GP[cv, at, :]
+            want = jnp.concatenate([jnp.zeros((cols, LANES), full), want], axis=1)
+            diff = raw - want
+            size = jnp.abs(diff)
+            value = jnp.where(
+                size < smooth_beta, 0.5 * diff * diff / smooth_beta, size - 0.5 * smooth_beta
+            )
+            slope = jnp.where(
+                size < smooth_beta, diff / smooth_beta, jnp.where(diff > 0.0, 1.0, -1.0)
+            )
+            g = jnp.where(chosen, slope * grad_scale, 0.0).astype(low)
+            G[4 + cut, cv, pl.ds(pl.multiple_of((r + 1) * cols, cols), cols), :] = g
+            return b_sum + fold(g.astype(full)), l_sum + fold(jnp.where(chosen, value, 0.0))
+
+        return row
+
+    nothing = jnp.zeros((8, CUT), full)
+
+    def l_copy(cut):
+        return remote(LS.at[cut, 1 - x], logits.at[cut], ls.at[cut], lr.at[cut], (par, z))
+
+    def e_copy():
+        return remote(ES.at[1 - x], deltas, es.at[0], er.at[0], (par, z))
+
+    U[...] = jnp.zeros(U.shape, full)
+    remote(code, CP.at[1 - x], fs.at[1], fr.at[1], (par, z)).wait_recv()
+
+    @pl.when(is_box)
+    def _():
+        remote(goals, GP.at[1 - x], fs.at[2], fr.at[2], (par, z)).wait_recv()
+
+    def head(cut, carry):
+        slot = 4 + cut
+
+        @pl.when(is_cls & (cut == 2))
+        def _():
+            for b in range(4):
+                x_copy(b // 2, b % 2).wait_recv()
+                d_copy(6, b // 2, b % 2, k).start()
+
+        gathered(slot)
+        shift = bias[pl.ds(2 * layers + cut, 1), :]
+
+        def canvas(cv, carry):
+            b_sum, l_sum = carry
+            ACC[...] = conv(layers, slot, cv)
+            return lax.cond(
+                is_cls,
+                lambda: lax.fori_loop(0, rows, cls_rows(cut, cv, shift), (b_sum, l_sum)),
+                lambda: lax.fori_loop(0, rows, box_rows(cut, cv, shift), (b_sum, l_sum)),
+            )
+
+        b_sum, l_sum = lax.fori_loop(0, 2, canvas, (nothing, nothing))
+        send_g(slot)
+
+        @pl.when(is_cls)
+        def _():
+            l_copy(cut).start()
+
+        @pl.when(is_box)
+        def _():
+            e_copy().start()
+
+        BG[pl.ds(slot, 1), :] = jnp.sum(b_sum, axis=0, keepdims=True)
+        BG[pl.ds(7, 1), :] = BG[pl.ds(7, 1), :] + jnp.sum(l_sum, axis=0, keepdims=True)
+        weight_grad(layers, slot)
+        do_rd(slot)
+
+        @pl.when(is_cls & (cut == 1))
+        def _():
+            do_ry(4)
+
+        @pl.when(is_cls & (cut == 2))
+        def _():
+            do_ry(5)
+            do_rz(4)
+
+        take_g(slot)
+        input_grad(slot, True)
+        return carry
+
+    lax.fori_loop(2 * x, 3, head, 0)
+
+    @pl.when(is_cls)
+    def _():
+        do_rx()
+        for cut in range(3):
+            logits[cut] = LS[cut, 0]
+
+    @pl.when(is_box)
+    def _():
+        deltas[...] = ES[1]
+
+    def b_copy(src, dst, dev):
+        return remote(src, BR.at[dst], bs.at[dst], br.at[dst], dev)
+
+    def backward(j, carry):
+        layer = layers - 1 - j
+
+        def canvas(cv, b_sum):
+            def row(r, b_sum):
+                at = pl.ds(pl.multiple_of(r * cols, cols), cols)
+                g = (upstream_row(cv, r) * silu_slope(Z[layer, cv, at, :])).astype(low)
+                G[layer, cv, pl.ds(pl.multiple_of((r + 1) * cols, cols), cols), :] = g
+                return b_sum + fold(g.astype(full))
+
+            return lax.fori_loop(0, rows, row, b_sum)
+
+        b_sum = lax.fori_loop(0, 2, canvas, nothing)
+        send_g(layer)
+        BG[pl.ds(layer, 1), :] = jnp.sum(b_sum, axis=0, keepdims=True)
+        weight_grad(layer, layer)
+        do_rd(layer)
+
+        @pl.when(j == 3)
+        def _():
+            b_copy(BG, 0, (sib, z)).start()
+
+        @pl.when(j > 0)
+        def _():
+            do_ry(layer + 1)
+
+        @pl.when(j > 1)
+        def _():
+            do_rz(layer + 2)
+
+        @pl.when(j > 2)
+        def _():
+            do_rp_layer(3)
+
+        @pl.when(is_cls & (j == 0))
+        def _():
+            do_rz(5)
+            do_rp_head(4)
+
+        @pl.when(is_cls & (j == 1))
+        def _():
+            do_rp_head(5)
+
+        @pl.when(is_box & (j == 1))
+        def _():
+            do_ry(6, relay=True)
+
+        @pl.when(is_box & (j == 2))
+        def _():
+            do_rz(6)
+
+        @pl.when(is_box & (j == 3))
+        def _():
+            do_rp_head(6)
+
+        take_g(layer)
+        input_grad(layer, False)
+        return carry
+
+    lax.fori_loop(0, layers, backward, 0)
+
+    def feature_rows(cv, dst):
+        def row(r, carry):
+            dst[pl.ds(pl.multiple_of(r * cols, cols), cols), :] = upstream_row(cv, r)
+            return carry
+
+        lax.fori_loop(0, rows, row, 0)
+
+    f_copy = remote(FS, FR, fs.at[3], fr.at[3], (par, z))
+    feature_rows(1 - x, FS)
+    f_copy.start()
+    do_ry(0)
+    do_rz(1)
+    do_rp_layer(2)
+    b_copy(BG, 0, (sib, z)).wait_recv()
+    BR[6] = BG[...] + BR[0]
+    b_copy(BR.at[6], 1, (yn, z)).start()
+    feature_rows(x, fgrad)
+    b_copy(BR.at[6], 1, (yn, z)).wait_recv()
+    total = BR[6] + BR[1]
+    for zz in range(4):
+        @pl.when(z == zz)
+        def _():
+            BR[7 + zz] = total
+            for o in (1, 2, 3):
+                remote(
+                    BR.at[7 + zz], BR.at[7 + zz], bs.at[1 + o], br.at[1 + o], (d, zpeer(o))
+                ).start()
+    do_rz(0)
+    do_rp_layer(1)
+    for o in (1, 2, 3):
+        for zz in range(4):
+            @pl.when(zfrom(o) == zz)
+            def _():
+                remote(
+                    BR.at[7 + zz], BR.at[7 + zz], bs.at[1 + o], br.at[1 + o], (d, zpeer(o))
+                ).wait_recv()
+    total = (BR[7] + BR[8]) + (BR[9] + BR[10])
+    BR[5] = total
+    last = remote(BR.at[5], bsum.at[x], bs.at[5], br.at[5], (par, z))
+    last.start()
+    bsum[x] = total
+    f_copy.wait_recv()
+    fgrad[...] = fgrad[...] + FR[...]
+    do_rp_layer(0)
+    remote(BR.at[5], bsum.at[1 - x], bs.at[5], br.at[5], (par, z)).wait_recv()
+    loss = jnp.sum(bsum[0, 7:8, :] + bsum[1, 7:8, :], axis=1, keepdims=True)
+    loss_out[...] = jnp.broadcast_to(loss, (8, LANES)) / jnp.maximum(count, 1.0)
+
+    for layer in range(layers):
+        rp_send(layer, tgrad.at[layer, 1 - x]).wait_recv()
+
+    @pl.when(is_cls)
+    def _():
+        rp_send(6, hgrad.at[2]).wait_recv()
+        e_copy().wait_recv()
+        for b in range(4):
+            rx_send(b).wait_send()
+            d_copy(6, b // 2, b % 2, k).wait_send()
+        for cut in range(3):
+            l_copy(cut).wait_send()
+        p_head(2, 4).wait_send()
+        goal_copy.wait_send()
+
+    @pl.when(is_box)
+    def _():
+        for cut in range(2):
+            rp_send(4 + cut, hgrad.at[cut]).wait_recv()
+        for cut in range(3):
+            l_copy(cut).wait_recv()
+        for b in range(4):
+            x_copy(b // 2, b % 2).wait_send()
+            d_copy(6, b // 2, b % 2, k).wait_send()
+        e_copy().wait_send()
+        p_head(0, 4).wait_send()
+        p_head(1, 5).wait_send()
+
+    def close_gather(step, carry):
+        for xx in range(2):
+            for o in (1, 2, 3):
+                z_send(step, xx, o).wait_send()
+            y_copy(step, xx, y).wait_send()
+        return carry
+
+    lax.fori_loop(0, 6 - x, close_gather, 0)
+
+    def close_slot(slot, carry):
+        @pl.when((slot < 4) | is_cls)
+        def _():
+            for b in range(4):
+                d_copy(slot, b // 2, b % 2, k).wait_send()
+
+        return carry
+
+    lax.fori_loop(0, 6 - 2 * x, close_slot, 0)
+
+    def close_layer(layer, carry):
+        @pl.when(layer < layers)
+        def _():
+            p_send(jnp.minimum(layer, layers - 1)).wait_send()
+
+        @pl.when(down_ok())
+        def _():
+            for cv in range(2):
+                a_edge(layer, 0, cv).wait_send()
+
+        @pl.when(up_ok())
+        def _():
+            for cv in range(2):
+                a_edge(layer, 1, cv).wait_send()
+
+        return carry
+
+    lax.fori_loop(0, layers + 1, close_layer, 0)
+
+    def close_grad(slot, carry):
+        @pl.when(is_cls | (slot < 4) | (slot == 6))
+        def _():
+            for b in range(4):
+                rd_send(slot, b).wait_send()
+
+            @pl.when(down_ok())
+            def _():
+                for cv in range(2):
+                    g_edge(slot, 0, cv).wait_send()
+
+            @pl.when(up_ok())
+            def _():
+                for cv in range(2):
+                    g_edge(slot, 1, cv).wait_send()
+
+        @pl.when((slot < 4) | (is_cls & (slot < 6)) | (is_box & (slot == 6)))
+        def _():
+            for xx in range(2):
+                ry_send(slot, xx).wait_send()
+                for o in (1, 2, 3):
+                    rz_send(slot, xx, o).wait_send()
+            rp_send(slot, RP.at[slot]).wait_send()
+
+        return carry
+
+    lax.fori_loop(0, layers + 3, close_grad, 0)
+    pltpu_feature.wait_send()
+    code_copy.wait_send()
+    f_copy.wait_send()
+    n_copy(0, 4, (sib, z)).wait_send()
+    n_copy(1, 5, (yn, z)).wait_send()
+    n_copy(2, 6, (par, z)).wait_send()
+    b_copy(BG, 0, (sib, z)).wait_send()
+    b_copy(BR.at[6], 1, (yn, z)).wait_send()
+    for o in (1, 2, 3):
+        n_copy(3, 6 + o, (d, zpeer(o))).wait_send()
+        remote(BR.at[7], BR.at[7], bs.at[1 + o], br.at[1 + o], (d, zpeer(o))).wait_send()
+    last.wait_send()
+
+
+def finish_kernel(
+    scal, lg, dl, fg, tg, hg, tw, hw, tm, tv, hm, hv,
+    o_lg, o_dl, o_fg, o_tg, o_bg, o_hg, o_tn, o_hn, o_tm, o_tv, o_hm, o_hv, o_tc, o_hc,
+    *, layers, cls_out, box_out,
+):
+    tail = cls_out - 2 * CUT
+
+    def adam(weight, grad, first, second):
+        first_new = beta_one * first + (1.0 - beta_one) * grad
+        second_new = beta_two * second + (1.0 - beta_two) * grad * grad
+        first_hat = first_new / scal[0]
+        second_hat = second_new / scal[1]
+        weight_new = weight - learn_rate * (
+            first_hat / (jnp.sqrt(second_hat) + adam_eps) + decay_rate * weight
+        )
+        return weight_new, first_new, second_new
+
+    def layer_body(layer, carry):
+        for t in range(2):
+            grad = tg[layer, t]
+            (o_tg if t == 0 else o_bg)[layer] = grad
+            w_new, m_new, v_new = adam(tw[layer, t], grad, tm[layer, t], tv[layer, t])
+            o_tn[layer, t] = w_new
+            o_tm[layer, t] = m_new
+            o_tv[layer, t] = v_new
+            o_tc[layer, t] = w_new.astype(low)
+        return carry
+
+    lax.fori_loop(0, layers, layer_body, 0)
+    for cut, width in ((0, CUT), (1, CUT), (2, tail + box_out)):
+        at = slice(cut * CUT, cut * CUT + width)
+        grad = hg[cut][:, :width]
+        o_hg[:, at] = grad
+        w_new, m_new, v_new = adam(hw[:, at], grad, hm[:, at], hv[:, at])
+        o_hn[:, at] = w_new
+        o_hm[:, at] = m_new
+        o_hv[:, at] = v_new
+        o_hc[:, at] = w_new.astype(low)
+        if cut < 2:
+            o_lg[:, at] = lg[cut]
+        else:
+            o_lg[:, cut * CUT : cls_out] = lg[cut][:, :tail]
+    o_dl[...] = dl[:, tail : tail + box_out]
+    o_fg[...] = fg[...]
+
+
+def fused_shards(
+    features,
+    crop_ids,
+    labels,
+    positive,
+    box_targets,
+    tower_weights,
+    head_weights,
+    biases,
+    tower_m,
+    tower_v,
+    head_m,
+    head_v,
+    bias_m,
+    bias_v,
+    step_count,
+):
+    canvases, rows, cols, channels = features.shape
+    layers = tower_weights.shape[0]
+    shard_rows = tower_weights.shape[2]
+    anchors = labels.shape[-1]
+    head_out = head_weights.shape[1]
+    box_out = 4 * anchors
+    cls_out = head_out - box_out
+    px = rows * cols
+    piece = shard_rows // 8
+    box_from = cls_out - 2 * CUT - LANES
+    shard = lax.axis_index("tower")
+    same_rows = crop_ids[:, 1:] == crop_ids[:, :-1]
+    edge_true = jnp.ones((crop_ids.shape[0], 1), dtype=jnp.bool_)
+    row_ok = jnp.concatenate([edge_true, same_rows], 1) & jnp.concatenate([same_rows, edge_true], 1)
+    own_ok = lax.dynamic_slice_in_dim(row_ok, shard * rows, rows, 1)
+    valid = (labels >= 0) & own_ok[:, :, None, None]
+    code = jnp.where(valid, jnp.where(positive > 0, labels - 200, -100), 0).astype(low)
+    code = jnp.pad(code.reshape(px, anchors), ((0, 0), (0, LANES - anchors)))
+    goals = jnp.pad(
+        box_targets.reshape(px, box_out), ((0, 0), (box_from, LANES - box_from - box_out))
+    )
+    tow = tower_weights.astype(low).reshape(layers, 2, piece, 8, channels)
+    hed = jnp.pad(head_weights.astype(low), ((0, 0), (0, 3 * CUT - head_out)))
+    hed = hed.reshape(shard_rows, 3, CUT).transpose(1, 0, 2).reshape(3, piece, 8, CUT)
+    bias = jnp.pad(biases, (0, (2 * layers + 8) * CUT - biases.shape[0])).reshape(-1, CUT)
+    units = 32 * piece
+    block = 4 * piece
+    dma = pltpu.SemaphoreType.DMA
+    vm = pl.BlockSpec(memory_space=pltpu.VMEM)
+    shape = jax.ShapeDtypeStruct
+    logits, deltas, fgrad, tgrad, hgrad, bsum, loss = pl.pallas_call(
+        partial(
+            mega_kernel,
+            rows=rows, cols=cols, layers=layers, cls_out=cls_out, box_out=box_out, anchors=anchors, piece=piece,
+        ),
+        out_shape=(
+            shape((3, px, CUT), low),
+            shape((px, CUT), low),
+            shape((px, CUT), full),
+            shape((layers, 2, piece, 8, CUT), full),
+            shape((3, piece, 8, CUT), full),
+            shape((2, 8, CUT), full),
+            shape((8, LANES), full),
+        ),
+        in_specs=[vm] * 6,
+        out_specs=[vm] * 7,
+        scratch_shapes=[
+            pltpu.VMEM((7, units, 8, CUT), low),
+            pltpu.VMEM((7, units, 8, CUT), low),
+            pltpu.VMEM((7, 4, block, 8, CUT), low),
+            pltpu.VMEM((7, 2, block, 8, CUT), low),
+            pltpu.VMEM((7, 2, 3, piece, 8, CUT), low),
+            pltpu.VMEM((4, block, 8, CUT), low),
+            pltpu.VMEM((7, piece, 8, CUT), full),
+            pltpu.VMEM((layers + 1, 2, px + 2 * cols, 3 * CUT), low),
+            pltpu.VMEM((layers + 1, 2, 2, cols, CUT), low),
+            pltpu.VMEM((7, 2, px + 2 * cols, CUT), low),
+            pltpu.VMEM((layers, 2, px, CUT), full),
+            pltpu.VMEM((3, 2, px, CUT), full),
+            pltpu.VMEM((px, CUT), full),
+            pltpu.VMEM((px, CUT), low),
+            pltpu.VMEM((2, px, LANES), low),
+            pltpu.VMEM((2, px, LANES), full),
+            pltpu.VMEM((3, 2, px, CUT), low),
+            pltpu.VMEM((2, px, CUT), low),
+            pltpu.VMEM((px, CUT), full),
+            pltpu.VMEM((px, CUT), full),
+            pltpu.VMEM((10, 8, LANES), full),
+            pltpu.VMEM((8, CUT), full),
+            pltpu.VMEM((11, 8, CUT), full),
+            dma((6,)), dma((6,)),
+            dma((6, 2, 3)), dma((6, 2, 3)),
+            dma((6, 2)), dma((6, 2)),
+            dma((7, 4)), dma((7, 4)),
+            dma((4,)), dma((4,)),
+            dma((4,)), dma((4,)),
+            dma((layers + 1, 2, 2)), dma((layers + 1, 2, 2)),
+            dma((7, 2, 2)), dma((7, 2, 2)),
+            dma((3,)), dma((3,)),
+            dma((1,)), dma((1,)),
+            dma((7, 4)), dma((7, 4)),
+            dma((7, 2)), dma((7, 2)),
+            dma((7, 2, 3)), dma((7, 2, 3)),
+            dma((4,)), dma((4,)),
+            dma((7,)), dma((7,)),
+            dma((10,)), dma((10,)),
+            dma((6,)), dma((6,)),
+        ],
+        compiler_params=pltpu.CompilerParams(
+            vmem_limit_bytes=60 * 1024 * 1024, collective_id=0, has_side_effects=True
+        ),
+    )(features.reshape(px, channels), code, goals, tow, hed, bias)
+
+    step_float = step_count[0].astype(full)
+    scal = jnp.stack([1.0 - jnp.power(beta_one, step_float), 1.0 - jnp.power(beta_two, step_float)])
+    tgrad = tgrad.reshape(layers, 2, shard_rows, channels)
+    hgrad = hgrad.reshape(3, shard_rows, CUT)
+    tower_shape = tower_weights.shape
+    head_shape = head_weights.shape
+    outs = pl.pallas_call(
+        partial(finish_kernel, layers=layers, cls_out=cls_out, box_out=box_out),
+        out_shape=(
+            shape((px, cls_out), low),
+            shape((px, box_out), low),
+            shape((px, channels), full),
+            shape((layers, shard_rows, channels), full),
+            shape((layers, shard_rows, channels), full),
+            shape(head_shape, full),
+            shape(tower_shape, full),
+            shape(head_shape, full),
+            shape(tower_shape, full),
+            shape(tower_shape, full),
+            shape(head_shape, full),
+            shape(head_shape, full),
+            shape(tower_shape, low),
+            shape(head_shape, low),
+        ),
+        in_specs=[pl.BlockSpec(memory_space=pltpu.SMEM)] + [vm] * 11,
+        out_specs=[vm] * 14,
+        compiler_params=pltpu.CompilerParams(vmem_limit_bytes=40 * 1024 * 1024),
+    )(scal, logits, deltas, fgrad, tgrad, hgrad, tower_weights, head_weights, tower_m, tower_v, head_m, head_v)
+    (
+        o_lg, o_dl, o_fg, o_tg, o_bg, o_hg, o_tn, o_hn, o_tm, o_tv, o_hm, o_hv, o_tc, o_hc,
+    ) = outs
+    tail = cls_out - 2 * CUT
+    bias_grad = jnp.concatenate(
+        [
+            jnp.stack([bsum[0, :layers], bsum[1, :layers]], 1).reshape(-1),
+            bsum[0, 4:7].reshape(-1)[:cls_out],
+            bsum[1, 6, tail : tail + box_out],
+        ]
+    )
+    bias_new, bias_m_new, bias_v_new = adam_update(biases, bias_grad, bias_m, bias_v, step_float, 0.0)
+    split_at = bias_grad.shape[0] - box_out
+    field = (canvases, rows, cols, -1)
+    return (
+        o_lg.reshape(field),
+        o_dl.reshape(field),
+        loss[0, 0],
+        o_fg.reshape(field),
+        o_tg,
+        o_bg,
+        o_hg,
+        bias_grad[:split_at],
+        bias_grad[split_at:],
+        o_tn,
+        o_hn,
+        bias_new,
+        o_tm,
+        o_tv,
+        o_hm,
+        o_hv,
+        bias_m_new,
+        bias_v_new,
+        o_tc,
+        o_hc,
+    )
+
+
 def solution(mesh):
     placed = (
         P("dp", "tower", None, None),
@@ -307,8 +1383,9 @@
         P(),
         P(),
     )
+    fused = mesh.shape["dp"] == 8 and mesh.shape["tower"] == 4
     return jax.shard_map(
-        shards,
+        fused_shards if fused else plain_shards,
         mesh=mesh,
         in_specs=placed,
         out_specs=(

time: 665 us -> 184 us (0.28); the launches traced: 654 us -> 180 us
  waiting for transfers between devices: 278 us -> 0 us
  Pallas kernels: 0 us -> 163 us
  local copies, waits for them, and re-layouts: 102 us -> 13.3 us
  blocking collectives: 83.2 us -> 0 us
  matrix products: 61.8 us -> 0 us
  other arithmetic: 56.3 us -> 3.09 us
  starting transfers between devices: 51 us -> 0 us
  between operations: 22.1 us -> 1.5 us
    reduce_scatter x1 -> x0, waiting for transfers between devices: 211 us -> none  [shards(): lax.psum_scatter(jnp.stack(tower_grads, 0), ('dp', 'tower'), scatter_dime...]
    pallas_call x0 -> x2, Pallas kernels: none -> 163 us  [the longest x1 159 us: fused_shards(): pl.pallas_call(partial(mega_kernel, rows=rows, cols=cols, layers=layers,...]
    psum x2 -> x0, blocking collectives: 83.2 us -> none  [the longest x1 42.3 us: shards(): count_all = lax.psum(jnp.sum(own_chosen), ('dp', 'tower'))]
    dot_general x162 -> x0, matrix products: 61.8 us -> none  [the longest x54 22.4 us: conv_forward(): jnp.einsum('snk,skm->snm', window, weight[:, tap_index * channels:(tap_in...]
    ppermute x20 -> x0, starting transfers between devices: 50.9 us -> none  [the longest x10 37.2 us: with_halo(): before = lax.ppermute(last, axis, up)]
    unnamed x5 -> x0, waiting for transfers between devices: 27 us -> none
    all_gather x2 -> x0, waiting for transfers between devices: 25.6 us -> none  [the longest x1 25.6 us: shards(): lax.all_gather(tower_weights.astype(jnp.bfloat16), ('dp', 'tower'), axis=...]
    broadcast_in_dim x12 -> x0, local copies, waits for them, and re-layouts: 24.9 us -> none  [the longest x1 16.6 us: shards(): head_wgrad[None, None]]
  transfers between devices with their start and end apart: 24 -> 0, of which waited for: 10 -> 0; matrix products, arithmetic and copies ran while one was open for 23% -> 0% of each run, Pallas kernels for 0% -> 0%
where the time goes in v1:
time: 184 us; the launch traced here: 180 us
  Pallas kernels  163 us (89%)
  local copies, waits for them, and re-layouts  13.3 us (7%)
  other arithmetic  3.09 us (2%)
    pallas_call x1, Pallas kernels, fused_shards(): pl.pallas_call(partial(mega_kernel, rows=rows, cols=cols, layers=layers,...  159 us
    unnamed x39, local copies, waits for them, and re-layouts  8.79 us

profile of v1, /device:TPU:0, one launch (start us, length us, event | category | flops | bytes accessed | tf_op | source)
XLA Modules:
  0.0 180.5 jit_solution(8545555782052791350)
XLA Ops:
  0.7 0.0 copy-start.17
  0.7 0.6 copy-done.17
  1.3 0.1 slice_compare_fusion
  1.4 0.1 add_and_fusion
  1.5 0.1 dynamic-slice_bitcast_fusion
  1.6 0.9 select_convert_fusion
  2.4 0.2 copy.39
  2.6 0.0 copy-start.11
  2.6 0.7 pad.16.code
  3.3 0.3 copy-done.11
  3.5 0.1 copy.40
  3.7 0.0 copy-start.1
  3.7 0.8 pad.17.goals
  4.5 0.1 copy-done.1
  4.6 0.0 copy-start
  4.7 0.7 copy.47
  5.4 0.3 copy-done
  5.7 0.0 copy-start.12
  5.7 0.0 copy-start.4
  5.7 0.7 convert_bitcast_fusion.tow
  6.5 0.0 copy-done.12
  6.5 0.0 copy-start.3
  6.5 0.6 reshape.151.bias
  7.1 0.0 copy-start.8
  7.1 0.0 copy-start.9
  7.1 159.3 %shard_map.302 = (bf16[3,512,256]{2,1,0:T(8,128)(2,1)}, bf16[512,256]{1,0:T(8,128)(2,1)}, f32[512,256]{1,0:T(8,128)}, f32[4,2,9,8,256]{4,3,2,1,0:T(8,128)}, f32[...) custom-call(bf16[512,256]{1,0:T(8,128)(2,1)} %bitcast.37, bf16[512,128]{1,0:T(8,128)(2,1)} %pad.16.code, ...), custom_call_target="tpu_custom_call" | custom-call | tf_op jit(solution)/shard_map/pallas_call | solution.py:1239
  167.2 0.1 pad_maximum_fusion.2.scal
  167.3 0.0 copy-done.4
  167.3 0.0 copy-done.3
  167.3 0.0 copy-done.8
  167.3 0.0 copy-done.9
  167.3 0.0 copy-start.2
  167.3 1.1 copy-done.2
  168.4 0.0 copy-start.5
  168.4 1.1 copy-done.5
  169.5 0.0 copy-start.6
  169.5 1.0 copy-done.6
  170.5 0.0 copy-start.7
  170.5 0.9 copy-done.7
  171.5 0.0 copy-start.10
  171.5 0.9 copy-done.10
  172.4 3.3 %shard_map.303 = (bf16[512,720]{1,0:T(8,128)(2,1)}, bf16[512,36]{1,0:T(8,128)(2,1)S(1)}, f32[512,256]{1,0:T(8,128)}, f32[4,72,256]{2,1,0:T(8,128)}, f32[4,72,256...) custom-call(f32[2]{0:T(128)S(1)} %pad_maximum_fusion.2.scal, ...), custom_call_target="tpu_custom_call" | custom-call | tf_op jit(solution)/shard_map/pallas_call | solution.py:1308
  175.7 0.8 copy.43
  176.5 0.0 copy-start.15
  176.5 0.7 copy-done.15
  177.3 0.1 slice_bitcast_fusion.2
  177.3 0.0 copy-start.16
  177.3 0.0 copy-start.13
  177.3 0.0 copy-start.14
  177.3 0.1 concatenate.31
  177.4 0.4 copy-done.16
  177.8 0.2 copy-done.13
  178.1 0.0 copy-done.14
  178.1 0.6 multiply_subtract_fusion
  178.7 0.6 pad_maximum_fusion
  179.3 1.2 slice.28
  (10 shorter events, 0.1 us)
Async XLA Ops:
  0.7 0.7 copy-start.17
  2.6 1.0 copy-start.11
  3.7 0.9 copy-start.1
  4.6 1.1 copy-start
  5.7 0.8 copy-start.12
  5.7 161.5 %copy-start.4 = (f32[4,2,72,256]{3,2,1,0:T(8,128)S(1)}, f32[4,2,72,256]{3,2,1,0:T(8,128)}, u32[]{:S(2)}) copy-start(f32[4,2,72,256]{3,2,1,0:T(8,128)} %tv.1) | copy-start | bytes 1769476
  6.5 160.8 %copy-start.3 = (f32[4,2,72,256]{3,2,1,0:T(8,128)S(1)}, f32[4,2,72,256]{3,2,1,0:T(8,128)}, u32[]{:S(2)}) copy-start(f32[4,2,72,256]{3,2,1,0:T(8,128)} %tm.1) | copy-start | bytes 1769476
  7.1 160.2 %copy-start.8 = (f32[72,756]{1,0:T(8,128)S(1)}, f32[72,756]{1,0:T(8,128)}, u32[]{:S(2)}) copy-start(f32[72,756]{1,0:T(8,128)} %hm.1) | copy-start | bytes 653188
  7.1 160.2 %copy-start.9 = (f32[72,756]{1,0:T(8,128)S(1)}, f32[72,756]{1,0:T(8,128)}, u32[]{:S(2)}) copy-start(f32[72,756]{1,0:T(8,128)} %hv.1) | copy-start | bytes 653188
  167.3 1.1 copy-start.2
  168.4 1.1 copy-start.5
  169.5 1.0 copy-start.6
  170.5 0.9 copy-start.7
  171.5 0.9 copy-start.10
  176.5 0.7 copy-start.15
  177.3 0.5 copy-start.16
  177.3 0.7 copy-start.13
  177.3 0.7 copy-start.14

commit v2 on v1

--- a/solution.py
+++ b/solution.py
@@ -1,3 +1,4 @@
+import math
 from functools import partial
 
 import jax
@@ -299,9 +300,9 @@
 
 
 def mega_kernel(
-    feat, code, goals, tow, hed, bias,
+    feat, crops, marked, lit, goals, tow, hed, bias_all,
     logits, deltas, fgrad, tgrad, hgrad, bsum, loss_out,
-    W, D, RD, RY, RZ, RX, RP, A3, HA, G, Z, U, ACC, FP, CP, GP, LS, ES, FS, FR, CNT, BG, BR,
+    W, D, RD, RY, RZ, RX, RP, A3, HA, G, Z, U, ACC, FP, CP, GP, LS, ES, FS, FR, CNT, BG, BR, TB, HB, bias,
     ps, pr, zs, zr, ys, yr, ds, dr, xs, xr, fs, fr, hs, hr, gs, gr, ls, lr, es, er,
     rds, rdr, rys, ryr, rzs, rzr, rxs, rxr, rps, rpr, ns, nr, bs, br,
     *, rows, cols, layers, cls_out, box_out, anchors, piece,
@@ -347,12 +348,12 @@
 
     def p_send(step):
         return remote(
-            tow.at[step, 1 - x], W.at[step, pcs(y, x, k, z)], ps.at[step], pr.at[step], (par, z)
+            TB.at[step], W.at[step, pcs(y, x, k, z)], ps.at[step], pr.at[step], (par, z)
         )
 
     def p_head(cut, index):
         return remote(
-            hed.at[cut], W.at[4 + cut, pcs(y, x, k, z)], ps.at[index], pr.at[index], (par, z)
+            HB.at[cut], W.at[4 + cut, pcs(y, x, k, z)], ps.at[index], pr.at[index], (par, z)
         )
 
     def p_recv(step):
@@ -387,19 +388,16 @@
         @pl.when(has(step))
         def _():
             p_recv(step).wait_recv()
-            for o in (1, 3, 2):
-                for xx in range(2):
+            for xx in range(2):
+                for o in (2, 1, 3):
                     z_send(step, xx, o).start()
 
-    def spread(step, yy):
-        slot = slot_of(step)
-        for xx in range(2):
-            d_copy(slot, yy, xx, k).start()
+    def spread(step, yy, xx):
+        d_copy(slot_of(step), yy, xx, k).start()
 
         @pl.when(is_box & (step == 4))
         def _():
-            for xx in range(2):
-                x_copy(yy, xx).start()
+            x_copy(yy, xx).start()
 
     def do_y(step):
         @pl.when(has(step))
@@ -407,58 +405,72 @@
             for xx in range(2):
                 for o in (1, 2, 3):
                     z_recv(step, xx, o).wait_recv()
-            for xx in range(2):
                 y_copy(step, xx, y).start()
-            spread(step, y)
+                spread(step, y, xx)
 
     def do_d(step):
         @pl.when(has(step))
         def _():
             for xx in range(2):
                 y_copy(step, xx, 1 - y).wait_recv()
-            spread(step, 1 - y)
+                spread(step, 1 - y, xx)
 
     def gathered(slot):
         for b in range(4):
             d_copy(slot, b // 2, b % 2, 1 - k).wait_recv()
 
-    for step in range(4):
+    for step in range(layers):
+        TB[step] = tow[step, 1 - x].astype(low)
         p_send(step).start()
-        if step == 0:
-            pltpu_feature = remote(feat, FP, fs.at[0], fr.at[0], (par, z))
-        W[step, pcs(y, x, k, z)] = tow[step, x]
+        W[step, pcs(y, x, k, z)] = tow[step, x].astype(low)
+    pltpu_feature = remote(feat, FP, fs.at[0], fr.at[0], (par, z))
     pltpu_feature.start()
+    tail = cls_out + box_out - 2 * CUT
+    HB[2] = jnp.zeros((piece, 8, CUT), low)
+    for cut, width in ((2, tail), (0, CUT), (1, CUT)):
+        part = hed[:, cut * CUT : cut * CUT + width].astype(low)
+        HB[cut, :, :, 0:width] = part.reshape(piece, 8, width)
 
     @pl.when(is_cls)
     def _():
         p_head(2, 4).start()
-        W[4, pcs(y, x, k, z)] = hed[0]
-        W[5, pcs(y, x, k, z)] = hed[1]
+        W[4, pcs(y, x, k, z)] = HB[0]
+        W[5, pcs(y, x, k, z)] = HB[1]
 
     @pl.when(is_box)
     def _():
         p_head(0, 4).start()
         p_head(1, 5).start()
-        W[6, pcs(y, x, k, z)] = hed[2]
-
-    code_copy = remote(code, CP.at[x], fs.at[1], fr.at[1], (par, z))
-    code_copy.start()
-    goal_copy = remote(goals, GP.at[x], fs.at[2], fr.at[2], (par, z))
-    CP[x] = code[...]
-    GP[x] = goals[...]
-
-    @pl.when(is_cls)
-    def _():
-        goal_copy.start()
-
+        W[6, pcs(y, x, k, z)] = HB[2]
+
+    code_copy = remote(CP.at[x], CP.at[x], fs.at[1], fr.at[1], (par, z))
+    goal_copy = remote(GP.at[x], GP.at[x], fs.at[2], fr.at[2], (par, z))
     do_z(0)
     do_z(1)
 
     def n_copy(index, dst, dev):
         return remote(CNT.at[index], CNT.at[dst], ns.at[dst], nr.at[dst], dev)
 
-    picked = (code[...].astype(full) < -110.0).astype(full)
-    CNT[0] = jnp.broadcast_to(jnp.sum(picked.reshape(px // 8, 8, LANES), axis=0).sum(), (8, LANES))
+    r_at = lax.broadcasted_iota(jnp.int32, (rows, cols), 0)
+    inside = jnp.zeros((rows, cols), jnp.int32)
+    for r in range(rows):
+        row = z * rows + r
+        here = crops[0, row]
+        above = crops[0, jnp.maximum(row - 1, 0)]
+        below = crops[0, jnp.minimum(row + 1, 4 * rows - 1)]
+        ok = jnp.where((here == above) & (here == below), 1, 0)
+        inside = jnp.where(r_at == r, ok, inside)
+    CP[x] = jnp.zeros((rows, 16, cols), full)
+    picked = jnp.zeros((rows, cols), full)
+    for a in range(anchors):
+        label = marked[a]
+        valid = (label >= 0) & (inside > 0)
+        chosen = valid & (lit[a] > 0)
+        mark = jnp.where(chosen, label - 200, jnp.where(valid, -100, 0)).astype(full)
+        picked = picked + jnp.where(chosen, 1.0, 0.0)
+        for r in range(rows):
+            CP[x, r, a : a + 1, :] = mark[r : r + 1, :]
+    CNT[0] = jnp.broadcast_to(jnp.sum(picked), (8, LANES))
     n_copy(0, 4, (sib, z)).start()
 
     col = lax.broadcasted_iota(jnp.int32, (cols, CUT), 0)
@@ -489,29 +501,30 @@
         dev = (d, lax.rem(z + 1, 4)) if side == 0 else (d, lax.rem(z + 3, 4))
         return remote(src, HA.at[layer, side, cv], hs.at[layer, side, cv], hr.at[layer, side, cv], dev)
 
-    def send_edges(layer, cvs):
+    def send_edges(layer, cv):
         @pl.when(down_ok())
         def _():
-            for cv in cvs:
-                a_edge(layer, 0, cv).start()
+            a_edge(layer, 0, cv).start()
 
         @pl.when(up_ok())
         def _():
-            for cv in cvs:
-                a_edge(layer, 1, cv).start()
-
-    def take_edges(layer):
+            a_edge(layer, 1, cv).start()
+
+    def take_edges(layer, cv):
         @pl.when(up_ok())
         def _():
-            for cv in range(2):
-                a_edge(layer, 0, cv).wait_recv()
-                put_row(layer, cv, 0, HA[layer, 0, cv].astype(full))
+            a_edge(layer, 0, cv).wait_recv()
+            put_row(layer, cv, 0, HA[layer, 0, cv].astype(full))
 
         @pl.when(down_ok())
         def _():
-            for cv in range(2):
-                a_edge(layer, 1, cv).wait_recv()
-                put_row(layer, cv, rows + 1, HA[layer, 1, cv].astype(full))
+            a_edge(layer, 1, cv).wait_recv()
+            put_row(layer, cv, rows + 1, HA[layer, 1, cv].astype(full))
+
+    def rim_first(body, carry, send):
+        carry = lax.fori_loop(0, 2, lambda i, c: body(i * (rows - 1), c), carry)
+        send()
+        return lax.fori_loop(1, rows - 1, body, carry)
 
     def g_edge(slot, side, cv):
         src = G.at[slot, cv, pl.ds((rows if side == 0 else 1) * cols, cols)]
@@ -523,27 +536,23 @@
         dst = G.at[slot, cv, pl.ds(0 if side == 0 else (rows + 1) * cols, cols)]
         return remote(dst, dst, gs.at[slot, side, cv], gr.at[slot, side, cv], (d, lax.rem(z + 1, 4)))
 
-    def send_g(slot):
+    def send_g(slot, cv):
         @pl.when(down_ok())
         def _():
-            for cv in range(2):
-                g_edge(slot, 0, cv).start()
+            g_edge(slot, 0, cv).start()
 
         @pl.when(up_ok())
         def _():
-            for cv in range(2):
-                g_edge(slot, 1, cv).start()
-
-    def take_g(slot):
+            g_edge(slot, 1, cv).start()
+
+    def take_g(slot, cv):
         @pl.when(up_ok())
         def _():
-            for cv in range(2):
-                g_recv(slot, 0, cv).wait_recv()
+            g_recv(slot, 0, cv).wait_recv()
 
         @pl.when(down_ok())
         def _():
-            for cv in range(2):
-                g_recv(slot, 1, cv).wait_recv()
+            g_recv(slot, 1, cv).wait_recv()
 
     def fill(layer_src, cv):
         def body(r, carry):
@@ -553,7 +562,7 @@
         lax.fori_loop(0, rows, body, 0)
 
     fill(feat, x)
-    send_edges(0, [x])
+    send_edges(0, x)
 
     def clear(at, layer_count, slot_count):
         def a_body(layer, carry):
@@ -578,6 +587,19 @@
         clear(pl.ds((rows + 1) * cols, cols), layers + 1, layers + 3)
 
     BG[...] = jnp.zeros((8, CUT), full)
+    GP[x] = jnp.zeros((rows, 40, cols), full)
+
+    def goal_rows(q, carry):
+        for r in range(rows):
+            GP[x, r, pl.ds(q, 1), :] = goals[q, r : r + 1, :]
+        return carry
+
+    lax.fori_loop(0, box_out, goal_rows, 0)
+    for q in range(2 * layers + 2):
+        bias[q : q + 1, :] = bias_all[q * CUT : (q + 1) * CUT].reshape(1, CUT)
+    q = 2 * layers + 2
+    bias[q : q + 1, :] = jnp.zeros((1, CUT), full)
+    bias[q : q + 1, 0:tail] = bias_all[q * CUT : q * CUT + tail].reshape(1, tail)
 
     n_copy(0, 4, (sib, z)).wait_recv()
     CNT[1] = CNT[0] + CNT[4]
@@ -589,7 +611,7 @@
     n_copy(2, 6, (par, z)).start()
     pltpu_feature.wait_recv()
     fill(FP, 1 - x)
-    send_edges(0, [1 - x])
+    send_edges(0, 1 - x)
     n_copy(2, 6, (par, z)).wait_recv()
     CNT[3] = CNT[2] + CNT[6]
     for o in (1, 2, 3):
@@ -597,6 +619,11 @@
     do_y(1)
     do_d(0)
     do_z(3)
+    code_copy.start()
+
+    @pl.when(is_cls)
+    def _():
+        goal_copy.start()
 
     def conv(layer, slot, cv):
         total = None
@@ -611,10 +638,10 @@
 
     def forward(layer, carry):
         gathered(layer)
-        take_edges(layer)
         shift = bias[pl.ds(2 * layer + x, 1), :]
 
         def canvas(cv, carry):
+            take_edges(layer, cv)
             Z[layer, cv] = conv(layer, layer, cv)
 
             def row(r, carry):
@@ -624,11 +651,10 @@
                 put_row(layer + 1, cv, r + 1, silu_value(value))
                 return carry
 
-            lax.fori_loop(0, rows, row, 0)
+            rim_first(row, 0, lambda: send_edges(layer + 1, cv))
             return carry
 
         lax.fori_loop(0, 2, canvas, 0)
-        send_edges(layer + 1, range(2))
         do_y_when = layer + 2
         do_y(do_y_when)
         do_d(layer + 1)
@@ -645,7 +671,8 @@
         n_copy(3, 6 + o, (d, zpeer(o))).wait_recv()
     count = CNT[3] + CNT[7] + CNT[8] + CNT[9]
     grad_scale = (1.0 / jnp.maximum(count, 1.0))[0:1, 0:1]
-    take_edges(layers)
+    for cv in range(2):
+        take_edges(layers, cv)
 
     def rd_send(slot, b):
         src = D.at[slot, blk(b // 2, b % 2, 1 - k)]
@@ -696,6 +723,14 @@
                 terms.append(RX.at[b])
             add_into(slot, start_of(1 - y, xx, k), terms)
             ry_send(slot, xx).start()
+
+    def do_rx():
+        for b in range(4):
+            rd_send(6, b).wait_recv()
+            add_into(6, start_of(b // 2, b % 2, k), [RD.at[6, b]])
+            rx_send(b).start()
+
+    def do_rz(slot, relay=False):
         for xx in range(2):
             b = y * 2 + xx
             rd_send(slot, b).wait_recv()
@@ -703,18 +738,9 @@
             if relay:
                 rx_send(b).wait_recv()
                 terms.append(RX.at[b])
+            ry_send(slot, xx).wait_recv()
+            terms.append(RY.at[slot, xx])
             add_into(slot, start_of(y, xx, k), terms)
-
-    def do_rx():
-        for b in range(4):
-            rd_send(6, b).wait_recv()
-            add_into(6, start_of(b // 2, b % 2, k), [RD.at[6, b]])
-            rx_send(b).start()
-
-    def do_rz(slot):
-        for xx in range(2):
-            ry_send(slot, xx).wait_recv()
-            add_into(slot, start_of(y, xx, k), [RY.at[slot, xx]])
             for o in (2, 1, 3):
                 rz_send(slot, xx, o).start()
 
@@ -754,6 +780,7 @@
 
     def input_grad(slot, add):
         def canvas(cv, carry):
+            take_g(slot, cv)
             for dx in range(3):
                 total = None
                 for dy in range(3):
@@ -780,8 +807,14 @@
         return jnp.sum(value.reshape(cols // 8, 8, CUT), axis=0)
 
     lane = lax.broadcasted_iota(jnp.int32, (1, CUT), 1)
-    lane_tab = lax.broadcasted_iota(jnp.int32, (LANES, CUT), 1)
-    anchor_tab = lax.broadcasted_iota(jnp.int32, (LANES, CUT), 0)
+    lane_tab = lax.broadcasted_iota(jnp.int32, (16, CUT), 1)
+    anchor_tab = lax.broadcasted_iota(jnp.int32, (16, CUT), 0)
+
+    def spread_marks(cv, r, table):
+        return lax.dot_general(
+            CP[cv, r].astype(low), table, (((0,), (0,)), ((), ())), preferred_element_type=full
+        )
+
     box_from = cls_out - 2 * CUT
 
     def cls_rows(cut, cv, shift):
@@ -800,7 +833,7 @@
             at = pl.ds(pl.multiple_of(r * cols, cols), cols)
             raw = ACC[at, :] + shift
             LS[cut, cv, at, :] = raw.astype(low)
-            marks = jnp.dot(CP[cv, at, :], spread_tab, preferred_element_type=full)
+            marks = spread_marks(cv, r, spread_tab)
             hit = marks == number
             seen = marks < -50.0
             s = jnp.where(hit, -raw, raw)
@@ -823,15 +856,20 @@
         spread_tab = (
             (spot >= anchor_tab * 4) & (spot < (anchor_tab + 1) * 4) & (anchor_tab < anchors)
         ).astype(full).astype(low)
+        goal_lane = lax.broadcasted_iota(jnp.int32, (40, LANES), 1) - (box_from - LANES)
+        goal_tab = (goal_lane == lax.broadcasted_iota(jnp.int32, (40, LANES), 0)).astype(full)
 
         def row(r, carry):
             b_sum, l_sum = carry
             at = pl.ds(pl.multiple_of(r * cols, cols), cols)
             raw = ACC[at, :] + shift
             ES[cv, at, :] = raw.astype(low)
-            marks = jnp.dot(CP[cv, at, :], spread_tab, preferred_element_type=full)
+            marks = spread_marks(cv, r, spread_tab)
             chosen = marks < -110.0
-            want = GP[cv, at, :]
+            want = lax.dot_general(
+                GP[cv, r], goal_tab, (((0,), (0,)), ((), ())),
+                precision=lax.Precision.HIGHEST, preferred_element_type=full,
+            )
             want = jnp.concatenate([jnp.zeros((cols, LANES), full), want], axis=1)
             diff = raw - want
             size = jnp.abs(diff)
@@ -856,11 +894,11 @@
         return remote(ES.at[1 - x], deltas, es.at[0], er.at[0], (par, z))
 
     U[...] = jnp.zeros(U.shape, full)
-    remote(code, CP.at[1 - x], fs.at[1], fr.at[1], (par, z)).wait_recv()
+    remote(CP.at[1 - x], CP.at[1 - x], fs.at[1], fr.at[1], (par, z)).wait_recv()
 
     @pl.when(is_box)
     def _():
-        remote(goals, GP.at[1 - x], fs.at[2], fr.at[2], (par, z)).wait_recv()
+        remote(GP.at[1 - x], GP.at[1 - x], fs.at[2], fr.at[2], (par, z)).wait_recv()
 
     def head(cut, carry):
         slot = 4 + cut
@@ -879,12 +917,11 @@
             ACC[...] = conv(layers, slot, cv)
             return lax.cond(
                 is_cls,
-                lambda: lax.fori_loop(0, rows, cls_rows(cut, cv, shift), (b_sum, l_sum)),
-                lambda: lax.fori_loop(0, rows, box_rows(cut, cv, shift), (b_sum, l_sum)),
+                lambda: rim_first(cls_rows(cut, cv, shift), (b_sum, l_sum), lambda: send_g(slot, cv)),
+                lambda: rim_first(box_rows(cut, cv, shift), (b_sum, l_sum), lambda: send_g(slot, cv)),
             )
 
         b_sum, l_sum = lax.fori_loop(0, 2, canvas, (nothing, nothing))
-        send_g(slot)
 
         @pl.when(is_cls)
         def _():
@@ -899,24 +936,28 @@
         weight_grad(layers, slot)
         do_rd(slot)
 
-        @pl.when(is_cls & (cut == 1))
-        def _():
-            do_ry(4)
+        input_grad(slot, True)
+
+        @pl.when(cut < 2)
+        def _():
+            do_ry(slot)
+
+        @pl.when(cut == 1)
+        def _():
+            do_rz(4)
 
         @pl.when(is_cls & (cut == 2))
         def _():
-            do_ry(5)
-            do_rz(4)
-
-        take_g(slot)
-        input_grad(slot, True)
+            do_rx()
+            do_rz(5)
+            do_rp_head(4)
+
         return carry
 
     lax.fori_loop(2 * x, 3, head, 0)
 
     @pl.when(is_cls)
     def _():
-        do_rx()
         for cut in range(3):
             logits[cut] = LS[cut, 0]
 
@@ -924,6 +965,14 @@
     def _():
         deltas[...] = ES[1]
 
+    def feature_rows(cv, dst):
+        def row(r, carry):
+            dst[pl.ds(pl.multiple_of(r * cols, cols), cols), :] = upstream_row(cv, r).astype(dst.dtype)
+            return carry
+
+        lax.fori_loop(0, rows, row, 0)
+
+    f_copy = remote(FS, FR, fs.at[3], fr.at[3], (par, z))
     def b_copy(src, dst, dev):
         return remote(src, BR.at[dst], bs.at[dst], br.at[dst], dev)
 
@@ -937,10 +986,9 @@
                 G[layer, cv, pl.ds(pl.multiple_of((r + 1) * cols, cols), cols), :] = g
                 return b_sum + fold(g.astype(full))
 
-            return lax.fori_loop(0, rows, row, b_sum)
+            return rim_first(row, b_sum, lambda: send_g(layer, cv))
 
         b_sum = lax.fori_loop(0, 2, canvas, nothing)
-        send_g(layer)
         BG[pl.ds(layer, 1), :] = jnp.sum(b_sum, axis=0, keepdims=True)
         weight_grad(layer, layer)
         do_rd(layer)
@@ -949,58 +997,41 @@
         def _():
             b_copy(BG, 0, (sib, z)).start()
 
+        @pl.when(j == layers - 1)
+        def _():
+            do_ry(0)
+
+        input_grad(layer, False)
+
+        @pl.when(j == layers - 1)
+        def _():
+            feature_rows(1 - x, FS)
+            f_copy.start()
+
+        @pl.when(j < layers - 1)
+        def _():
+            do_ry(layer)
+
+        @pl.when(is_cls & (j == 0))
+        def _():
+            do_rp_head(5)
+
         @pl.when(j > 0)
         def _():
-            do_ry(layer + 1)
+            do_rz(layer + 1)
 
         @pl.when(j > 1)
         def _():
-            do_rz(layer + 2)
-
-        @pl.when(j > 2)
-        def _():
-            do_rp_layer(3)
-
-        @pl.when(is_cls & (j == 0))
-        def _():
-            do_rz(5)
-            do_rp_head(4)
-
-        @pl.when(is_cls & (j == 1))
-        def _():
-            do_rp_head(5)
-
-        @pl.when(is_box & (j == 1))
-        def _():
-            do_ry(6, relay=True)
-
-        @pl.when(is_box & (j == 2))
-        def _():
-            do_rz(6)
-
-        @pl.when(is_box & (j == 3))
-        def _():
-            do_rp_head(6)
-
-        take_g(layer)
-        input_grad(layer, False)
+            do_rp_layer(layer + 2)
+
         return carry
 
     lax.fori_loop(0, layers, backward, 0)
 
-    def feature_rows(cv, dst):
-        def row(r, carry):
-            dst[pl.ds(pl.multiple_of(r * cols, cols), cols), :] = upstream_row(cv, r)
-            return carry
-
-        lax.fori_loop(0, rows, row, 0)
-
-    f_copy = remote(FS, FR, fs.at[3], fr.at[3], (par, z))
-    feature_rows(1 - x, FS)
-    f_copy.start()
-    do_ry(0)
-    do_rz(1)
-    do_rp_layer(2)
+    @pl.when(is_box)
+    def _():
+        do_ry(6, relay=True)
+
     b_copy(BG, 0, (sib, z)).wait_recv()
     BR[6] = BG[...] + BR[0]
     b_copy(BR.at[6], 1, (yn, z)).start()
@@ -1017,6 +1048,11 @@
                 ).start()
     do_rz(0)
     do_rp_layer(1)
+
+    @pl.when(is_box)
+    def _():
+        do_rz(6, relay=True)
+
     for o in (1, 2, 3):
         for zz in range(4):
             @pl.when(zfrom(o) == zz)
@@ -1030,8 +1066,13 @@
     last.start()
     bsum[x] = total
     f_copy.wait_recv()
-    fgrad[...] = fgrad[...] + FR[...]
+    fgrad[...] = fgrad[...] + FR[...].astype(full)
     do_rp_layer(0)
+
+    @pl.when(is_box)
+    def _():
+        do_rp_head(6)
+
     remote(BR.at[5], bsum.at[1 - x], bs.at[5], br.at[5], (par, z)).wait_recv()
     loss = jnp.sum(bsum[0, 7:8, :] + bsum[1, 7:8, :], axis=1, keepdims=True)
     loss_out[...] = jnp.broadcast_to(loss, (8, LANES)) / jnp.maximum(count, 1.0)
@@ -1144,49 +1185,144 @@
 
 
 def finish_kernel(
-    scal, lg, dl, fg, tg, hg, tw, hw, tm, tv, hm, hv,
+    step, lg, dl, fg, tg, hg, bsum, loss_in, tw, hw, tm, tv, hm, hv, bw, bm, bv,
     o_lg, o_dl, o_fg, o_tg, o_bg, o_hg, o_tn, o_hn, o_tm, o_tv, o_hm, o_hv, o_tc, o_hc,
-    *, layers, cls_out, box_out,
+    o_loss, o_gb, o_gx, o_wb, o_mb, o_vb,
+    TG, TW, TM, TV, TC, HG, HGO, HW, HM, HV, HC, LG, LO, DT, DS, FG,
+    t_in, t_out, h_in, h_out, m_sem,
+    *, layers, rows, cols, cls_out, box_out,
 ):
     tail = cls_out - 2 * CUT
-
-    def adam(weight, grad, first, second):
+    last = tail + box_out
+
+    def t_loads(layer):
+        pairs = ((tg, TG), (tw, TW), (tm, TM), (tv, TV))
+        return [
+            pltpu.make_async_copy(a.at[layer], b.at[layer], t_in.at[layer, i])
+            for i, (a, b) in enumerate(pairs)
+        ]
+
+    def t_stores(layer):
+        pairs = (
+            (TG.at[layer, 0], o_tg.at[layer]),
+            (TG.at[layer, 1], o_bg.at[layer]),
+            (TW.at[layer], o_tn.at[layer]),
+            (TM.at[layer], o_tm.at[layer]),
+            (TV.at[layer], o_tv.at[layer]),
+            (TC.at[layer], o_tc.at[layer]),
+        )
+        return [pltpu.make_async_copy(a, b, t_out.at[layer, i]) for i, (a, b) in enumerate(pairs)]
+
+    h_loads = [
+        pltpu.make_async_copy(a, b, h_in.at[i])
+        for i, (a, b) in enumerate(((hg, HG), (hw, HW), (hm, HM), (hv, HV)))
+    ]
+    h_stores = [
+        pltpu.make_async_copy(a, b, h_out.at[i])
+        for i, (a, b) in enumerate(((HGO, o_hg), (HW, o_hn), (HM, o_hm), (HV, o_hv), (HC, o_hc)))
+    ]
+    lg_load = pltpu.make_async_copy(lg, LG, m_sem.at[0])
+    lg_store = pltpu.make_async_copy(LO, o_lg, m_sem.at[1])
+    fg_load = pltpu.make_async_copy(fg, FG, m_sem.at[2])
+    fg_store = pltpu.make_async_copy(FG, o_fg, m_sem.at[3])
+    for layer in range(layers):
+        for copy in t_loads(layer):
+            copy.start()
+    for copy in h_loads:
+        copy.start()
+    fg_load.start()
+    lg_load.start()
+
+    steps = jnp.broadcast_to(step[0].astype(full), (8, CUT))
+    keep_one = (1.0 - jnp.exp(steps * math.log(beta_one)))[0:1, :]
+    keep_two = (1.0 - jnp.exp(steps * math.log(beta_two)))[0:1, :]
+
+    def adam(weight, grad, first, second, decay):
+        one, two = keep_one[:, : grad.shape[1]], keep_two[:, : grad.shape[1]]
         first_new = beta_one * first + (1.0 - beta_one) * grad
         second_new = beta_two * second + (1.0 - beta_two) * grad * grad
-        first_hat = first_new / scal[0]
-        second_hat = second_new / scal[1]
+        first_hat = first_new / one
+        second_hat = second_new / two
         weight_new = weight - learn_rate * (
-            first_hat / (jnp.sqrt(second_hat) + adam_eps) + decay_rate * weight
+            first_hat / (jnp.sqrt(second_hat) + adam_eps) + decay * weight
         )
         return weight_new, first_new, second_new
 
-    def layer_body(layer, carry):
+    fg_load.wait()
+    fg_store.start()
+
+    o_loss[0] = loss_in[0, 0]
+    for q in range(2 * layers + 3):
+        if q < 2 * layers:
+            grad, width = bsum[q % 2, q // 2 : q // 2 + 1, :], CUT
+        elif q < 2 * layers + 2:
+            grad, width = bsum[0, q - layers : q - layers + 1, :], CUT
+        else:
+            lane = lax.broadcasted_iota(jnp.int32, (1, CUT), 1)
+            boxes = bsum[1, 6:7, :]
+            grad, width = jnp.where(lane < tail, bsum[0, 6:7, :], boxes)[:, :last], last
+            o_gx[...] = pltpu.roll(boxes, CUT - tail, 1)[:, :box_out].reshape(box_out)
+        at = pl.ds(q * CUT, width)
+        w_new, m_new, v_new = adam(
+            bw[at].reshape(1, width), grad, bm[at].reshape(1, width), bv[at].reshape(1, width), 0.0
+        )
+        o_wb[at] = w_new.reshape(width)
+        o_mb[at] = m_new.reshape(width)
+        o_vb[at] = v_new.reshape(width)
+        most = min(width, cls_out + 2 * layers * CUT - q * CUT)
+        o_gb[pl.ds(q * CUT, most)] = grad[:, :most].reshape(most)
+    pick_lane = lax.broadcasted_iota(jnp.int32, (40, LANES), 1) - (tail - LANES)
+    pick = (pick_lane == lax.broadcasted_iota(jnp.int32, (40, LANES), 0)).astype(full).astype(low)
+    for r in range(rows):
+        DT[r] = lax.dot_general(
+            pick, dl[r * cols : (r + 1) * cols, LANES:], (((1,), (1,)), ((), ())), preferred_element_type=full
+        )
+
+    def turn(q, carry):
+        for r in range(rows):
+            DS[q, r : r + 1, :] = DT[r, pl.ds(q, 1), :]
+        return carry
+
+    lax.fori_loop(0, box_out, turn, 0)
+    o_dl[...] = DS[...].astype(low)
+
+    for layer in range(layers):
+        for copy in t_loads(layer):
+            copy.wait()
         for t in range(2):
-            grad = tg[layer, t]
-            (o_tg if t == 0 else o_bg)[layer] = grad
-            w_new, m_new, v_new = adam(tw[layer, t], grad, tm[layer, t], tv[layer, t])
-            o_tn[layer, t] = w_new
-            o_tm[layer, t] = m_new
-            o_tv[layer, t] = v_new
-            o_tc[layer, t] = w_new.astype(low)
-        return carry
-
-    lax.fori_loop(0, layers, layer_body, 0)
-    for cut, width in ((0, CUT), (1, CUT), (2, tail + box_out)):
+            w_new, m_new, v_new = adam(
+                TW[layer, t], TG[layer, t], TM[layer, t], TV[layer, t], decay_rate
+            )
+            TW[layer, t] = w_new
+            TM[layer, t] = m_new
+            TV[layer, t] = v_new
+            TC[layer, t] = w_new.astype(low)
+        for copy in t_stores(layer):
+            copy.start()
+    lg_load.wait()
+    for cut, width in ((0, CUT), (1, CUT), (2, tail)):
+        LO[:, cut * CUT : cut * CUT + width] = LG[cut][:, :width]
+    lg_store.start()
+    for copy in h_loads:
+        copy.wait()
+    for cut, width in ((0, CUT), (1, CUT), (2, last)):
         at = slice(cut * CUT, cut * CUT + width)
-        grad = hg[cut][:, :width]
-        o_hg[:, at] = grad
-        w_new, m_new, v_new = adam(hw[:, at], grad, hm[:, at], hv[:, at])
-        o_hn[:, at] = w_new
-        o_hm[:, at] = m_new
-        o_hv[:, at] = v_new
-        o_hc[:, at] = w_new.astype(low)
-        if cut < 2:
-            o_lg[:, at] = lg[cut]
-        else:
-            o_lg[:, cut * CUT : cls_out] = lg[cut][:, :tail]
-    o_dl[...] = dl[:, tail : tail + box_out]
-    o_fg[...] = fg[...]
+        grad = HG[cut][:, :width]
+        HGO[:, at] = grad
+        w_new, m_new, v_new = adam(HW[:, at], grad, HM[:, at], HV[:, at], decay_rate)
+        HW[:, at] = w_new
+        HM[:, at] = m_new
+        HV[:, at] = v_new
+        HC[:, at] = w_new.astype(low)
+    for copy in h_stores:
+        copy.start()
+    for layer in range(layers):
+        for copy in t_stores(layer):
+            copy.wait()
+    for copy in h_stores:
+        copy.wait()
+    lg_store.wait()
+    fg_store.wait()
 
 
 def fused_shards(
@@ -1215,22 +1351,11 @@
     cls_out = head_out - box_out
     px = rows * cols
     piece = shard_rows // 8
-    box_from = cls_out - 2 * CUT - LANES
-    shard = lax.axis_index("tower")
-    same_rows = crop_ids[:, 1:] == crop_ids[:, :-1]
-    edge_true = jnp.ones((crop_ids.shape[0], 1), dtype=jnp.bool_)
-    row_ok = jnp.concatenate([edge_true, same_rows], 1) & jnp.concatenate([same_rows, edge_true], 1)
-    own_ok = lax.dynamic_slice_in_dim(row_ok, shard * rows, rows, 1)
-    valid = (labels >= 0) & own_ok[:, :, None, None]
-    code = jnp.where(valid, jnp.where(positive > 0, labels - 200, -100), 0).astype(low)
-    code = jnp.pad(code.reshape(px, anchors), ((0, 0), (0, LANES - anchors)))
-    goals = jnp.pad(
-        box_targets.reshape(px, box_out), ((0, 0), (box_from, LANES - box_from - box_out))
-    )
-    tow = tower_weights.astype(low).reshape(layers, 2, piece, 8, channels)
-    hed = jnp.pad(head_weights.astype(low), ((0, 0), (0, 3 * CUT - head_out)))
-    hed = hed.reshape(shard_rows, 3, CUT).transpose(1, 0, 2).reshape(3, piece, 8, CUT)
-    bias = jnp.pad(biases, (0, (2 * layers + 8) * CUT - biases.shape[0])).reshape(-1, CUT)
+    tow = tower_weights.reshape(layers, 2, piece, 8, channels)
+    by_anchor = (0, 3, 1, 2)
+    marked = jnp.transpose(labels, by_anchor)[0]
+    lit = jnp.transpose(positive, by_anchor)[0]
+    goals = jnp.transpose(box_targets, by_anchor)[0]
     units = 32 * piece
     block = 4 * piece
     dma = pltpu.SemaphoreType.DMA
@@ -1250,7 +1375,7 @@
             shape((2, 8, CUT), full),
             shape((8, LANES), full),
         ),
-        in_specs=[vm] * 6,
+        in_specs=[vm, pl.BlockSpec(memory_space=pltpu.SMEM)] + [vm] * 6,
         out_specs=[vm] * 7,
         scratch_shapes=[
             pltpu.VMEM((7, units, 8, CUT), low),
@@ -1267,15 +1392,18 @@
             pltpu.VMEM((3, 2, px, CUT), full),
             pltpu.VMEM((px, CUT), full),
             pltpu.VMEM((px, CUT), low),
-            pltpu.VMEM((2, px, LANES), low),
-            pltpu.VMEM((2, px, LANES), full),
+            pltpu.VMEM((2, rows, 16, cols), full),
+            pltpu.VMEM((2, rows, 40, cols), full),
             pltpu.VMEM((3, 2, px, CUT), low),
             pltpu.VMEM((2, px, CUT), low),
-            pltpu.VMEM((px, CUT), full),
-            pltpu.VMEM((px, CUT), full),
+            pltpu.VMEM((px, CUT), low),
+            pltpu.VMEM((px, CUT), low),
             pltpu.VMEM((10, 8, LANES), full),
             pltpu.VMEM((8, CUT), full),
             pltpu.VMEM((11, 8, CUT), full),
+            pltpu.VMEM((layers, piece, 8, CUT), low),
+            pltpu.VMEM((3, piece, 8, CUT), low),
+            pltpu.VMEM((16, CUT), full),
             dma((6,)), dma((6,)),
             dma((6, 2, 3)), dma((6, 2, 3)),
             dma((6, 2)), dma((6, 2)),
@@ -1297,19 +1425,23 @@
         compiler_params=pltpu.CompilerParams(
             vmem_limit_bytes=60 * 1024 * 1024, collective_id=0, has_side_effects=True
         ),
-    )(features.reshape(px, channels), code, goals, tow, hed, bias)
-
-    step_float = step_count[0].astype(full)
-    scal = jnp.stack([1.0 - jnp.power(beta_one, step_float), 1.0 - jnp.power(beta_two, step_float)])
-    tgrad = tgrad.reshape(layers, 2, shard_rows, channels)
-    hgrad = hgrad.reshape(3, shard_rows, CUT)
+    )(features.reshape(px, channels), crop_ids, marked, lit, goals, tow, head_weights, biases)
+
     tower_shape = tower_weights.shape
     head_shape = head_weights.shape
-    outs = pl.pallas_call(
-        partial(finish_kernel, layers=layers, cls_out=cls_out, box_out=box_out),
+    anys = pl.BlockSpec(memory_space=pl.ANY)
+    smem = pl.BlockSpec(memory_space=pltpu.SMEM)
+    biases_out = biases.shape[0]
+    (
+        o_lg, o_dl, o_fg, o_tg, o_bg, o_hg, o_tn, o_hn, o_tm, o_tv, o_hm, o_hv, o_tc, o_hc,
+        o_loss, o_gb, o_gx, o_wb, o_mb, o_vb,
+    ) = pl.pallas_call(
+        partial(
+            finish_kernel, layers=layers, rows=rows, cols=cols, cls_out=cls_out, box_out=box_out
+        ),
         out_shape=(
             shape((px, cls_out), low),
-            shape((px, box_out), low),
+            shape((box_out, rows, cols), low),
             shape((px, channels), full),
             shape((layers, shard_rows, channels), full),
             shape((layers, shard_rows, channels), full),
@@ -1322,44 +1454,59 @@
             shape(head_shape, full),
             shape(tower_shape, low),
             shape(head_shape, low),
+            shape((1,), full),
+            shape((biases_out - box_out,), full),
+            shape((box_out,), full),
+            shape((biases_out,), full),
+            shape((biases_out,), full),
+            shape((biases_out,), full),
         ),
-        in_specs=[pl.BlockSpec(memory_space=pltpu.SMEM)] + [vm] * 11,
-        out_specs=[vm] * 14,
-        compiler_params=pltpu.CompilerParams(vmem_limit_bytes=40 * 1024 * 1024),
-    )(scal, logits, deltas, fgrad, tgrad, hgrad, tower_weights, head_weights, tower_m, tower_v, head_m, head_v)
-    (
-        o_lg, o_dl, o_fg, o_tg, o_bg, o_hg, o_tn, o_hn, o_tm, o_tv, o_hm, o_hv, o_tc, o_hc,
-    ) = outs
-    tail = cls_out - 2 * CUT
-    bias_grad = jnp.concatenate(
-        [
-            jnp.stack([bsum[0, :layers], bsum[1, :layers]], 1).reshape(-1),
-            bsum[0, 4:7].reshape(-1)[:cls_out],
-            bsum[1, 6, tail : tail + box_out],
-        ]
-    )
-    bias_new, bias_m_new, bias_v_new = adam_update(biases, bias_grad, bias_m, bias_v, step_float, 0.0)
-    split_at = bias_grad.shape[0] - box_out
+        in_specs=[smem, anys, vm, anys, anys, anys, vm, vm] + [anys] * 6 + [vm] * 3,
+        out_specs=[anys, vm] + [anys] * 12 + [smem] + [vm] * 5,
+        scratch_shapes=[
+            pltpu.VMEM(tower_shape, full),
+            pltpu.VMEM(tower_shape, full),
+            pltpu.VMEM(tower_shape, full),
+            pltpu.VMEM(tower_shape, full),
+            pltpu.VMEM(tower_shape, low),
+            pltpu.VMEM((3, shard_rows, CUT), full),
+            pltpu.VMEM(head_shape, full),
+            pltpu.VMEM(head_shape, full),
+            pltpu.VMEM(head_shape, full),
+            pltpu.VMEM(head_shape, full),
+            pltpu.VMEM(head_shape, low),
+            pltpu.VMEM((3, px, CUT), low),
+            pltpu.VMEM((px, cls_out), low),
+            pltpu.VMEM((rows, 40, cols), full),
+            pltpu.VMEM((box_out, rows, cols), full),
+            pltpu.VMEM((px, channels), full),
+            dma((layers, 4)), dma((layers, 6)), dma((4,)), dma((5,)), dma((4,)),
+        ],
+        compiler_params=pltpu.CompilerParams(vmem_limit_bytes=60 * 1024 * 1024),
+    )(
+        step_count, logits, deltas, fgrad, tgrad.reshape(tower_shape), hgrad.reshape(3, shard_rows, CUT), bsum, loss,
+        tower_weights, head_weights, tower_m, tower_v, head_m, head_v, biases, bias_m, bias_v,
+    )
     field = (canvases, rows, cols, -1)
     return (
         o_lg.reshape(field),
-        o_dl.reshape(field),
-        loss[0, 0],
+        jnp.transpose(o_dl[None], (0, 2, 3, 1)),
+        o_loss.reshape(()),
         o_fg.reshape(field),
         o_tg,
         o_bg,
         o_hg,
-        bias_grad[:split_at],
-        bias_grad[split_at:],
+        o_gb,
+        o_gx,
         o_tn,
         o_hn,
-        bias_new,
+        o_wb,
         o_tm,
         o_tv,
         o_hm,
         o_hv,
-        bias_m_new,
-        bias_v_new,
+        o_mb,
+        o_vb,
         o_tc,
         o_hc,
     )

time: 184 us -> 162 us (0.88); the launches traced: 180 us -> 161 us
  local copies, waits for them, and re-layouts: 13.3 us -> 0 us
  other arithmetic: 3.09 us -> 0 us
  Pallas kernels: 163 us -> 160 us
    unnamed x39 -> x0, local copies, waits for them, and re-layouts: 8.79 us -> none
    pallas_call x1, Pallas kernels: 159 us -> 153 us  [fused_shards(): pl.pallas_call(partial(mega_kernel, rows=rows, cols=cols, layers=layers,...]
    pallas_call x1, Pallas kernels: 3.3 us -> 6.87 us  [fused_shards(): pl.pallas_call(partial(finish_kernel, layers=layers, rows=rows, cols=cols...]
where the time goes in v2:
time: 162 us; the launch traced here: 161 us
  Pallas kernels  160 us (99%)
    pallas_call x1, Pallas kernels, fused_shards(): pl.pallas_call(partial(mega_kernel, rows=rows, cols=cols, layers=layers,...  153 us
    pallas_call x1, Pallas kernels, fused_shards(): pl.pallas_call(partial(finish_kernel, layers=layers, rows=rows, cols=cols...  6.87 us

profile of v2, /device:TPU:0, one launch (start us, length us, event | category | flops | bytes accessed | tf_op | source)
XLA Modules:
  0.0 161.4 jit_solution(8697677770399328629)
XLA Ops:
  1.3 153.2 %shard_map.302 = (bf16[3,512,256]{2,1,0:T(8,128)(2,1)}, bf16[512,256]{1,0:T(8,128)(2,1)}, f32[512,256]{1,0:T(8,128)}, f32[4,2,9,8,256]{4,3,2,1,0:T(8,128)}, f32[...) custom-call(bf16[512,256]{1,0:T(8,128)(2,1)} %bitcast.21, s32[1,32]{1,0:T(1,128)} %crops.1, ...), custom_call_target="tpu_custom_call" | custom-call | tf_op jit(solution)/shard_map/pallas_call | solution.py:1364
  154.5 6.9 %shard_map.303 = (bf16[512,720]{1,0:T(8,128)(2,1)}, bf16[36,8,64]{2,1,0:T(8,128)(2,1)}, f32[512,256]{1,0:T(8,128)}, f32[4,72,256]{2,1,0:T(8,128)}, f32[4,72,256]...) custom-call(s32[1]{0:T(128)S(6)} %copy.35.step, ...), custom_call_target="tpu_custom_call" | custom-call | tf_op jit(solution)/shard_map/pallas_call | solution.py:1438

commit v3 on v2

--- a/solution.py
+++ b/solution.py
@@ -302,7 +302,7 @@
 def mega_kernel(
     feat, crops, marked, lit, goals, tow, hed, bias_all,
     logits, deltas, fgrad, tgrad, hgrad, bsum, loss_out,
-    W, D, RD, RY, RZ, RX, RP, A3, HA, G, Z, U, ACC, FP, CP, GP, LS, ES, FS, FR, CNT, BG, BR, TB, HB, bias,
+    W, D, RD, RY, RZ, RX, RP, A3, HA, G, Z, U, ACC, FP, CP, GP, LS, CNT, BG, BR, TB, HB, bias, MK,
     ps, pr, zs, zr, ys, yr, ds, dr, xs, xr, fs, fr, hs, hr, gs, gr, ls, lr, es, er,
     rds, rdr, rys, ryr, rzs, rzr, rxs, rxr, rps, rpr, ns, nr, bs, br,
     *, rows, cols, layers, cls_out, box_out, anchors, piece,
@@ -339,21 +339,43 @@
         return lax.rem(z + 4 - o, 4)
 
     barrier = pltpu.get_barrier_semaphore()
-    for dev in [(sib, z), (par, z), (yn, z)] + [(d, zpeer(o)) for o in (1, 2, 3)]:
+    peers = [(sib, z), (par, z), (yn, z), (par, zpeer(1)), (par, zpeer(3))]
+    for dev in peers + [(d, zpeer(o)) for o in (1, 2, 3)]:
         pl.semaphore_signal(barrier, inc=1, device_id=dev, device_id_type=MESH)
-    pl.semaphore_wait(barrier, 6)
+    pl.semaphore_wait(barrier, 8)
+
+    def f_edge(side, across):
+        src = feat.at[pl.ds((rows - 1) * cols if side == 0 else 0, cols)]
+        dev = (par if across else d, zpeer(1) if side == 0 else zpeer(3))
+        return remote(src, HA.at[0, side, x], hs.at[0, side, across], hr.at[0, side, across], dev)
+
+    def f_edge_in(side, across):
+        dst = HA.at[0, side, 1 - x if across else x]
+        return remote(dst, dst, hs.at[0, side, across], hr.at[0, side, across], (par, zpeer(1)))
+
+    @pl.when(z < 3)
+    def _():
+        for across in range(2):
+            f_edge(0, across).start()
+
+    @pl.when(z > 0)
+    def _():
+        for across in range(2):
+            f_edge(1, across).start()
 
     def slot_of(step):
-        return jnp.where(step == 4, 4 + 2 * x, step)
-
-    def p_send(step):
+        odd = jnp.where(step == 1, 6, jnp.where(step == 3, 5, 3))
+        return jnp.where(is_cls, step, jnp.where(lax.rem(step, 2) == 0, step // 2, odd))
+
+    def p_send(layer):
+        theirs = jnp.where(is_cls, jnp.minimum(2 * layer, 5), layer)
         return remote(
-            TB.at[step], W.at[step, pcs(y, x, k, z)], ps.at[step], pr.at[step], (par, z)
+            TB.at[layer], W.at[layer, pcs(y, x, k, z)], ps.at[layer], pr.at[theirs], (par, z)
         )
 
-    def p_head(cut, index):
+    def p_head(cut, index, theirs):
         return remote(
-            HB.at[cut], W.at[4 + cut, pcs(y, x, k, z)], ps.at[index], pr.at[index], (par, z)
+            HB.at[cut], W.at[4 + cut, pcs(y, x, k, z)], ps.at[index], pr.at[theirs], (par, z)
         )
 
     def p_recv(step):
@@ -377,12 +399,12 @@
         here = W.at[slot, blk(yy, xx, kk)]
         return remote(here, here, ds.at[slot, yy * 2 + xx], dr.at[slot, yy * 2 + xx], (sib, z))
 
-    def x_copy(yy, xx):
-        here = W.at[6, blk(yy, xx, k)]
-        return remote(here, here, xs.at[yy * 2 + xx], xr.at[yy * 2 + xx], (par, z))
+    def x_copy(slot, yy, xx):
+        here = W.at[slot, blk(yy, xx, k)]
+        return remote(here, here, xs.at[slot - 5, yy * 2 + xx], xr.at[slot - 5, yy * 2 + xx], (par, z))
 
     def has(step):
-        return (step < 5) | is_cls
+        return (step < 5) | (is_box & (step < 6))
 
     def do_z(step):
         @pl.when(has(step))
@@ -393,18 +415,27 @@
                     z_send(step, xx, o).start()
 
     def spread(step, yy, xx):
-        d_copy(slot_of(step), yy, xx, k).start()
-
-        @pl.when(is_box & (step == 4))
-        def _():
-            x_copy(yy, xx).start()
-
-    def do_y(step):
+        slot = slot_of(step)
+
+        @pl.when(slot >= 5)
+        def _():
+            x_copy(slot, yy, xx).start()
+
+        @pl.when(slot != 5)
+        def _():
+            d_copy(slot, yy, xx, k).start()
+
+    def do_y(step, lead=False):
         @pl.when(has(step))
         def _():
             for xx in range(2):
                 for o in (1, 2, 3):
                     z_recv(step, xx, o).wait_recv()
+                if lead:
+                    if xx == 0:
+                        p_recv(step + 1).wait_recv()
+                    for o in (2, 1, 3):
+                        z_send(step + 1, xx, o).start()
                 y_copy(step, xx, y).start()
                 spread(step, y, xx)
 
@@ -415,16 +446,32 @@
                 y_copy(step, xx, 1 - y).wait_recv()
                 spread(step, 1 - y, xx)
 
+    def pump(step, carry=0):
+        do_y(step)
+        do_d(step - 1)
+
+        @pl.when(step < 5)
+        def _():
+            do_z(step + 1)
+
+        return carry
+
+    def handed_over(slot):
+        for b in range(4):
+            x_copy(slot, b // 2, b % 2).wait_recv()
+            d_copy(slot, b // 2, b % 2, k).start()
+
     def gathered(slot):
         for b in range(4):
             d_copy(slot, b // 2, b % 2, 1 - k).wait_recv()
 
+    pltpu_feature = remote(feat, FP, fs.at[0], fr.at[0], (par, z))
     for step in range(layers):
         TB[step] = tow[step, 1 - x].astype(low)
         p_send(step).start()
+        if step == 0:
+            pltpu_feature.start()
         W[step, pcs(y, x, k, z)] = tow[step, x].astype(low)
-    pltpu_feature = remote(feat, FP, fs.at[0], fr.at[0], (par, z))
-    pltpu_feature.start()
     tail = cls_out + box_out - 2 * CUT
     HB[2] = jnp.zeros((piece, 8, CUT), low)
     for cut, width in ((2, tail), (0, CUT), (1, CUT)):
@@ -433,23 +480,122 @@
 
     @pl.when(is_cls)
     def _():
-        p_head(2, 4).start()
+        p_head(2, 4, 1).start()
+        p_head(1, 5, 3).start()
         W[4, pcs(y, x, k, z)] = HB[0]
-        W[5, pcs(y, x, k, z)] = HB[1]
 
     @pl.when(is_box)
     def _():
-        p_head(0, 4).start()
-        p_head(1, 5).start()
+        p_head(0, 4, 4).start()
+        W[5, pcs(y, x, k, z)] = HB[1]
         W[6, pcs(y, x, k, z)] = HB[2]
 
     code_copy = remote(CP.at[x], CP.at[x], fs.at[1], fr.at[1], (par, z))
     goal_copy = remote(GP.at[x], GP.at[x], fs.at[2], fr.at[2], (par, z))
     do_z(0)
-    do_z(1)
 
     def n_copy(index, dst, dev):
         return remote(CNT.at[index], CNT.at[dst], ns.at[dst], nr.at[dst], dev)
+
+    col = lax.broadcasted_iota(jnp.int32, (cols, CUT), 0)
+    first_col = col == 0
+    last_col = col == cols - 1
+
+    def move_right(v):
+        return jnp.where(first_col, 0.0, pltpu.roll(v, 1, 0))
+
+    def move_left(v):
+        return jnp.where(last_col, 0.0, pltpu.roll(v, cols - 1, 0))
+
+    def put_row(layer, cv, row, value):
+        at = pl.ds(pl.multiple_of(row * cols, cols), cols)
+        A3[layer, cv, at, 0:CUT] = move_right(value).astype(low)
+        A3[layer, cv, at, CUT : 2 * CUT] = value.astype(low)
+        A3[layer, cv, at, 2 * CUT : 3 * CUT] = move_left(value).astype(low)
+
+    def up_ok():
+        return z > 0
+
+    def down_ok():
+        return z < 3
+
+    def a_edge(layer, side, cv):
+        row = rows if side == 0 else 1
+        src = A3.at[layer, cv, pl.ds(row * cols, cols), pl.ds(CUT, CUT)]
+        dev = (d, lax.rem(z + 1, 4)) if side == 0 else (d, lax.rem(z + 3, 4))
+        return remote(src, HA.at[layer, side, cv], hs.at[layer, side, cv], hr.at[layer, side, cv], dev)
+
+    def send_edges(layer, cv):
+        @pl.when(down_ok())
+        def _():
+            a_edge(layer, 0, cv).start()
+
+        @pl.when(up_ok())
+        def _():
+            a_edge(layer, 1, cv).start()
+
+    def first_edges():
+        for side, there in ((0, z > 0), (1, z < 3)):
+            @pl.when(there)
+            def _():
+                for across in range(2):
+                    f_edge_in(side, across).wait_recv()
+                    cv = 1 - x if across else x
+                    put_row(0, cv, 0 if side == 0 else rows + 1, HA[0, side, cv].astype(full))
+
+    def take_edges(layer, cv):
+        @pl.when(up_ok())
+        def _():
+            a_edge(layer, 0, cv).wait_recv()
+            put_row(layer, cv, 0, HA[layer, 0, cv].astype(full))
+
+        @pl.when(down_ok())
+        def _():
+            a_edge(layer, 1, cv).wait_recv()
+            put_row(layer, cv, rows + 1, HA[layer, 1, cv].astype(full))
+
+    def rim_first(body, carry, send):
+        carry = lax.fori_loop(0, 2, lambda i, c: body(i * (rows - 1), c), carry)
+        send()
+        return lax.fori_loop(1, rows - 1, body, carry)
+
+    def g_edge(slot, side, cv):
+        src = G.at[slot, cv, pl.ds((rows if side == 0 else 1) * cols, cols)]
+        dst = G.at[slot, cv, pl.ds(0 if side == 0 else (rows + 1) * cols, cols)]
+        dev = (d, lax.rem(z + 1, 4)) if side == 0 else (d, lax.rem(z + 3, 4))
+        return remote(src, dst, gs.at[slot, side, cv], gr.at[slot, side, cv], dev)
+
+    def g_recv(slot, side, cv):
+        dst = G.at[slot, cv, pl.ds(0 if side == 0 else (rows + 1) * cols, cols)]
+        return remote(dst, dst, gs.at[slot, side, cv], gr.at[slot, side, cv], (d, lax.rem(z + 1, 4)))
+
+    def send_g(slot, cv):
+        @pl.when(down_ok())
+        def _():
+            g_edge(slot, 0, cv).start()
+
+        @pl.when(up_ok())
+        def _():
+            g_edge(slot, 1, cv).start()
+
+    def take_g(slot, cv):
+        @pl.when(up_ok())
+        def _():
+            g_recv(slot, 0, cv).wait_recv()
+
+        @pl.when(down_ok())
+        def _():
+            g_recv(slot, 1, cv).wait_recv()
+
+    def fill(layer_src, cv):
+        def body(r, carry):
+            put_row(0, cv, r + 1, layer_src[pl.ds(pl.multiple_of(r * cols, cols), cols), :].astype(full))
+            return carry
+
+        lax.fori_loop(0, rows, body, 0)
+
+    fill(feat, x)
+    do_y(0, lead=True)
 
     r_at = lax.broadcasted_iota(jnp.int32, (rows, cols), 0)
     inside = jnp.zeros((rows, cols), jnp.int32)
@@ -473,96 +619,11 @@
     CNT[0] = jnp.broadcast_to(jnp.sum(picked), (8, LANES))
     n_copy(0, 4, (sib, z)).start()
 
-    col = lax.broadcasted_iota(jnp.int32, (cols, CUT), 0)
-    first_col = col == 0
-    last_col = col == cols - 1
-
-    def move_right(v):
-        return jnp.where(first_col, 0.0, pltpu.roll(v, 1, 0))
-
-    def move_left(v):
-        return jnp.where(last_col, 0.0, pltpu.roll(v, cols - 1, 0))
-
-    def put_row(layer, cv, row, value):
-        at = pl.ds(pl.multiple_of(row * cols, cols), cols)
-        A3[layer, cv, at, 0:CUT] = move_right(value).astype(low)
-        A3[layer, cv, at, CUT : 2 * CUT] = value.astype(low)
-        A3[layer, cv, at, 2 * CUT : 3 * CUT] = move_left(value).astype(low)
-
-    def up_ok():
-        return z > 0
-
-    def down_ok():
-        return z < 3
-
-    def a_edge(layer, side, cv):
-        row = rows if side == 0 else 1
-        src = A3.at[layer, cv, pl.ds(row * cols, cols), pl.ds(CUT, CUT)]
-        dev = (d, lax.rem(z + 1, 4)) if side == 0 else (d, lax.rem(z + 3, 4))
-        return remote(src, HA.at[layer, side, cv], hs.at[layer, side, cv], hr.at[layer, side, cv], dev)
-
-    def send_edges(layer, cv):
-        @pl.when(down_ok())
-        def _():
-            a_edge(layer, 0, cv).start()
-
-        @pl.when(up_ok())
-        def _():
-            a_edge(layer, 1, cv).start()
-
-    def take_edges(layer, cv):
-        @pl.when(up_ok())
-        def _():
-            a_edge(layer, 0, cv).wait_recv()
-            put_row(layer, cv, 0, HA[layer, 0, cv].astype(full))
-
-        @pl.when(down_ok())
-        def _():
-            a_edge(layer, 1, cv).wait_recv()
-            put_row(layer, cv, rows + 1, HA[layer, 1, cv].astype(full))
-
-    def rim_first(body, carry, send):
-        carry = lax.fori_loop(0, 2, lambda i, c: body(i * (rows - 1), c), carry)
-        send()
-        return lax.fori_loop(1, rows - 1, body, carry)
-
-    def g_edge(slot, side, cv):
-        src = G.at[slot, cv, pl.ds((rows if side == 0 else 1) * cols, cols)]
-        dst = G.at[slot, cv, pl.ds(0 if side == 0 else (rows + 1) * cols, cols)]
-        dev = (d, lax.rem(z + 1, 4)) if side == 0 else (d, lax.rem(z + 3, 4))
-        return remote(src, dst, gs.at[slot, side, cv], gr.at[slot, side, cv], dev)
-
-    def g_recv(slot, side, cv):
-        dst = G.at[slot, cv, pl.ds(0 if side == 0 else (rows + 1) * cols, cols)]
-        return remote(dst, dst, gs.at[slot, side, cv], gr.at[slot, side, cv], (d, lax.rem(z + 1, 4)))
-
-    def send_g(slot, cv):
-        @pl.when(down_ok())
-        def _():
-            g_edge(slot, 0, cv).start()
-
-        @pl.when(up_ok())
-        def _():
-            g_edge(slot, 1, cv).start()
-
-    def take_g(slot, cv):
-        @pl.when(up_ok())
-        def _():
-            g_recv(slot, 0, cv).wait_recv()
-
-        @pl.when(down_ok())
-        def _():
-            g_recv(slot, 1, cv).wait_recv()
-
-    def fill(layer_src, cv):
-        def body(r, carry):
-            put_row(0, cv, r + 1, layer_src[pl.ds(pl.multiple_of(r * cols, cols), cols), :].astype(full))
-            return carry
-
-        lax.fori_loop(0, rows, body, 0)
-
-    fill(feat, x)
-    send_edges(0, x)
+    code_copy.start()
+    pltpu_feature.wait_recv()
+    fill(FP, 1 - x)
+    first_edges()
+    pump(1)
 
     def clear(at, layer_count, slot_count):
         def a_body(layer, carry):
@@ -601,29 +662,49 @@
     bias[q : q + 1, :] = jnp.zeros((1, CUT), full)
     bias[q : q + 1, 0:tail] = bias_all[q * CUT : q * CUT + tail].reshape(1, tail)
 
+    U[...] = jnp.zeros(U.shape, full)
+
+    @pl.when(is_cls)
+    def _():
+        goal_copy.start()
+
     n_copy(0, 4, (sib, z)).wait_recv()
     CNT[1] = CNT[0] + CNT[4]
     n_copy(1, 5, (yn, z)).start()
-    do_y(0)
-    do_z(2)
-    n_copy(1, 5, (yn, z)).wait_recv()
-    CNT[2] = CNT[1] + CNT[5]
-    n_copy(2, 6, (par, z)).start()
-    pltpu_feature.wait_recv()
-    fill(FP, 1 - x)
-    send_edges(0, 1 - x)
-    n_copy(2, 6, (par, z)).wait_recv()
-    CNT[3] = CNT[2] + CNT[6]
-    for o in (1, 2, 3):
-        n_copy(3, 6 + o, (d, zpeer(o))).start()
-    do_y(1)
-    do_d(0)
-    do_z(3)
-    code_copy.start()
-
-    @pl.when(is_cls)
-    def _():
-        goal_copy.start()
+
+    lane_tab = lax.broadcasted_iota(jnp.int32, (16, CUT), 1)
+    anchor_tab = lax.broadcasted_iota(jnp.int32, (16, CUT), 0)
+
+    def write_marks():
+        remote(CP.at[1 - x], CP.at[1 - x], fs.at[1], fr.at[1], (par, z)).wait_recv()
+        spot = lane_tab - (cls_out - 2 * CUT)
+        box_tab = jnp.where(
+            (spot >= anchor_tab * 4) & (spot < (anchor_tab + 1) * 4) & (anchor_tab < anchors), 1.0, 0.0
+        )
+        tables = []
+        for cut in range(3):
+            channel = lane_tab + cut * CUT
+            table = jnp.where(
+                (channel >= anchor_tab * classes) & (channel < (anchor_tab + 1) * classes) & (channel < cls_out),
+                1.0,
+                0.0,
+            )
+            if cut == 2:
+                side = x.astype(full)
+                table = table * (1.0 - side) + box_tab * side
+            tables.append(table.astype(low))
+
+        def row(r, carry):
+            at = pl.ds(pl.multiple_of(r * cols, cols), cols)
+            for cv in range(2):
+                codes = CP[cv, r].astype(low)
+                for cut in range(3):
+                    MK[cut, cv, at, :] = lax.dot_general(
+                        codes, tables[cut], (((0,), (0,)), ((), ())), preferred_element_type=full
+                    ).astype(low)
+            return carry
+
+        lax.fori_loop(0, rows, row, 0)
 
     def conv(layer, slot, cv):
         total = None
@@ -641,7 +722,10 @@
         shift = bias[pl.ds(2 * layer + x, 1), :]
 
         def canvas(cv, carry):
-            take_edges(layer, cv)
+            @pl.when(layer > 0)
+            def _():
+                take_edges(layer, cv)
+
             Z[layer, cv] = conv(layer, layer, cv)
 
             def row(r, carry):
@@ -655,22 +739,36 @@
             return carry
 
         lax.fori_loop(0, 2, canvas, 0)
-        do_y_when = layer + 2
-        do_y(do_y_when)
-        do_d(layer + 1)
-
-        @pl.when(layer < 2)
-        def _():
-            do_z(layer + 4)
+        first = jnp.where(is_cls, layer + 2, 2 * layer + 2)
+        after = jnp.where(is_cls, jnp.minimum(layer + 3, 5), jnp.minimum(2 * layer + 4, 7))
+        lax.fori_loop(first, after, pump, 0)
+
+        @pl.when(layer == 0)
+        def _():
+            n_copy(1, 5, (yn, z)).wait_recv()
+            CNT[2] = CNT[1] + CNT[5]
+            n_copy(2, 6, (par, z)).start()
+
+        @pl.when(layer == 1)
+        def _():
+            write_marks()
+            n_copy(2, 6, (par, z)).wait_recv()
+            CNT[3] = CNT[2] + CNT[6]
+            for o in (1, 2, 3):
+                n_copy(3, 6 + o, (d, zpeer(o))).start()
 
         return carry
 
     lax.fori_loop(0, layers, forward, 0)
-    do_d(5)
     for o in (1, 2, 3):
         n_copy(3, 6 + o, (d, zpeer(o))).wait_recv()
     count = CNT[3] + CNT[7] + CNT[8] + CNT[9]
     grad_scale = (1.0 / jnp.maximum(count, 1.0))[0:1, 0:1]
+
+    @pl.when(is_cls)
+    def _():
+        handed_over(6)
+
     for cv in range(2):
         take_edges(layers, cv)
 
@@ -688,19 +786,20 @@
             src, RZ.at[slot, xx, o - 1], rzs.at[slot, xx, o - 1], rzr.at[slot, xx, o - 1], (d, zpeer(o))
         )
 
-    def rx_send(b):
-        src = D.at[6, blk(b // 2, b % 2, k)]
+    def rx_send(slot, b):
+        src = D.at[slot, blk(b // 2, b % 2, k)]
         return remote(src, RX.at[b], rxs.at[b], rxr.at[b], (par, z))
 
-    def add_into(slot, place, terms):
+    def add_into(slot, place, terms, own=True):
         units = block // 3
 
         def body(i, carry):
             here = pl.ds(place + i * units, units)
             there = pl.ds(i * units, units)
-            total = D[slot, here].astype(full)
+            total = D[slot, here].astype(full) if own else None
             for ref in terms:
-                total = total + ref[there].astype(full)
+                term = ref[there].astype(full)
+                total = term if total is None else total + term
             D[slot, here] = total.astype(low)
             return carry
 
@@ -713,34 +812,34 @@
         for b in range(4):
             rd_send(slot, b).start()
 
-    def do_ry(slot, relay=False):
+    def here_terms(slot, b, own, relay):
+        terms = []
+        if own:
+            rd_send(slot, b).wait_recv()
+            terms.append(RD.at[slot, b])
+        if relay:
+            rx_send(slot, b).wait_recv()
+            terms.append(RX.at[b])
+        return terms
+
+    def do_ry(slot, own=True, relay=False, halves=(0, 1)):
+        for xx in halves:
+            terms = here_terms(slot, (1 - y) * 2 + xx, own, relay)
+            add_into(slot, start_of(1 - y, xx, k), terms, own)
+            ry_send(slot, xx).start()
+
+    def do_rx(slot):
+        for b in range(4):
+            rd_send(slot, b).wait_recv()
+            add_into(slot, start_of(b // 2, b % 2, k), [RD.at[slot, b]])
+            rx_send(slot, b).start()
+
+    def do_rz(slot, own=True, relay=False):
         for xx in range(2):
-            b = (1 - y) * 2 + xx
-            rd_send(slot, b).wait_recv()
-            terms = [RD.at[slot, b]]
-            if relay:
-                rx_send(b).wait_recv()
-                terms.append(RX.at[b])
-            add_into(slot, start_of(1 - y, xx, k), terms)
-            ry_send(slot, xx).start()
-
-    def do_rx():
-        for b in range(4):
-            rd_send(6, b).wait_recv()
-            add_into(6, start_of(b // 2, b % 2, k), [RD.at[6, b]])
-            rx_send(b).start()
-
-    def do_rz(slot, relay=False):
-        for xx in range(2):
-            b = y * 2 + xx
-            rd_send(slot, b).wait_recv()
-            terms = [RD.at[slot, b]]
-            if relay:
-                rx_send(b).wait_recv()
-                terms.append(RX.at[b])
+            terms = here_terms(slot, y * 2 + xx, own, relay)
             ry_send(slot, xx).wait_recv()
             terms.append(RY.at[slot, xx])
-            add_into(slot, start_of(y, xx, k), terms)
+            add_into(slot, start_of(y, xx, k), terms, own)
             for o in (2, 1, 3):
                 rz_send(slot, xx, o).start()
 
@@ -807,21 +906,12 @@
         return jnp.sum(value.reshape(cols // 8, 8, CUT), axis=0)
 
     lane = lax.broadcasted_iota(jnp.int32, (1, CUT), 1)
-    lane_tab = lax.broadcasted_iota(jnp.int32, (16, CUT), 1)
-    anchor_tab = lax.broadcasted_iota(jnp.int32, (16, CUT), 0)
-
-    def spread_marks(cv, r, table):
-        return lax.dot_general(
-            CP[cv, r].astype(low), table, (((0,), (0,)), ((), ())), preferred_element_type=full
-        )
-
     box_from = cls_out - 2 * CUT
 
+    def log_one_plus(e):
+        return jnp.where(e < 0.015625, e * (1.0 + e * (e * (1.0 / 3.0) - 0.5)), jnp.log(1.0 + e))
+
     def cls_rows(cut, cv, shift):
-        channel = lane_tab + cut * CUT
-        spread_tab = (
-            (channel >= anchor_tab * classes) & (channel < (anchor_tab + 1) * classes) & (channel < cls_out)
-        ).astype(full).astype(low)
         here = lane + cut * CUT
         number = here
         for a in range(1, anchors):
@@ -833,7 +923,7 @@
             at = pl.ds(pl.multiple_of(r * cols, cols), cols)
             raw = ACC[at, :] + shift
             LS[cut, cv, at, :] = raw.astype(low)
-            marks = spread_marks(cv, r, spread_tab)
+            marks = MK[cut, cv, at, :].astype(full)
             hit = marks == number
             seen = marks < -50.0
             s = jnp.where(hit, -raw, raw)
@@ -842,7 +932,7 @@
             other = e * inv
             q = jnp.where(s >= 0.0, inv, other)
             p = jnp.where(s >= 0.0, other, inv)
-            soft = jnp.maximum(s, 0.0) + jnp.log1p(e)
+            soft = jnp.maximum(s, 0.0) + log_one_plus(e)
             t = jnp.where(seen, jnp.where(hit, focal_alpha, 1.0 - focal_alpha), 0.0) * q * q
             slope = t * (2.0 * p * soft + q) * grad_scale
             g = jnp.where(hit, -slope, slope).astype(low)
@@ -852,10 +942,6 @@
         return row
 
     def box_rows(cut, cv, shift):
-        spot = lane_tab - box_from
-        spread_tab = (
-            (spot >= anchor_tab * 4) & (spot < (anchor_tab + 1) * 4) & (anchor_tab < anchors)
-        ).astype(full).astype(low)
         goal_lane = lax.broadcasted_iota(jnp.int32, (40, LANES), 1) - (box_from - LANES)
         goal_tab = (goal_lane == lax.broadcasted_iota(jnp.int32, (40, LANES), 0)).astype(full)
 
@@ -863,8 +949,8 @@
             b_sum, l_sum = carry
             at = pl.ds(pl.multiple_of(r * cols, cols), cols)
             raw = ACC[at, :] + shift
-            ES[cv, at, :] = raw.astype(low)
-            marks = spread_marks(cv, r, spread_tab)
+            LS[0, cv, at, :] = raw.astype(low)
+            marks = MK[cut, cv, at, :].astype(full)
             chosen = marks < -110.0
             want = lax.dot_general(
                 GP[cv, r], goal_tab, (((0,), (0,)), ((), ())),
@@ -891,24 +977,15 @@
         return remote(LS.at[cut, 1 - x], logits.at[cut], ls.at[cut], lr.at[cut], (par, z))
 
     def e_copy():
-        return remote(ES.at[1 - x], deltas, es.at[0], er.at[0], (par, z))
-
-    U[...] = jnp.zeros(U.shape, full)
-    remote(CP.at[1 - x], CP.at[1 - x], fs.at[1], fr.at[1], (par, z)).wait_recv()
+        return remote(LS.at[0, 1 - x], deltas, es.at[0], er.at[0], (par, z))
 
     @pl.when(is_box)
     def _():
         remote(GP.at[1 - x], GP.at[1 - x], fs.at[2], fr.at[2], (par, z)).wait_recv()
 
-    def head(cut, carry):
+    def head(i, carry):
+        cut = 2 - i
         slot = 4 + cut
-
-        @pl.when(is_cls & (cut == 2))
-        def _():
-            for b in range(4):
-                x_copy(b // 2, b % 2).wait_recv()
-                d_copy(6, b // 2, b % 2, k).start()
-
         gathered(slot)
         shift = bias[pl.ds(2 * layers + cut, 1), :]
 
@@ -923,10 +1000,6 @@
 
         b_sum, l_sum = lax.fori_loop(0, 2, canvas, (nothing, nothing))
 
-        @pl.when(is_cls)
-        def _():
-            l_copy(cut).start()
-
         @pl.when(is_box)
         def _():
             e_copy().start()
@@ -938,32 +1011,36 @@
 
         input_grad(slot, True)
 
-        @pl.when(cut < 2)
+        @pl.when(is_cls & (i == 0))
+        def _():
+            do_d(4)
+            handed_over(5)
+
+        @pl.when(is_cls & (i == 0))
+        def _():
+            do_rx(slot)
+
+        @pl.when(i > 0)
         def _():
             do_ry(slot)
 
-        @pl.when(cut == 1)
-        def _():
-            do_rz(4)
-
-        @pl.when(is_cls & (cut == 2))
-        def _():
-            do_rx()
+        @pl.when(i == 2)
+        def _():
             do_rz(5)
-            do_rp_head(4)
 
         return carry
 
-    lax.fori_loop(2 * x, 3, head, 0)
+    lax.fori_loop(0, 3 - 2 * x, head, 0)
 
     @pl.when(is_cls)
     def _():
         for cut in range(3):
+            l_copy(cut).start()
             logits[cut] = LS[cut, 0]
 
     @pl.when(is_box)
     def _():
-        deltas[...] = ES[1]
+        deltas[...] = LS[0, 1]
 
     def feature_rows(cv, dst):
         def row(r, carry):
@@ -972,7 +1049,8 @@
 
         lax.fori_loop(0, rows, row, 0)
 
-    f_copy = remote(FS, FR, fs.at[3], fr.at[3], (par, z))
+    FS = MK.at[0, 0]
+    f_copy = remote(FS, FP, fs.at[3], fr.at[3], (par, z))
     def b_copy(src, dst, dev):
         return remote(src, BR.at[dst], bs.at[dst], br.at[dst], dev)
 
@@ -999,12 +1077,13 @@
 
         @pl.when(j == layers - 1)
         def _():
-            do_ry(0)
+            do_ry(0, halves=(0,))
 
         input_grad(layer, False)
 
         @pl.when(j == layers - 1)
         def _():
+            do_ry(0, halves=(1,))
             feature_rows(1 - x, FS)
             f_copy.start()
 
@@ -1012,25 +1091,37 @@
         def _():
             do_ry(layer)
 
+        @pl.when(is_cls | (j > 0))
+        def _():
+            do_rz(layer + 1)
+
         @pl.when(is_cls & (j == 0))
         def _():
             do_rp_head(5)
 
-        @pl.when(j > 0)
-        def _():
-            do_rz(layer + 1)
+        @pl.when(is_cls & (j == 1))
+        def _():
+            do_rp_head(4)
 
         @pl.when(j > 1)
         def _():
             do_rp_layer(layer + 2)
 
+        @pl.when(is_box & (j == 0))
+        def _():
+            do_ry(6, relay=True)
+
+        @pl.when(is_box & (j == 1))
+        def _():
+            do_rz(6, relay=True)
+
+        @pl.when(is_box & (j == 2))
+        def _():
+            do_rp_head(6)
+
         return carry
 
     lax.fori_loop(0, layers, backward, 0)
-
-    @pl.when(is_box)
-    def _():
-        do_ry(6, relay=True)
 
     b_copy(BG, 0, (sib, z)).wait_recv()
     BR[6] = BG[...] + BR[0]
@@ -1048,10 +1139,6 @@
                 ).start()
     do_rz(0)
     do_rp_layer(1)
-
-    @pl.when(is_box)
-    def _():
-        do_rz(6, relay=True)
 
     for o in (1, 2, 3):
         for zz in range(4):
@@ -1066,12 +1153,8 @@
     last.start()
     bsum[x] = total
     f_copy.wait_recv()
-    fgrad[...] = fgrad[...] + FR[...].astype(full)
+    fgrad[...] = fgrad[...] + FP[...].astype(full)
     do_rp_layer(0)
-
-    @pl.when(is_box)
-    def _():
-        do_rp_head(6)
 
     remote(BR.at[5], bsum.at[1 - x], bs.at[5], br.at[5], (par, z)).wait_recv()
     loss = jnp.sum(bsum[0, 7:8, :] + bsum[1, 7:8, :], axis=1, keepdims=True)
@@ -1082,14 +1165,16 @@
 
     @pl.when(is_cls)
     def _():
+        e_copy().wait_recv()
         rp_send(6, hgrad.at[2]).wait_recv()
-        e_copy().wait_recv()
         for b in range(4):
-            rx_send(b).wait_send()
+            rx_send(6, b).wait_send()
+            d_copy(5, b // 2, b % 2, k).wait_send()
             d_copy(6, b // 2, b % 2, k).wait_send()
         for cut in range(3):
             l_copy(cut).wait_send()
-        p_head(2, 4).wait_send()
+        p_head(2, 4, 1).wait_send()
+        p_head(1, 5, 3).wait_send()
         goal_copy.wait_send()
 
     @pl.when(is_box)
@@ -1099,11 +1184,11 @@
         for cut in range(3):
             l_copy(cut).wait_recv()
         for b in range(4):
-            x_copy(b // 2, b % 2).wait_send()
+            x_copy(5, b // 2, b % 2).wait_send()
+            x_copy(6, b // 2, b % 2).wait_send()
             d_copy(6, b // 2, b % 2, k).wait_send()
         e_copy().wait_send()
-        p_head(0, 4).wait_send()
-        p_head(1, 5).wait_send()
+        p_head(0, 4, 4).wait_send()
 
     def close_gather(step, carry):
         for xx in range(2):
@@ -1112,29 +1197,27 @@
             y_copy(step, xx, y).wait_send()
         return carry
 
-    lax.fori_loop(0, 6 - x, close_gather, 0)
+    lax.fori_loop(0, 5 + x, close_gather, 0)
 
     def close_slot(slot, carry):
-        @pl.when((slot < 4) | is_cls)
-        def _():
-            for b in range(4):
-                d_copy(slot, b // 2, b % 2, k).wait_send()
+        for b in range(4):
+            d_copy(slot, b // 2, b % 2, k).wait_send()
 
         return carry
 
-    lax.fori_loop(0, 6 - 2 * x, close_slot, 0)
+    lax.fori_loop(0, 5 - x, close_slot, 0)
 
     def close_layer(layer, carry):
         @pl.when(layer < layers)
         def _():
             p_send(jnp.minimum(layer, layers - 1)).wait_send()
 
-        @pl.when(down_ok())
+        @pl.when(down_ok() & (layer > 0))
         def _():
             for cv in range(2):
                 a_edge(layer, 0, cv).wait_send()
 
-        @pl.when(up_ok())
+        @pl.when(up_ok() & (layer > 0))
         def _():
             for cv in range(2):
                 a_edge(layer, 1, cv).wait_send()
@@ -1171,6 +1254,17 @@
 
     lax.fori_loop(0, layers + 3, close_grad, 0)
     pltpu_feature.wait_send()
+
+    @pl.when(z < 3)
+    def _():
+        for across in range(2):
+            f_edge(0, across).wait_send()
+
+    @pl.when(z > 0)
+    def _():
+        for across in range(2):
+            f_edge(1, across).wait_send()
+
     code_copy.wait_send()
     f_copy.wait_send()
     n_copy(0, 4, (sib, z)).wait_send()
@@ -1188,24 +1282,16 @@
     step, lg, dl, fg, tg, hg, bsum, loss_in, tw, hw, tm, tv, hm, hv, bw, bm, bv,
     o_lg, o_dl, o_fg, o_tg, o_bg, o_hg, o_tn, o_hn, o_tm, o_tv, o_hm, o_hv, o_tc, o_hc,
     o_loss, o_gb, o_gx, o_wb, o_mb, o_vb,
-    TG, TW, TM, TV, TC, HG, HGO, HW, HM, HV, HC, LG, LO, DT, DS, FG,
-    t_in, t_out, h_in, h_out, m_sem,
+    TW, TM, TV, TC, HGO, HW, HM, HV, HC, LO, DT, DS, t_out, h_out, m_sem,
     *, layers, rows, cols, cls_out, box_out,
 ):
     tail = cls_out - 2 * CUT
     last = tail + box_out
 
-    def t_loads(layer):
-        pairs = ((tg, TG), (tw, TW), (tm, TM), (tv, TV))
-        return [
-            pltpu.make_async_copy(a.at[layer], b.at[layer], t_in.at[layer, i])
-            for i, (a, b) in enumerate(pairs)
-        ]
-
     def t_stores(layer):
         pairs = (
-            (TG.at[layer, 0], o_tg.at[layer]),
-            (TG.at[layer, 1], o_bg.at[layer]),
+            (tg.at[layer, 0], o_tg.at[layer]),
+            (tg.at[layer, 1], o_bg.at[layer]),
             (TW.at[layer], o_tn.at[layer]),
             (TM.at[layer], o_tm.at[layer]),
             (TV.at[layer], o_tv.at[layer]),
@@ -1213,25 +1299,16 @@
         )
         return [pltpu.make_async_copy(a, b, t_out.at[layer, i]) for i, (a, b) in enumerate(pairs)]
 
-    h_loads = [
-        pltpu.make_async_copy(a, b, h_in.at[i])
-        for i, (a, b) in enumerate(((hg, HG), (hw, HW), (hm, HM), (hv, HV)))
-    ]
     h_stores = [
         pltpu.make_async_copy(a, b, h_out.at[i])
         for i, (a, b) in enumerate(((HGO, o_hg), (HW, o_hn), (HM, o_hm), (HV, o_hv), (HC, o_hc)))
     ]
-    lg_load = pltpu.make_async_copy(lg, LG, m_sem.at[0])
-    lg_store = pltpu.make_async_copy(LO, o_lg, m_sem.at[1])
-    fg_load = pltpu.make_async_copy(fg, FG, m_sem.at[2])
-    fg_store = pltpu.make_async_copy(FG, o_fg, m_sem.at[3])
-    for layer in range(layers):
-        for copy in t_loads(layer):
-            copy.start()
-    for copy in h_loads:
-        copy.start()
-    fg_load.start()
-    lg_load.start()
+    lg_store = pltpu.make_async_copy(LO, o_lg, m_sem.at[0])
+    fg_store = pltpu.make_async_copy(fg, o_fg, m_sem.at[1])
+    fg_store.start()
+    for cut, width in ((0, CUT), (1, CUT), (2, tail)):
+        LO[:, cut * CUT : cut * CUT + width] = lg[cut][:, :width]
+    lg_store.start()
 
     steps = jnp.broadcast_to(step[0].astype(full), (8, CUT))
     keep_one = (1.0 - jnp.exp(steps * math.log(beta_one)))[0:1, :]
@@ -1248,9 +1325,28 @@
         )
         return weight_new, first_new, second_new
 
-    fg_load.wait()
-    fg_store.start()
-
+    for layer in range(layers):
+        for t in range(2):
+            w_new, m_new, v_new = adam(
+                tw[layer, t], tg[layer, t], tm[layer, t], tv[layer, t], decay_rate
+            )
+            TW[layer, t] = w_new
+            TM[layer, t] = m_new
+            TV[layer, t] = v_new
+            TC[layer, t] = w_new.astype(low)
+        for copy in t_stores(layer):
+            copy.start()
+    for cut, width in ((0, CUT), (1, CUT), (2, last)):
+        at = slice(cut * CUT, cut * CUT + width)
+        grad = hg[cut][:, :width]
+        HGO[:, at] = grad
+        w_new, m_new, v_new = adam(hw[:, at], grad, hm[:, at], hv[:, at], decay_rate)
+        HW[:, at] = w_new
+        HM[:, at] = m_new
+        HV[:, at] = v_new
+        HC[:, at] = w_new.astype(low)
+    for copy in h_stores:
+        copy.start()
     o_loss[0] = loss_in[0, 0]
     for q in range(2 * layers + 3):
         if q < 2 * layers:
@@ -1286,36 +1382,6 @@
     lax.fori_loop(0, box_out, turn, 0)
     o_dl[...] = DS[...].astype(low)
 
-    for layer in range(layers):
-        for copy in t_loads(layer):
-            copy.wait()
-        for t in range(2):
-            w_new, m_new, v_new = adam(
-                TW[layer, t], TG[layer, t], TM[layer, t], TV[layer, t], decay_rate
-            )
-            TW[layer, t] = w_new
-            TM[layer, t] = m_new
-            TV[layer, t] = v_new
-            TC[layer, t] = w_new.astype(low)
-        for copy in t_stores(layer):
-            copy.start()
-    lg_load.wait()
-    for cut, width in ((0, CUT), (1, CUT), (2, tail)):
-        LO[:, cut * CUT : cut * CUT + width] = LG[cut][:, :width]
-    lg_store.start()
-    for copy in h_loads:
-        copy.wait()
-    for cut, width in ((0, CUT), (1, CUT), (2, last)):
-        at = slice(cut * CUT, cut * CUT + width)
-        grad = HG[cut][:, :width]
-        HGO[:, at] = grad
-        w_new, m_new, v_new = adam(HW[:, at], grad, HM[:, at], HV[:, at], decay_rate)
-        HW[:, at] = w_new
-        HM[:, at] = m_new
-        HV[:, at] = v_new
-        HC[:, at] = w_new.astype(low)
-    for copy in h_stores:
-        copy.start()
     for layer in range(layers):
         for copy in t_stores(layer):
             copy.wait()
@@ -1395,20 +1461,18 @@
             pltpu.VMEM((2, rows, 16, cols), full),
             pltpu.VMEM((2, rows, 40, cols), full),
             pltpu.VMEM((3, 2, px, CUT), low),
-            pltpu.VMEM((2, px, CUT), low),
-            pltpu.VMEM((px, CUT), low),
-            pltpu.VMEM((px, CUT), low),
             pltpu.VMEM((10, 8, LANES), full),
             pltpu.VMEM((8, CUT), full),
             pltpu.VMEM((11, 8, CUT), full),
             pltpu.VMEM((layers, piece, 8, CUT), low),
             pltpu.VMEM((3, piece, 8, CUT), low),
             pltpu.VMEM((16, CUT), full),
+            pltpu.VMEM((3, 2, px, CUT), low),
             dma((6,)), dma((6,)),
             dma((6, 2, 3)), dma((6, 2, 3)),
             dma((6, 2)), dma((6, 2)),
             dma((7, 4)), dma((7, 4)),
-            dma((4,)), dma((4,)),
+            dma((2, 4)), dma((2, 4)),
             dma((4,)), dma((4,)),
             dma((layers + 1, 2, 2)), dma((layers + 1, 2, 2)),
             dma((7, 2, 2)), dma((7, 2, 2)),
@@ -1461,26 +1525,22 @@
             shape((biases_out,), full),
             shape((biases_out,), full),
         ),
-        in_specs=[smem, anys, vm, anys, anys, anys, vm, vm] + [anys] * 6 + [vm] * 3,
+        in_specs=[smem] + [vm] * 16,
         out_specs=[anys, vm] + [anys] * 12 + [smem] + [vm] * 5,
         scratch_shapes=[
             pltpu.VMEM(tower_shape, full),
             pltpu.VMEM(tower_shape, full),
             pltpu.VMEM(tower_shape, full),
-            pltpu.VMEM(tower_shape, full),
             pltpu.VMEM(tower_shape, low),
-            pltpu.VMEM((3, shard_rows, CUT), full),
             pltpu.VMEM(head_shape, full),
             pltpu.VMEM(head_shape, full),
             pltpu.VMEM(head_shape, full),
             pltpu.VMEM(head_shape, full),
             pltpu.VMEM(head_shape, low),
-            pltpu.VMEM((3, px, CUT), low),
             pltpu.VMEM((px, cls_out), low),
             pltpu.VMEM((rows, 40, cols), full),
             pltpu.VMEM((box_out, rows, cols), full),
-            pltpu.VMEM((px, channels), full),
-            dma((layers, 4)), dma((layers, 6)), dma((4,)), dma((5,)), dma((4,)),
+            dma((layers, 6)), dma((5,)), dma((2,)),
         ],
         compiler_params=pltpu.CompilerParams(vmem_limit_bytes=60 * 1024 * 1024),
     )(

time: 162 us -> 146 us (0.901)
  Pallas kernels: 160 us -> 145 us
    pallas_call x1, Pallas kernels: 153 us -> 139 us  [fused_shards(): pl.pallas_call(partial(mega_kernel, rows=rows, cols=cols, layers=layers,...]
where the time goes in v3:
time: 146 us
  Pallas kernels  145 us (99%)
    pallas_call x1, Pallas kernels, fused_shards(): pl.pallas_call(partial(mega_kernel, rows=rows, cols=cols, layers=layers,...  139 us
    pallas_call x1, Pallas kernels, fused_shards(): pl.pallas_call(partial(finish_kernel, layers=layers, rows=rows, cols=cols...  5.63 us

profile of v3, /device:TPU:0, one launch (start us, length us, event | category | flops | bytes accessed | tf_op | source)
XLA Modules:
  0.0 145.9 jit_solution(12597917394472278190)
XLA Ops:
  1.3 138.9 %shard_map.302 = (bf16[3,512,256]{2,1,0:T(8,128)(2,1)}, bf16[512,256]{1,0:T(8,128)(2,1)}, f32[512,256]{1,0:T(8,128)}, f32[4,2,9,8,256]{4,3,2,1,0:T(8,128)}, f32[...) custom-call(bf16[512,256]{1,0:T(8,128)(2,1)} %bitcast.21, s32[1,32]{1,0:T(1,128)} %crops.1, ...), custom_call_target="tpu_custom_call" | custom-call | tf_op jit(solution)/shard_map/pallas_call | solution.py:1430
  140.2 5.6 %shard_map.303 = (bf16[512,720]{1,0:T(8,128)(2,1)}, bf16[36,8,64]{2,1,0:T(8,128)(2,1)}, f32[512,256]{1,0:T(8,128)}, f32[4,72,256]{2,1,0:T(8,128)}, f32[4,72,256]...) custom-call(s32[1]{0:T(128)S(6)} %copy.35.step, ...), custom_call_target="tpu_custom_call" | custom-call | tf_op jit(solution)/shard_map/pallas_call | solution.py:1502

commit v4 on v3

--- a/solution.py
+++ b/solution.py
@@ -364,7 +364,7 @@
             f_edge(1, across).start()
 
     def slot_of(step):
-        odd = jnp.where(step == 1, 6, jnp.where(step == 3, 5, 3))
+        odd = jnp.where(step == 1, 5, jnp.where(step == 3, 6, 3))
         return jnp.where(is_cls, step, jnp.where(lax.rem(step, 2) == 0, step // 2, odd))
 
     def p_send(layer):
@@ -469,8 +469,6 @@
     for step in range(layers):
         TB[step] = tow[step, 1 - x].astype(low)
         p_send(step).start()
-        if step == 0:
-            pltpu_feature.start()
         W[step, pcs(y, x, k, z)] = tow[step, x].astype(low)
     tail = cls_out + box_out - 2 * CUT
     HB[2] = jnp.zeros((piece, 8, CUT), low)
@@ -480,8 +478,8 @@
 
     @pl.when(is_cls)
     def _():
-        p_head(2, 4, 1).start()
-        p_head(1, 5, 3).start()
+        p_head(2, 4, 3).start()
+        p_head(1, 5, 1).start()
         W[4, pcs(y, x, k, z)] = HB[0]
 
     @pl.when(is_box)
@@ -490,6 +488,7 @@
         W[5, pcs(y, x, k, z)] = HB[1]
         W[6, pcs(y, x, k, z)] = HB[2]
 
+    pltpu_feature.start()
     code_copy = remote(CP.at[x], CP.at[x], fs.at[1], fr.at[1], (par, z))
     goal_copy = remote(GP.at[x], GP.at[x], fs.at[2], fr.at[2], (par, z))
     do_z(0)
@@ -767,7 +766,7 @@
 
     @pl.when(is_cls)
     def _():
-        handed_over(6)
+        handed_over(5)
 
     for cv in range(2):
         take_edges(layers, cv)
@@ -984,7 +983,7 @@
         remote(GP.at[1 - x], GP.at[1 - x], fs.at[2], fr.at[2], (par, z)).wait_recv()
 
     def head(i, carry):
-        cut = 2 - i
+        cut = jnp.where(i == 2, 0, i + 1)
         slot = 4 + cut
         gathered(slot)
         shift = bias[pl.ds(2 * layers + cut, 1), :]
@@ -1009,28 +1008,28 @@
         weight_grad(layers, slot)
         do_rd(slot)
 
+        @pl.when(is_cls & (i == 2))
+        def _():
+            do_rz(5)
+
         input_grad(slot, True)
 
         @pl.when(is_cls & (i == 0))
         def _():
             do_d(4)
-            handed_over(5)
-
-        @pl.when(is_cls & (i == 0))
-        def _():
-            do_rx(slot)
-
-        @pl.when(i > 0)
+            handed_over(6)
+
+        @pl.when(is_cls & (i == 1))
+        def _():
+            do_rx(6)
+
+        @pl.when(i != 1)
         def _():
             do_ry(slot)
 
-        @pl.when(i == 2)
-        def _():
-            do_rz(5)
-
         return carry
 
-    lax.fori_loop(0, 3 - 2 * x, head, 0)
+    lax.fori_loop(x, 3 - x, head, 0)
 
     @pl.when(is_cls)
     def _():
@@ -1075,6 +1074,10 @@
         def _():
             b_copy(BG, 0, (sib, z)).start()
 
+        @pl.when(is_cls | (j > 0))
+        def _():
+            do_rz(layer + 1)
+
         @pl.when(j == layers - 1)
         def _():
             do_ry(0, halves=(0,))
@@ -1091,10 +1094,6 @@
         def _():
             do_ry(layer)
 
-        @pl.when(is_cls | (j > 0))
-        def _():
-            do_rz(layer + 1)
-
         @pl.when(is_cls & (j == 0))
         def _():
             do_rp_head(5)
@@ -1107,15 +1106,15 @@
         def _():
             do_rp_layer(layer + 2)
 
-        @pl.when(is_box & (j == 0))
+        @pl.when(is_box & (j == 1))
         def _():
             do_ry(6, relay=True)
 
-        @pl.when(is_box & (j == 1))
+        @pl.when(is_box & (j == 2))
         def _():
             do_rz(6, relay=True)
 
-        @pl.when(is_box & (j == 2))
+        @pl.when(is_box & (j == 3))
         def _():
             do_rp_head(6)
 
@@ -1173,8 +1172,8 @@
             d_copy(6, b // 2, b % 2, k).wait_send()
         for cut in range(3):
             l_copy(cut).wait_send()
-        p_head(2, 4, 1).wait_send()
-        p_head(1, 5, 3).wait_send()
+        p_head(2, 4, 3).wait_send()
+        p_head(1, 5, 1).wait_send()
         goal_copy.wait_send()
 
     @pl.when(is_box)

time: 146 us -> 141 us (0.966)
  Pallas kernels: 145 us -> 140 us
    pallas_call x1, Pallas kernels: 139 us -> 134 us  [fused_shards(): pl.pallas_call(partial(mega_kernel, rows=rows, cols=cols, layers=layers,...]
where the time goes in v4:
time: 141 us
  Pallas kernels  140 us (99%)
    pallas_call x1, Pallas kernels, fused_shards(): pl.pallas_call(partial(mega_kernel, rows=rows, cols=cols, layers=layers,...  134 us
    pallas_call x1, Pallas kernels, fused_shards(): pl.pallas_call(partial(finish_kernel, layers=layers, rows=rows, cols=cols...  5.63 us

profile of v4, /device:TPU:0, one launch (start us, length us, event | category | flops | bytes accessed | tf_op | source)
XLA Modules:
  0.0 140.9 jit_solution(1452800967118266181)
XLA Ops:
  1.3 133.9 %shard_map.302 = (bf16[3,512,256]{2,1,0:T(8,128)(2,1)}, bf16[512,256]{1,0:T(8,128)(2,1)}, f32[512,256]{1,0:T(8,128)}, f32[4,2,9,8,256]{4,3,2,1,0:T(8,128)}, f32[...) custom-call(bf16[512,256]{1,0:T(8,128)(2,1)} %bitcast.21, s32[1,32]{1,0:T(1,128)} %crops.1, ...), custom_call_target="tpu_custom_call" | custom-call | tf_op jit(solution)/shard_map/pallas_call | solution.py:1429
  135.2 5.6 %shard_map.303 = (bf16[512,720]{1,0:T(8,128)(2,1)}, bf16[36,8,64]{2,1,0:T(8,128)(2,1)}, f32[512,256]{1,0:T(8,128)}, f32[4,72,256]{2,1,0:T(8,128)}, f32[4,72,256]...) custom-call(s32[1]{0:T(128)S(6)} %copy.35.step, ...), custom_call_target="tpu_custom_call" | custom-call | tf_op jit(solution)/shard_map/pallas_call | solution.py:1501

commit v5 on v4

--- a/solution.py
+++ b/solution.py
@@ -556,7 +556,7 @@
     def rim_first(body, carry, send):
         carry = lax.fori_loop(0, 2, lambda i, c: body(i * (rows - 1), c), carry)
         send()
-        return lax.fori_loop(1, rows - 1, body, carry)
+        return lax.fori_loop(1, rows - 1, body, carry, unroll=3)
 
     def g_edge(slot, side, cv):
         src = G.at[slot, cv, pl.ds((rows if side == 0 else 1) * cols, cols)]
@@ -621,8 +621,8 @@
     code_copy.start()
     pltpu_feature.wait_recv()
     fill(FP, 1 - x)
+    pump(1)
     first_edges()
-    pump(1)
 
     def clear(at, layer_count, slot_count):
         def a_body(layer, carry):
@@ -927,7 +927,7 @@
             seen = marks < -50.0
             s = jnp.where(hit, -raw, raw)
             e = jnp.exp(-jnp.abs(s))
-            inv = 1.0 / (1.0 + e)
+            inv = pl.reciprocal(1.0 + e)
             other = e * inv
             q = jnp.where(s >= 0.0, inv, other)
             p = jnp.where(s >= 0.0, other, inv)

time: 141 us -> 141 us (level)
  no operation moved by 1% of the time
where the time goes in v5:
time: 141 us
  Pallas kernels  139 us (99%)
    pallas_call x1, Pallas kernels, fused_shards(): pl.pallas_call(partial(mega_kernel, rows=rows, cols=cols, layers=layers,...  134 us
    pallas_call x1, Pallas kernels, fused_shards(): pl.pallas_call(partial(finish_kernel, layers=layers, rows=rows, cols=cols...  5.63 us

profile of v5, /device:TPU:0, one launch (start us, length us, event | category | flops | bytes accessed | tf_op | source)
XLA Modules:
  0.0 140.6 jit_solution(10945701593688515916)
XLA Ops:
  1.3 133.7 %shard_map.302 = (bf16[3,512,256]{2,1,0:T(8,128)(2,1)}, bf16[512,256]{1,0:T(8,128)(2,1)}, f32[512,256]{1,0:T(8,128)}, f32[4,2,9,8,256]{4,3,2,1,0:T(8,128)}, f32[...) custom-call(bf16[512,256]{1,0:T(8,128)(2,1)} %bitcast.21, s32[1,32]{1,0:T(1,128)} %crops.1, ...), custom_call_target="tpu_custom_call" | custom-call | tf_op jit(solution)/shard_map/pallas_call | solution.py:1429
  135.0 5.6 %shard_map.303 = (bf16[512,720]{1,0:T(8,128)(2,1)}, bf16[36,8,64]{2,1,0:T(8,128)(2,1)}, f32[512,256]{1,0:T(8,128)}, f32[4,72,256]{2,1,0:T(8,128)}, f32[4,72,256]...) custom-call(s32[1]{0:T(128)S(6)} %copy.35.step, ...), custom_call_target="tpu_custom_call" | custom-call | tf_op jit(solution)/shard_map/pallas_call | solution.py:1501

commit v6 on v5

--- a/solution.py
+++ b/solution.py
@@ -1014,18 +1014,18 @@
 
         input_grad(slot, True)
 
+        @pl.when(is_cls & (i == 1))
+        def _():
+            do_rx(6)
+
+        @pl.when(i != 1)
+        def _():
+            do_ry(slot)
+
         @pl.when(is_cls & (i == 0))
         def _():
             do_d(4)
             handed_over(6)
-
-        @pl.when(is_cls & (i == 1))
-        def _():
-            do_rx(6)
-
-        @pl.when(i != 1)
-        def _():
-            do_ry(slot)
 
         return carry
 

time: 141 us -> 141 us (level)
  no operation moved by 1% of the time
where the time goes in v6:
time: 141 us
  Pallas kernels  140 us (99%)
    pallas_call x1, Pallas kernels, fused_shards(): pl.pallas_call(partial(mega_kernel, rows=rows, cols=cols, layers=layers,...  134 us
    pallas_call x1, Pallas kernels, fused_shards(): pl.pallas_call(partial(finish_kernel, layers=layers, rows=rows, cols=cols...  5.63 us

profile of v6, /device:TPU:0, one launch (start us, length us, event | category | flops | bytes accessed | tf_op | source)
XLA Modules:
  0.0 140.9 jit_solution(3385101859636497297)
XLA Ops:
  1.3 133.9 %shard_map.302 = (bf16[3,512,256]{2,1,0:T(8,128)(2,1)}, bf16[512,256]{1,0:T(8,128)(2,1)}, f32[512,256]{1,0:T(8,128)}, f32[4,2,9,8,256]{4,3,2,1,0:T(8,128)}, f32[...) custom-call(bf16[512,256]{1,0:T(8,128)(2,1)} %bitcast.21, s32[1,32]{1,0:T(1,128)} %crops.1, ...), custom_call_target="tpu_custom_call" | custom-call | tf_op jit(solution)/shard_map/pallas_call | solution.py:1429
  135.2 5.6 %shard_map.303 = (bf16[512,720]{1,0:T(8,128)(2,1)}, bf16[36,8,64]{2,1,0:T(8,128)(2,1)}, f32[512,256]{1,0:T(8,128)}, f32[4,72,256]{2,1,0:T(8,128)}, f32[4,72,256]...) custom-call(s32[1]{0:T(128)S(6)} %copy.35.step, ...), custom_call_target="tpu_custom_call" | custom-call | tf_op jit(solution)/shard_map/pallas_call | solution.py:1501
